TPU v7x, 32 devices: a whole 2x2x4 slice. The times are simulated.
32 devices in a mesh: groups: 2 (over y), hist: 2 (over x), rows: 4 (over z), cols: 2 (over core).
Axes of the slice: x: 2, y: 2, z: 4, core: 2. Of those that a mesh axis runs over, the one named last changes fastest.
Arguments:
- hists: float32 [2, 1024, 4096], P('hist', ('groups', 'rows'), 'cols'), parts along dimension 1, may hold values from 0.2 to 2000, as said below
- log_scaling_fields: float32 [2, 1024, 4096], P('hist', ('groups', 'rows'), 'cols'), parts along dimension 1, may hold values from -1 to 1
- histogram_weight_list: float32 [2], replicated, may hold values from 0.25 to 4
Outputs:
- barycenter: float32 [1024, 4096], P(('groups', 'rows'), 'cols'), parts along dimension 0
- new_logs: float32 [2, 1024, 4096], P('hist', ('groups', 'rows'), 'cols'), parts along dimension 1
There are 2 independent parts, one for each index of `groups`. A program takes and returns all parts, laid end to end along the dimension named above; an argument that names none is the same for every part. Nothing has to cross between parts.
Inputs may be any that keep to these rules, and one draw needn't show every extreme that they name: `hists`: every entry is positive.
All inputs are finite; a program needn't handle non-finite values.
Results may differ from a plain program's by a relative error of at most 0.00021.
Values sent between devices are 32-bit elements; how exact they have to be, the bound alone decides.
No kernel may reach another device: no remote copies, remote signals or barrier semaphores. Data moves between devices by JAX's collectives and lax.ppermute only.
A program may use at most 64 MiB of HBM per device.

v0:
```python
import jax
import jax.numpy as jnp
from jax import lax
from jax.sharding import PartitionSpec as P

HALF = 32


kernel_sigma = 16.0


def padded_2(cells, sides, width):
    for axis, dim in sides:
        count = lax.axis_size(axis)
        ends = count - 1
        head = lax.slice_in_dim(cells, 0, width, axis=dim)
        tail = lax.slice_in_dim(cells, cells.shape[dim] - width, cells.shape[dim], axis=dim)
        cells = jnp.concatenate(
            [
                lax.ppermute(tail, axis, [(i, (i + 1) % count) for i in range(ends)]),
                cells,
                lax.ppermute(head, axis, [((i + 1) % count, i) for i in range(ends)]),
            ],
            axis=dim,
        )
    return cells


def band_matrix(width_out):
    shape_full = (width_out + 2 * HALF, width_out)
    rows_in = lax.broadcasted_iota(jnp.int32, shape_full, 0)
    cols_out = lax.broadcasted_iota(jnp.int32, shape_full, 1)
    offsets = (rows_in - cols_out - HALF).astype(jnp.float32)
    tap_offsets = jnp.arange(-HALF, HALF + 1).astype(jnp.float32)
    tap_total = jnp.sum(jnp.exp(-tap_offsets * tap_offsets / (2.0 * kernel_sigma * kernel_sigma)))
    entries = jnp.exp(-offsets * offsets / (2.0 * kernel_sigma * kernel_sigma)) / tap_total
    return jnp.where(jnp.abs(offsets) <= HALF, entries, 0.0)


def column_pass(padded, width_out):
    block_list = []
    for offset in range(0, width_out, 256):
        span_cols = min(256, width_out - offset)
        window = padded[:, offset : offset + span_cols + 2 * HALF]
        block_list.append(
            jnp.dot(
                window,
                band_matrix(span_cols),
                precision=lax.Precision.HIGHEST,
                preferred_element_type=jnp.float32,
            )
        )
    return jnp.concatenate(block_list, axis=1)


def row_pass(across, height_out):
    return jnp.dot(
        band_matrix(height_out).T,
        across,
        precision=lax.Precision.HIGHEST,
        preferred_element_type=jnp.float32,
    )


def blurred_patch(padded, height_out, width_out):
    return row_pass(column_pass(padded, width_out), height_out)


def neighbor_total(values):
    return padded_2(values, (("rows", 0), ("cols", 1)), HALF)


def body(hists, log_scaling_fields, histogram_weight_list):
    masses = hists[0]
    local_log_values = log_scaling_fields[0]
    patch_height = masses.shape[0]
    patch_width = masses.shape[1]
    scaling_fields = jnp.exp(local_log_values)
    blurred_vertical = blurred_patch(neighbor_total(scaling_fields), patch_height, patch_width)
    ratios = masses / blurred_vertical
    smooth_u = blurred_patch(neighbor_total(ratios), patch_height, patch_width)
    log_blurred = jnp.log(smooth_u)
    log_portions = local_log_values + log_blurred
    position = lax.axis_index("hist")
    own_pick = lax.broadcasted_iota(jnp.int32, histogram_weight_list.shape, 0) == position
    own_weight = jnp.sum(jnp.where(own_pick, histogram_weight_list, 0.0)) / jnp.sum(
        histogram_weight_list
    )
    weighted = own_weight * log_portions
    cell_count = patch_height * lax.axis_size("rows") * patch_width * lax.axis_size("cols")
    log_mean = lax.psum(weighted, "hist")
    mean_field = jnp.exp(log_mean)
    total_mass = lax.psum(jnp.sum(mean_field), ("rows", "cols"))
    barycenter = mean_field * (cell_count / total_mass)
    new_logs = jnp.log(barycenter) - log_blurred
    return (barycenter, new_logs[None])


def solution(mesh):
    return jax.shard_map(
        body,
        mesh=mesh,
        in_specs=(
            P("hist", ("groups", "rows"), "cols"),
            P("hist", ("groups", "rows"), "cols"),
            P(),
        ),
        out_specs=(P(("groups", "rows"), "cols"), P("hist", ("groups", "rows"), "cols")),
        check_vma=False,
    )
```

profile of v0, /device:TPU:0, one launch (start us, length us, event | category | flops | bytes accessed | tf_op | source)
XLA Modules:
  0.0 137.4 jit_solution(3415353745641295112)
XLA Ops:
  7.2 0.0 all-reduce.2.cloned.1.call-start
  7.2 1.4 %bitcast_exponential_fusion = f32[128,2048]{1,0:T(8,128)S(1)} fusion(f32[1,128,2048]{2,1,0:T(8,128)} %param.4), kind=kLoop, calls=%fused_computation.21 | loop fusion | bytes 2097152 | tf_op jit(solution)/shard_map/exp | solution.py:78
  8.6 4.9 %collective-permute-start = (f32[32,2048]{1,0:T(8,128)S(1)}, f32[32,2048]{1,0:T(8,128)S(1)}, u32[]{:S(2)}, u32[]{:S(2)}) collective-permute-start(f32[32,2048]{1,0:T(8,128)S(1)} %get-tuple-element.12), channel_id=1, source_target_pairs={{0,2},{2,4},{4,6},{1,3},{3,5},{5,7},{8,10},{10,12},{12,14},{9,11},... | collective-permute-start | bytes 786440 | tf_op jit(solution)/shard_map/ppermute | solution.py:20
  13.6 1.3 collective-permute-start.1
  14.9 0.6 fusion.45
  15.5 3.6 %collective-permute-done = f32[32,2048]{1,0:T(8,128)S(1)} collective-permute-done((f32[32,2048]{1,0:T(8,128)S(1)}, f32[32,2048]{1,0:T(8,128)S(1)}, u32[]{:S(2)}, u32[]{:S(2)}) %collective-permute-start) | collective-permute-done | bytes 262176 | tf_op jit(solution)/shard_map/ppermute | solution.py:20
  19.1 4.1 %collective-permute-done.1 = f32[32,2048]{1,0:T(8,128)S(1)} collective-permute-done((f32[32,2048]{1,0:T(8,128)S(1)}, f32[32,2048]{1,0:T(8,128)S(1)}, u32[]{:S(2)}, u32[]{:S(2)}) %collective-permute-start.1) | collective-permute-done | bytes 262176 | tf_op jit(solution)/shard_map/ppermute | solution.py:22
  23.3 0.1 pad_maximum_fusion.28
  23.3 1.3 collective-permute-start.2
  24.6 1.3 collective-permute-start.3
  25.9 0.1 pad_maximum_fusion
  26.1 1.2 convolution_dynamic-update-slice_fusion.15
  27.4 1.2 convolution_dynamic-update-slice_fusion.14
  28.6 1.2 convolution_dynamic-update-slice_fusion.13
  29.8 1.2 convolution_dynamic-update-slice_fusion.12
  31.1 1.2 convolution_dynamic-update-slice_fusion.11
  32.3 1.2 convolution_dynamic-update-slice_fusion.10
  33.5 1.2 convolution_dynamic-update-slice_fusion.9
  34.8 0.0 copy-start.3
  34.8 0.0 collective-permute-done.3
  34.8 1.3 convolution_dynamic-update-slice_fusion.8
  36.2 0.0 copy-start.2
  36.2 1.8 %convolution_divide_fusion = f32[128,2048]{1,0:T(8,128)S(1)} fusion(f32[192,2048]{1,0:T(8,128)S(1)} %convolution_dynamic-update-slice_fusion.8, f32[1,128,2048]{2,1,0:T(8,128)S(1)} %copy-done.3, f32[]{:T(128)} %fusion.45), kind=kOutput, calls=%fused_computation.1 | convolution fusion | flops 604487680 | bytes 3670020 | tf_op jit(solution)/shard_map/dot_general | solution.py:57
  38.0 3.5 %collective-permute-start.4 = (f32[32,2048]{1,0:T(8,128)S(1)}, f32[32,2048]{1,0:T(8,128)S(1)}, u32[]{:S(2)}, u32[]{:S(2)}) collective-permute-start(f32[32,2048]{1,0:T(8,128)S(1)} %get-tuple-element.10), channel_id=1, source_target_pairs={{0,2},{2,4},{4,6},{1,3},{3,5},{5,7},{8,10},{10,12},{12,14},{9,11},... | collective-permute-start | bytes 786440 | tf_op jit(solution)/shard_map/ppermute | solution.py:20
  41.5 1.3 collective-permute-start.5
  42.8 0.6 fusion.123
  44.7 3.2 %collective-permute-done.4 = f32[32,2048]{1,0:T(8,128)S(1)} collective-permute-done((f32[32,2048]{1,0:T(8,128)S(1)}, f32[32,2048]{1,0:T(8,128)S(1)}, u32[]{:S(2)}, u32[]{:S(2)}) %collective-permute-start.4) | collective-permute-done | bytes 262176 | tf_op jit(solution)/shard_map/ppermute | solution.py:20
  48.0 4.4 %collective-permute-done.5 = f32[32,2048]{1,0:T(8,128)S(1)} collective-permute-done((f32[32,2048]{1,0:T(8,128)S(1)}, f32[32,2048]{1,0:T(8,128)S(1)}, u32[]{:S(2)}, u32[]{:S(2)}) %collective-permute-start.5) | collective-permute-done | bytes 262176 | tf_op jit(solution)/shard_map/ppermute | solution.py:22
  52.4 0.1 pad_maximum_fusion.26
  52.5 1.9 %collective-permute-start.6 = (f32[192,32]{1,0:T(8,128)S(1)}, f32[192,32]{1,0:T(8,128)S(1)}, u32[]{:S(2)}, u32[]{:S(2)}) collective-permute-start(f32[192,32]{1,0:T(8,128)S(1)} %get-tuple-element.7), channel_id=1, source_target_pairs={{0,1},{2,3},{4,5},{6,7},{8,9},{10,11},{12,13},{14,15},{16,17},{18,... | collective-permute-start | bytes 73736 | tf_op jit(solution)/shard_map/ppermute | solution.py:20
  54.4 1.5 %collective-permute-start.7 = (f32[192,32]{1,0:T(8,128)S(1)}, f32[192,32]{1,0:T(8,128)S(1)}, u32[]{:S(2)}, u32[]{:S(2)}) collective-permute-start(f32[192,32]{1,0:T(8,128)S(1)} %get-tuple-element.6), channel_id=1, source_target_pairs={{1,0},{3,2},{5,4},{7,6},{9,8},{11,10},{13,12},{15,14},{17,16},{19,... | collective-permute-start | bytes 73736 | tf_op jit(solution)/shard_map/ppermute | solution.py:22
  55.9 0.1 pad_maximum_fusion.1
  56.0 1.2 convolution_dynamic-update-slice_fusion.7
  57.3 1.2 convolution_dynamic-update-slice_fusion.6
  58.5 1.2 convolution_dynamic-update-slice_fusion.5
  59.7 1.2 convolution_dynamic-update-slice_fusion.4
  61.0 1.2 convolution_dynamic-update-slice_fusion.3
  62.2 1.2 convolution_dynamic-update-slice_fusion.2
  63.5 1.2 convolution_dynamic-update-slice_fusion.1
  64.7 0.0 copy-start
  64.7 0.0 collective-permute-done.7
  64.7 1.3 convolution_dynamic-update-slice_fusion
  66.1 2.8 %fusion = (f32[128,2048]{1,0:T(8,128)}, f32[128,2048]{1,0:T(8,128)S(1)}) fusion(f32[1,128,2048]{2,1,0:T(8,128)S(1)} %copy-done, f32[]{:T(128)S(6)} %div.20, f32[192,2048]{1,0:T(8,128)S(1)} %convolution_dynamic-update-slice_fusion, f32[]{:T(128)} %fusion.45), kind=kOutput, calls=%fused_computation.22 | convolution fusion | flops 604749824 | bytes 4718600 | tf_op jit(solution)/shard_map/dot_general | solution.py:57
  68.9 0.0 all-reduce.2.cloned.1.call-update
  68.9 40.2 %all-reduce.2.cloned.1.call-done = f32[128,2048]{1,0:T(8,128)} async-done(((f32[128,2048]{1,0:T(8,128)}), f32[128,2048]{1,0:T(8,128)}) %all-reduce.2.cloned.1.call-update) | async-done | bytes 1048592 | tf_op jit(solution)/shard_map/psum | solution.py:91
  109.1 2.2 %exponential_reduce_fusion = f32[]{:T(128)} fusion(f32[128,2048]{1,0:T(8,128)} %all-reduce.2.cloned.1.call-done), kind=kLoop, calls=%fused_computation.25 | loop fusion | flops 262143 | bytes 1048580 | tf_op jit(solution)/shard_map/reduce_sum | solution.py:93
  111.3 17.0 %psum.15 = f32[]{:T(128)} all-reduce(f32[]{:T(128)} %exponential_reduce_fusion), channel_id=1, replica_groups=mesh['groups'=2,'hist'=2,'rows'=4,'cols'=2] {'rows','cols'}, use_global_device_ids=true, to_apply=%region_5.6 | all-reduce | flops 1 | bytes 8 | tf_op jit(solution)/shard_map/psum | solution.py:93
  129.0 1.6 %subtract_bitcast_fusion = (f32[1,128,2048]{2,1,0:T(8,128)}, f32[128,2048]{1,0:T(8,128)}) fusion(f32[128,2048]{1,0:T(8,128)S(1)} %get-tuple-element.15, f32[]{:T(128)S(6)} %div.29, f32[128,2048]{1,0:T(8,128)S(1)} %copy-done.1), kind=kLoop, calls=%fused_computation.23 | loop fusion | flops 524288 | bytes 4194308 | tf_op jit(solution)/shard_map/broadcast_in_dim | solution.py:96
  (9 shorter events, 0.1 us)
Async XLA Ops:
  7.2 102.0 %all-reduce.2.cloned.1.call-start = ((), (), s32[]{:S(2)}) async-start(), calls=%async_computation | async-start | bytes 2097152 | tf_op jit(solution)/shard_map/psum | solution.py:91
  8.6 10.5 %collective-permute-start = (f32[32,2048]{1,0:T(8,128)S(1)}, f32[32,2048]{1,0:T(8,128)S(1)}, u32[]{:S(2)}, u32[]{:S(2)}) collective-permute-start(f32[32,2048]{1,0:T(8,128)S(1)} %get-tuple-element.12), channel_id=1, source_target_pairs={{0,2},{2,4},{4,6},{1,3},{3,5},{5,7},{8,10},{10,12},{12,14},{9,11},... | collective-permute-start | bytes 786440 | tf_op jit(solution)/shard_map/ppermute | solution.py:20
  13.6 9.7 %collective-permute-start.1 = (f32[32,2048]{1,0:T(8,128)S(1)}, f32[32,2048]{1,0:T(8,128)S(1)}, u32[]{:S(2)}, u32[]{:S(2)}) collective-permute-start(f32[32,2048]{1,0:T(8,128)S(1)} %get-tuple-element.13), channel_id=1, source_target_pairs={{2,0},{4,2},{6,4},{3,1},{5,3},{7,5},{10,8},{12,10},{14,12},{11,9},... | collective-permute-start | bytes 786440 | tf_op jit(solution)/shard_map/ppermute | solution.py:22
  23.3 2.8 %collective-permute-start.2 = (f32[192,32]{1,0:T(8,128)S(1)}, f32[192,32]{1,0:T(8,128)S(1)}, u32[]{:S(2)}, u32[]{:S(2)}) collective-permute-start(f32[192,32]{1,0:T(8,128)S(1)} %get-tuple-element.9), channel_id=1, source_target_pairs={{0,1},{2,3},{4,5},{6,7},{8,9},{10,11},{12,13},{14,15},{16,17},{18,... | collective-permute-start | bytes 73736 | tf_op jit(solution)/shard_map/ppermute | solution.py:20
  24.6 10.1 %collective-permute-start.3 = (f32[192,32]{1,0:T(8,128)S(1)}, f32[192,32]{1,0:T(8,128)S(1)}, u32[]{:S(2)}, u32[]{:S(2)}) collective-permute-start(f32[192,32]{1,0:T(8,128)S(1)} %get-tuple-element.8), channel_id=1, source_target_pairs={{1,0},{3,2},{5,4},{7,6},{9,8},{11,10},{13,12},{15,14},{17,16},{19,... | collective-permute-start | bytes 73736 | tf_op jit(solution)/shard_map/ppermute | solution.py:22
  34.8 1.4 copy-start.3
  36.2 6.6 %copy-start.2 = (f32[2]{0:T(128)S(1)}, f32[2]{0:T(128)}, u32[]{:S(2)}) copy-start(f32[2]{0:T(128)} %param.5) | copy-start | bytes 28
  38.0 10.0 %collective-permute-start.4 = (f32[32,2048]{1,0:T(8,128)S(1)}, f32[32,2048]{1,0:T(8,128)S(1)}, u32[]{:S(2)}, u32[]{:S(2)}) collective-permute-start(f32[32,2048]{1,0:T(8,128)S(1)} %get-tuple-element.10), channel_id=1, source_target_pairs={{0,2},{2,4},{4,6},{1,3},{3,5},{5,7},{8,10},{10,12},{12,14},{9,11},... | collective-permute-start | bytes 786440 | tf_op jit(solution)/shard_map/ppermute | solution.py:20
  41.5 10.9 %collective-permute-start.5 = (f32[32,2048]{1,0:T(8,128)S(1)}, f32[32,2048]{1,0:T(8,128)S(1)}, u32[]{:S(2)}, u32[]{:S(2)}) collective-permute-start(f32[32,2048]{1,0:T(8,128)S(1)} %get-tuple-element.11), channel_id=1, source_target_pairs={{2,0},{4,2},{6,4},{3,1},{5,3},{7,5},{10,8},{12,10},{14,12},{11,9},... | collective-permute-start | bytes 786440 | tf_op jit(solution)/shard_map/ppermute | solution.py:22
  52.5 3.5 %collective-permute-start.6 = (f32[192,32]{1,0:T(8,128)S(1)}, f32[192,32]{1,0:T(8,128)S(1)}, u32[]{:S(2)}, u32[]{:S(2)}) collective-permute-start(f32[192,32]{1,0:T(8,128)S(1)} %get-tuple-element.7), channel_id=1, source_target_pairs={{0,1},{2,3},{4,5},{6,7},{8,9},{10,11},{12,13},{14,15},{16,17},{18,... | collective-permute-start | bytes 73736 | tf_op jit(solution)/shard_map/ppermute | solution.py:20
  54.4 10.3 %collective-permute-start.7 = (f32[192,32]{1,0:T(8,128)S(1)}, f32[192,32]{1,0:T(8,128)S(1)}, u32[]{:S(2)}, u32[]{:S(2)}) collective-permute-start(f32[192,32]{1,0:T(8,128)S(1)} %get-tuple-element.6), channel_id=1, source_target_pairs={{1,0},{3,2},{5,4},{7,6},{9,8},{11,10},{13,12},{15,14},{17,16},{19,... | collective-permute-start | bytes 73736 | tf_op jit(solution)/shard_map/ppermute | solution.py:22
  64.7 1.4 copy-start
  109.1 19.9 %copy-start.1 = (f32[128,2048]{1,0:T(8,128)S(1)}, f32[128,2048]{1,0:T(8,128)}, u32[]{:S(2)}) copy-start(f32[128,2048]{1,0:T(8,128)} %all-reduce.2.cloned.1.call-done) | copy-start | bytes 3145732
Sparse Core Ops, SparseCore 0:
  69.0 40.0 all-reduce.1
where the time goes:
time: 138 us; the launch traced here: 137 us
  waiting for transfers between devices  55.6 us (40%)
  matrix products  24.5 us (18%)
  starting transfers between devices  17 us (12%)
  blocking collectives  17 us (12%)
  between operations  16.4 us (12%)
  other arithmetic  5.45 us (4%)
  local copies, waits for them, and re-layouts  1.48 us (1%)
    psum x1, waiting for transfers between devices, body(): log_mean = lax.psum(weighted, 'hist')  40.2 us
    dot_general x16, matrix products, column_pass(): jnp.dot(window, band_matrix(span_cols), precision=lax.Precision.HIGHEST,...  19.9 us
    psum x1, blocking collectives, body(): total_mass = lax.psum(jnp.sum(mean_field), ('rows', 'cols'))  17 us
    ppermute x4, starting transfers between devices, padded_2(): lax.ppermute(tail, axis, [(i, (i + 1) % count) for i in range(ends)])  11.6 us
    ppermute x4, waiting for transfers between devices, padded_2(): lax.ppermute(head, axis, [((i + 1) % count, i) for i in range(ends)])  8.58 us
    ppermute x4, waiting for transfers between devices, padded_2(): lax.ppermute(tail, axis, [(i, (i + 1) % count) for i in range(ends)])  6.86 us
    ppermute x4, starting transfers between devices, padded_2(): lax.ppermute(head, axis, [((i + 1) % count, i) for i in range(ends)])  5.35 us
    dot_general x2, matrix products, row_pass(): jnp.dot(band_matrix(height_out).T, across, precision=lax.Precision.HIGHES...  4.6 us
  transfers between devices with their start and end apart: 9, of which 5 were waited for; matrix products, arithmetic and copies ran while one was open for 14% of the time, Pallas kernels for 0%

commit v1 on v0

v1 whole, which is shorter than its diff:
```python
import functools

import jax
import jax.numpy as jnp
import numpy as np
from jax import lax
from jax.experimental import pallas as pl
from jax.experimental.pallas import tpu as pltpu
from jax.sharding import PartitionSpec as P

HALF = 32
LANES = 128
kernel_sigma = 16.0


def band_matrix(rows_in, cols_out):
    taps = np.arange(-HALF, HALF + 1).astype(np.float64)
    total = np.sum(np.exp(-taps * taps / (2.0 * kernel_sigma * kernel_sigma)))
    offsets = np.arange(rows_in)[:, None] - np.arange(cols_out)[None, :] - HALF
    entries = np.exp(-offsets * offsets / (2.0 * kernel_sigma * kernel_sigma)) / total
    return np.where(np.abs(offsets) <= HALF, entries, 0.0).astype(np.float32)


def split_constant(matrix):
    high = matrix.astype(jnp.bfloat16)
    low = (matrix - high.astype(np.float32)).astype(jnp.bfloat16)
    return high, low


def column_band():
    high, low = split_constant(band_matrix(LANES + 2 * HALF, LANES))
    return jnp.asarray(np.concatenate([high, low], axis=1))


def row_band(rows_out):
    high, low = split_constant(band_matrix(rows_out + 2 * HALF, rows_out).T)
    return jnp.asarray(
        np.concatenate(
            [np.concatenate([high, high], axis=1), np.concatenate([low, np.zeros_like(low)], axis=1)], axis=0
        )
    )


def split(values):
    high = values.astype(jnp.bfloat16)
    low = (values - high.astype(jnp.float32)).astype(jnp.bfloat16)
    return high, low


def dot(left, right):
    return jnp.dot(left, right, preferred_element_type=jnp.float32)


def column_block(window, band):
    high, low = split(window)
    depth = window.shape[1]
    both = dot(high, band[:depth])
    return both[:, :LANES] + both[:, LANES:] + dot(low, band[:depth, :LANES])


def row_block(window, band):
    high, low = split(window)
    rows = band.shape[0] // 2
    both = dot(band, jnp.concatenate([high, low], axis=0))
    return both[:rows] + both[rows:]


def edge_flags():
    place = lax.axis_index("cols")
    return (place > 0).astype(jnp.float32), (place < lax.axis_size("cols") - 1).astype(jnp.float32)


def spread_kernel(logs, from_left, from_right, band, across, top, bottom, wide):
    has_left, has_right = edge_flags()
    width = logs.shape[1]
    edge = 2 * HALF
    wide[:, :] = jnp.concatenate(
        [from_left[:, :edge] * has_left, jnp.exp(logs[...]), from_right[:, :edge] * has_right], axis=1
    )
    taps = band[...]
    for start in range(0, width + edge, LANES):
        stop = min(start + LANES + 2 * HALF, width + 2 * edge)
        across[:, start : start + LANES] = column_block(wide[:, start:stop], taps)
    top[...] = across[:HALF, :]
    bottom[...] = across[across.shape[0] - HALF :, :]


def ratio_rows(smooth, masses, from_left, from_right):
    has_left, has_right = edge_flags()
    edge = 2 * HALF
    rows = masses.shape[0]
    wide = jnp.concatenate(
        [
            from_left[:, edge : edge + HALF] * has_left,
            masses,
            from_right[:, edge : edge + HALF] * has_right,
            jnp.zeros((rows, edge), jnp.float32),
        ],
        axis=1,
    )
    return jnp.where(wide > 0.0, wide / smooth, 0.0)


def chunks(width, step):
    return [(start, min(start + step, width)) for start in range(0, width, step)]


def column_pass(ratios, taps, out):
    for start in range(0, out.shape[1], LANES):
        out[:, start : start + LANES] = column_block(ratios[:, start : start + LANES + 2 * HALF], taps)


def inner_ratio_kernel(across, masses, from_left, from_right, band, rows_band, out, smooth, ratios):
    height = masses.shape[0]
    for start, stop in chunks(across.shape[1], 256):
        smooth[:, start:stop] = row_block(across[:, start:stop], rows_band[...])
    inner = slice(HALF, height - HALF)
    ratios[...] = ratio_rows(smooth[...], masses[inner, :], from_left[inner, :], from_right[inner, :])
    column_pass(ratios, band[...], out)


def rim_ratio_kernel(
    across, above, below, masses, from_left, from_right, band, rows_band, top, bottom, smooth, ratios, out
):
    height = masses.shape[0]
    taps = rows_band[...]
    for start, stop in chunks(across.shape[1], 256):
        upper = jnp.concatenate([above[:, start:stop], across[: 2 * HALF, start:stop]], axis=0)
        lower = jnp.concatenate([across[height - 2 * HALF :, start:stop], below[:, start:stop]], axis=0)
        smooth[:HALF, start:stop] = row_block(upper, taps)
        smooth[HALF:, start:stop] = row_block(lower, taps)
    rims = lambda ref: jnp.concatenate([ref[:HALF, :], ref[height - HALF :, :]], axis=0)
    ratios[...] = ratio_rows(smooth[...], rims(masses), rims(from_left), rims(from_right))
    column_pass(ratios, band[...], out)
    top[...] = out[:HALF, :]
    bottom[...] = out[HALF:, :]


def write_parts(weight, log_rows, log_smooth, own, first, later):
    own[...] = weight * (log_rows + log_smooth)
    count = lax.axis_size("hist")
    place = lax.axis_index("hist")
    share = own.shape[1] // count
    for shift in range(1, count):
        other = lax.rem(place + shift, count)
        first[shift - 1] = own[:, pl.ds(pl.multiple_of(other * share, LANES), share)]
        for step in range(1, count):
            block = lax.rem(other + step, count)
            later[shift - 1, :, (step - 1) * share : step * share] = own[
                :, pl.ds(pl.multiple_of(block * share, LANES), share)
            ]


def inner_log_kernel(weight, top, inner, bottom, logs, rows_band, smooth, own, first, later):
    height = logs.shape[0]
    taps = rows_band[...]
    for start, stop in chunks(inner.shape[1], 256):
        window = jnp.concatenate([top[:, start:stop], inner[:, start:stop], bottom[:, start:stop]], axis=0)
        smooth[:, start:stop] = jnp.log(row_block(window, taps))
    write_parts(weight[0, 0], logs[HALF : height - HALF, :], smooth[...], own, first, later)


def rim_log_kernel(weight, above, top, inner, bottom, below, logs, rows_band, smooth, own, first, later):
    height = logs.shape[0]
    depth = inner.shape[0]
    taps = rows_band[...]
    for start, stop in chunks(inner.shape[1], 256):
        part = lambda ref, rows=slice(None): ref[rows, start:stop]
        upper = jnp.concatenate([part(above), part(top), part(inner, slice(0, HALF))], axis=0)
        lower = jnp.concatenate([part(inner, slice(depth - HALF, depth)), part(bottom), part(below)], axis=0)
        smooth[:HALF, start:stop] = jnp.log(row_block(upper, taps))
        smooth[HALF:, start:stop] = jnp.log(row_block(lower, taps))
    log_rows = jnp.concatenate([logs[:HALF, :], logs[height - HALF :, :]], axis=0)
    write_parts(weight[0, 0], log_rows, smooth[...], own, first, later)


def whole(count):
    return [pl.BlockSpec(memory_space=pltpu.VMEM)] * count


def call(kernel, name, args, outs, scratch=(), scalars=0, cost=0):
    f32 = lambda shape: jax.ShapeDtypeStruct(shape, jnp.float32)
    return pl.pallas_call(
        kernel,
        name=name,
        out_shape=tuple(f32(shape) for shape in outs),
        in_specs=[pl.BlockSpec(memory_space=pltpu.SMEM)] * scalars + whole(len(args) - scalars),
        out_specs=tuple(whole(len(outs))),
        scratch_shapes=[pltpu.VMEM(shape, jnp.float32) for shape in scratch],
        compiler_params=pltpu.CompilerParams(vmem_limit_bytes=32 * 1024 * 1024),
        cost_estimate=pl.CostEstimate(flops=cost, bytes_accessed=cost // 256, transcendentals=0),
    )(*args)


def swap_columns(right_edge, left_edge):
    count = lax.axis_size("cols")
    if count == 2:
        sent = jnp.where(lax.axis_index("cols") == 0, right_edge, left_edge)
        got = lax.ppermute(sent, "cols", [(0, 1), (1, 0)])
        return got, got
    steps = [(i, i + 1) for i in range(count - 1)]
    return (
        lax.ppermute(right_edge, "cols", steps),
        lax.ppermute(left_edge, "cols", [(b, a) for a, b in steps]),
    )


def swap_rows(top, bottom):
    steps = [(i, i + 1) for i in range(lax.axis_size("rows") - 1)]
    return lax.ppermute(bottom, "rows", steps), lax.ppermute(top, "rows", [(b, a) for a, b in steps])


def share_over_hist(parts):
    count = lax.axis_size("hist")
    return [
        lax.ppermute(parts[shift - 1], "hist", [(i, (i + shift) % count) for i in range(count)])
        for shift in range(1, count)
    ]


def total_over(values, axes):
    for axis in axes:
        count = lax.axis_size(axis)
        span = 1
        while span < count:
            values = values + lax.ppermute(values, axis, [(i, i ^ span) for i in range(count)])
            span *= 2
    return values


def gathered_mean(own, first, later):
    count = lax.axis_size("hist")
    place = lax.axis_index("hist")
    share = own.shape[1] // count
    mine = lax.dynamic_slice_in_dim(own, place * share, share, axis=1) + sum(first)
    return mine, later


def body(hists, log_scaling_fields, histogram_weight_list):
    masses = hists[0]
    logs = log_scaling_fields[0]
    height, width = masses.shape
    count = lax.axis_size("hist")
    place = lax.axis_index("hist")
    edge = 2 * HALF
    inner = height - edge
    taps = column_band()
    inner_taps = row_band(inner)
    rim_taps = row_band(HALF)

    own_pick = lax.broadcasted_iota(jnp.int32, histogram_weight_list.shape, 0) == place
    weight = jnp.sum(jnp.where(own_pick, histogram_weight_list, 0.0)) / jnp.sum(histogram_weight_list)
    weight = weight.reshape(1, 1)

    gap = jnp.zeros((height, LANES - edge - HALF), jnp.float32)
    right_edge = jnp.concatenate([jnp.exp(logs[:, width - edge :]), masses[:, width - HALF :], gap], axis=1)
    left_edge = jnp.concatenate([jnp.exp(logs[:, :edge]), masses[:, :HALF], gap], axis=1)
    from_left, from_right = swap_columns(right_edge, left_edge)

    wide = width + LANES
    matmul = 2 * height * width * 3 * 256
    across, top, bottom = call(
        spread_kernel, "spread", (logs, from_left, from_right, taps),
        [(height, wide), (HALF, wide), (HALF, wide)], [(height, wide)], cost=matmul,
    )
    above, below = swap_rows(top, bottom)
    (second,) = call(
        inner_ratio_kernel, "inner_ratio", (across, masses, from_left, from_right, taps, inner_taps),
        [(inner, width)], [(inner, wide), (inner, wide)], cost=matmul,
    )
    second_top, second_bottom = call(
        rim_ratio_kernel, "rim_ratio", (across, above, below, masses, from_left, from_right, taps, rim_taps),
        [(HALF, width), (HALF, width)], [(edge, wide), (edge, wide), (edge, width)], cost=matmul,
    )
    second_above, second_below = swap_rows(second_top, second_bottom)

    share = width // count
    parts = [
        ((inner, width), (inner, width), (count - 1, inner, share), (count - 1, inner, width - share)),
        ((edge, width), (edge, width), (count - 1, edge, share), (count - 1, edge, width - share)),
    ]
    in_smooth, in_own, in_first, in_later = call(
        inner_log_kernel, "inner_log", (weight, second_top, second, second_bottom, logs, inner_taps),
        parts[0], scalars=1, cost=matmul,
    )
    in_first = share_over_hist(in_first)
    rim_smooth, rim_own, rim_first, rim_later = call(
        rim_log_kernel, "rim_log",
        (weight, second_above, second_top, second, second_bottom, second_below, logs, rim_taps),
        parts[1], scalars=1, cost=matmul,
    )
    rim_first = share_over_hist(rim_first)
    in_later = share_over_hist(in_later)
    rim_later = share_over_hist(rim_later)

    def own_share(own, first):
        return lax.dynamic_slice_in_dim(own, place * share, share, axis=1) + sum(first)

    partial = jnp.sum(jnp.exp(own_share(in_own, in_first)).reshape(-1, 8, share), axis=0) + jnp.sum(
        jnp.exp(own_share(rim_own, rim_first)).reshape(-1, 8, share), axis=0
    )
    partial = jnp.sum(partial.reshape(8, -1, LANES), axis=1)
    total = jnp.sum(total_over(partial, ("cols", "rows", "hist")))
    scale = height * lax.axis_size("rows") * width * lax.axis_size("cols") / total

    def log_mean(own, first, later):
        others = jnp.zeros_like(own)
        mine = lax.broadcasted_iota(jnp.int32, own.shape, 1) // share == place
        if count == 2:
            arrived = jnp.where(
                mine,
                jnp.concatenate([first[0], first[0]], axis=1),
                jnp.concatenate([later[0], later[0]], axis=1),
            )
            return own + arrived
        others = lax.dynamic_update_slice_in_dim(others, sum(first), place * share, axis=1)
        for shift in range(1, count):
            for step in range(1, count):
                block = lax.rem(place + step, count)
                piece = later[shift - 1][:, (step - 1) * share : step * share]
                start = block * share
                now = lax.dynamic_slice_in_dim(others, start, share, axis=1)
                others = lax.dynamic_update_slice_in_dim(others, now + piece, start, axis=1)
        return own + others

    def joined(inner_rows, rim_rows):
        return jnp.concatenate([rim_rows[:HALF], inner_rows, rim_rows[HALF:]], axis=0)

    mean = joined(log_mean(in_own, in_first, in_later), log_mean(rim_own, rim_first, rim_later))
    log_smooth = joined(in_smooth, rim_smooth)
    barycenter = jnp.exp(mean) * scale
    new_logs = mean + jnp.log(scale) - log_smooth
    return (barycenter, new_logs[None])


def solution(mesh):
    return jax.shard_map(
        body,
        mesh=mesh,
        in_specs=(
            P("hist", ("groups", "rows"), "cols"),
            P("hist", ("groups", "rows"), "cols"),
            P(),
        ),
        out_specs=(P(("groups", "rows"), "cols"), P("hist", ("groups", "rows"), "cols")),
        check_vma=False,
    )
```

time: 138 us -> 70.3 us (0.51)
  waiting for transfers between devices: 55.6 us -> 25.6 us
  matrix products: 24.5 us -> 0 us
  blocking collectives: 17 us -> 0 us
  between operations: 16.4 us -> 2.91 us
  starting transfers between devices: 17 us -> 23.5 us
  Pallas kernels: 0 us -> 5.8 us
  local copies, waits for them, and re-layouts: 1.48 us -> 6.14 us
    psum x1 -> x0, waiting for transfers between devices: 40.2 us -> none  [body(): log_mean = lax.psum(weighted, 'hist')]
    dot_general x18 -> x0, matrix products: 24.5 us -> none  [the longest x16 19.9 us: column_pass(): jnp.dot(window, band_matrix(span_cols), precision=lax.Precision.HIGHEST,...]
    psum x1 -> x0, blocking collectives: 17 us -> none  [body(): total_mass = lax.psum(jnp.sum(mean_field), ('rows', 'cols'))]
    ppermute x8 -> x13, waiting for transfers between devices: 15.4 us -> 25.6 us  [the longest x4 11.2 us: share_over_hist(): lax.ppermute(parts[shift - 1], 'hist', [(i, (i + shift) % count) for i in...]
    ppermute x8 -> x13, starting transfers between devices: 17 us -> 23.5 us  [the longest x2 8.31 us: swap_rows(): lax.ppermute(bottom, 'rows', steps)]
    pallas_call x0 -> x5, Pallas kernels: none -> 5.8 us  [call(): pl.pallas_call(kernel, name=name, out_shape=tuple((f32(shape) for shape i...]
    unnamed x8 -> x24, local copies, waits for them, and re-layouts: 0.02 us -> 3.89 us
    broadcast_in_dim x1 -> x0, other arithmetic: 1.61 us -> none  [body(): return (barycenter, new_logs[None])]
  transfers between devices with their start and end apart: 9 -> 13, of which waited for: 5 -> 10; matrix products, arithmetic and copies ran while one was open for 14% -> 4% of each run, Pallas kernels for 0% -> 5%
where the time goes in v1:
time: 70.3 us; the launch traced here: 69.9 us
  waiting for transfers between devices  25.6 us (36%)
  starting transfers between devices  23.5 us (33%)
  local copies, waits for them, and re-layouts  6.14 us (9%)
  other arithmetic  5.86 us (8%)
  Pallas kernels  5.8 us (8%)
  between operations  2.91 us (4%)
    ppermute x4, waiting for transfers between devices, share_over_hist(): lax.ppermute(parts[shift - 1], 'hist', [(i, (i + shift) % count) for i in...  11.2 us
    ppermute x2, starting transfers between devices, swap_rows(): lax.ppermute(bottom, 'rows', steps)  8.31 us
    ppermute x4, starting transfers between devices, total_over(): lax.ppermute(values, axis, [(i, i ^ span) for i in range(count)])  7.02 us
    pallas_call x5, Pallas kernels, call(): pl.pallas_call(kernel, name=name, out_shape=tuple((f32(shape) for shape i...  5.8 us
    ppermute x2, waiting for transfers between devices, swap_rows(): lax.ppermute(bottom, 'rows', steps)  5.22 us
    ppermute x4, starting transfers between devices, share_over_hist(): lax.ppermute(parts[shift - 1], 'hist', [(i, (i + shift) % count) for i in...  5.1 us
    ppermute x2, waiting for transfers between devices, swap_rows(): lax.ppermute(top, 'rows', [(b, a) for a, b in steps])  4.82 us
    unnamed x24, local copies, waits for them, and re-layouts  3.89 us
  transfers between devices with their start and end apart: 13, of which 10 were waited for; matrix products, arithmetic and copies ran while one was open for 4% of the time, Pallas kernels for 5%

profile of v1, /device:TPU:0, one launch (start us, length us, event | category | flops | bytes accessed | tf_op | source)
XLA Modules:
  0.0 69.9 jit_solution(16130089868692798416)
XLA Ops:
  0.6 0.0 copy-start.4
  0.6 0.0 copy-start.6
  0.7 1.0 %slice_exponential_fusion = (f32[128,64]{1,0:T(8,128)S(1)}, f32[128,64]{1,0:T(8,128)S(1)}) fusion(f32[128,2048]{1,0:T(8,128)} %bitcast.26), kind=kLoop, calls=%fused_computation.13 | loop fusion | bytes 131072 | tf_op jit(solution)/shard_map/exp | solution.py:257
  1.7 1.0 %fusion.9 = (f32[128,32]{1,0:T(8,128)S(1)}, f32[128,32]{1,0:T(8,128)S(1)}) fusion(f32[128,2048]{1,0:T(8,128)} %bitcast.23), kind=kLoop, calls=%fused_computation.30 | loop fusion | bytes 65536 | tf_op jit(solution)/shard_map/slice | solution.py:257
  2.7 0.1 pad.22.clone
  2.8 0.1 maximum_select_fusion.2
  2.9 0.5 collective-permute-start
  3.4 0.9 %collective-permute-done.from_left.from_right = f32[128,128]{1,0:T(8,128)S(1)} collective-permute-done((f32[128,128]{1,0:T(8,128)S(1)}, f32[128,128]{1,0:T(8,128)S(1)}, u32[]{:S(2)}, u32[]{:S(2)}) %collective-permute-start) | collective-permute-done | bytes 65568 | tf_op jit(solution)/shard_map/ppermute | solution.py:199
  4.3 1.2 %copy-done.1 = f32[1,128,2048]{2,1,0:T(8,128)S(1)} copy-done((f32[1,128,2048]{2,1,0:T(8,128)S(1)}, f32[1,128,2048]{2,1,0:T(8,128)}, u32[]{:S(2)}) %copy-start.1) | copy-done | bytes 1048600
  5.6 0.9 %copy-done.3 = bf16[192,256]{1,0:T(8,128)(2,1)S(1)} copy-done((bf16[192,256]{1,0:T(8,128)(2,1)S(1)}, bf16[192,256]{1,0:T(8,128)(2,1)}, u32[]{:S(2)}) %copy-start.3) | copy-done | bytes 98328
  6.5 1.5 %spread.1 = (f32[128,2176]{1,0:T(8,128)S(1)}, f32[32,2176]{1,0:T(8,128)S(1)}, f32[32,2176]{1,0:T(8,128)}) custom-call(f32[128,2048]{1,0:T(8,128)S(1)} %bitcast.27, f32[128,128]{1,0:T(8,128)S(1)} %collective-permute-done.from_left.from_right, f32[128,128]{1,0:T(8,128)S(1)} %collective-permute-done.from_left.from_right, bf16[192,256]{1,0:T(8,128)(2,1)S(1)} %copy-done.3), custom_call_target="tpu_custom_call" | custom-call | flops 402653184 | bytes 1572864 | tf_op jit(solution)/shard_map/spread/pallas_call | solution.py:183
  8.0 4.8 %collective-permute-start.1 = (f32[32,2176]{1,0:T(8,128)}, f32[32,2176]{1,0:T(8,128)S(1)}, u32[]{:S(2)}, u32[]{:S(2)}) collective-permute-start(f32[32,2176]{1,0:T(8,128)} %get-tuple-element.16), channel_id=1, source_target_pairs={{0,2},{2,4},{4,6},{1,3},{3,5},{5,7},{8,10},{10,12},{12,14},{9,11},... | collective-permute-start | bytes 835592 | tf_op jit(solution)/shard_map/ppermute | solution.py:210
  12.8 1.3 %collective-permute-start.2 = (f32[32,2176]{1,0:T(8,128)S(1)}, f32[32,2176]{1,0:T(8,128)S(1)}, u32[]{:S(2)}, u32[]{:S(2)}) collective-permute-start(f32[32,2176]{1,0:T(8,128)S(1)} %get-tuple-element.17), channel_id=1, source_target_pairs={{2,0},{4,2},{6,4},{3,1},{5,3},{7,5},{10,8},{12,10},{14,12},{11,9},... | collective-permute-start | bytes 835592 | tf_op jit(solution)/shard_map/ppermute | solution.py:210
  14.1 5.2 %collective-permute-done.1.above = f32[32,2176]{1,0:T(8,128)S(1)} collective-permute-done((f32[32,2176]{1,0:T(8,128)}, f32[32,2176]{1,0:T(8,128)S(1)}, u32[]{:S(2)}, u32[]{:S(2)}) %collective-permute-start.1) | collective-permute-done | bytes 278560 | tf_op jit(solution)/shard_map/ppermute | solution.py:210
  19.3 3.8 %collective-permute-done.2.below = f32[32,2176]{1,0:T(8,128)S(1)} collective-permute-done((f32[32,2176]{1,0:T(8,128)S(1)}, f32[32,2176]{1,0:T(8,128)S(1)}, u32[]{:S(2)}, u32[]{:S(2)}) %collective-permute-start.2) | collective-permute-done | bytes 278560 | tf_op jit(solution)/shard_map/ppermute | solution.py:210
  23.2 0.0 copy-start.5
  23.2 1.1 %rim_ratio.1 = (f32[32,2048]{1,0:T(8,128)S(1)}, f32[32,2048]{1,0:T(8,128)S(1)}) custom-call(f32[128,2176]{1,0:T(8,128)S(1)} %get-tuple-element.15.across, f32[32,2176]{1,0:T(8,128)S(1)} %collective-permute-done.1.above, f32[32,2176]{1,0:T(8,128)S(1)} %collective-permute-done.2.below, f32[128,2048]{1,0:T(8,128)S(1)} %bitcast.24, ...), custom_call_target="tpu_custom_call" | custom-call | flops 402653184 | bytes 1572864 | tf_op jit(solution)/shard_map/rim_ratio/pallas_call | solution.py:183
  24.3 3.5 %collective-permute-start.3 = (f32[32,2048]{1,0:T(8,128)S(1)}, f32[32,2048]{1,0:T(8,128)S(1)}, u32[]{:S(2)}, u32[]{:S(2)}) collective-permute-start(f32[32,2048]{1,0:T(8,128)S(1)} %get-tuple-element.18.bottom), channel_id=1, source_target_pairs={{0,2},{2,4},{4,6},{1,3},{3,5},{5,7},{8,10},{10,12},{12,14},{9,11},... | collective-permute-start | bytes 786440 | tf_op jit(solution)/shard_map/ppermute | solution.py:210
  27.8 1.3 %collective-permute-start.4 = (f32[32,2048]{1,0:T(8,128)S(1)}, f32[32,2048]{1,0:T(8,128)S(1)}, u32[]{:S(2)}, u32[]{:S(2)}) collective-permute-start(f32[32,2048]{1,0:T(8,128)S(1)} %get-tuple-element.19.top), channel_id=1, source_target_pairs={{2,0},{4,2},{6,4},{3,1},{5,3},{7,5},{10,8},{12,10},{14,12},{11,9},... | collective-permute-start | bytes 786440 | tf_op jit(solution)/shard_map/ppermute | solution.py:210
  29.1 0.6 fusion.8
  31.0 0.9 %inner_ratio.1.inner = f32[64,2048]{1,0:T(8,128)S(1)} custom-call(f32[128,2176]{1,0:T(8,128)S(1)} %get-tuple-element.15.across, f32[128,2048]{1,0:T(8,128)S(1)} %bitcast.25, f32[128,128]{1,0:T(8,128)S(1)} %collective-permute-done.from_left.from_right, f32[128,128]{1,0:T(8,128)S(1)} %collective-permute-done.from_left.from_right, ...), custom_call_target="tpu_custom_call" | custom-call | flops 402653184 | bytes 1572864 | tf_op jit(solution)/shard_map/inner_ratio/pallas_call | solution.py:183
  31.9 0.3 copy-done.2
  32.3 1.1 %inner_log.1 = (f32[64,2048]{1,0:T(8,128)S(1)}, f32[64,2048]{1,0:T(8,128)S(1)}, f32[1,64,1024]{2,1,0:T(8,128)}, f32[1,64,1024]{2,1,0:T(8,128)S(1)}) custom-call(f32[1,1]{1,0:T(1,128)} %bitcast.weight, f32[32,2048]{1,0:T(8,128)S(1)} %get-tuple-element.19.top, f32[64,2048]{1,0:T(8,128)S(1)} %inner_ratio.1.inner, f32[32,2048]{1,0:T(8,128)S(1)} %get-tuple-element.18.bottom, ...), custom_call_target="tpu_custom_call" | custom-call | flops 402653184 | bytes 1572864 | tf_op jit(solution)/shard_map/inner_log/pallas_call | solution.py:183
  33.4 0.7 %copy-done.7 = f32[1,64,1024]{2,1,0:T(8,128)} copy-done((f32[1,64,1024]{2,1,0:T(8,128)}, f32[1,64,1024]{2,1,0:T(8,128)S(1)}, u32[]{:S(2)}) %copy-start.7) | copy-done | bytes 262168
  34.1 1.5 %collective-permute-start.7 = (f32[64,1024]{1,0:T(8,128)}, f32[64,1024]{1,0:T(8,128)}, u32[]{:S(2)}, u32[]{:S(2)}) collective-permute-start(f32[64,1024]{1,0:T(8,128)} %bitcast.5), channel_id=1, source_target_pairs={{0,8},{8,0},{1,9},{9,1},{2,10},{10,2},{3,11},{11,3},{4,12},{12,4},... | collective-permute-start | bytes 786440 | tf_op jit(solution)/shard_map/ppermute | solution.py:216
  35.6 1.0 %collective-permute-done.4.below = f32[32,2048]{1,0:T(8,128)S(1)} collective-permute-done((f32[32,2048]{1,0:T(8,128)S(1)}, f32[32,2048]{1,0:T(8,128)S(1)}, u32[]{:S(2)}, u32[]{:S(2)}) %collective-permute-start.4) | collective-permute-done | bytes 262176 | tf_op jit(solution)/shard_map/ppermute | solution.py:210
  36.6 1.2 %rim_log.1 = (f32[64,2048]{1,0:T(8,128)S(1)}, f32[64,2048]{1,0:T(8,128)S(1)}, f32[1,64,1024]{2,1,0:T(8,128)}, f32[1,64,1024]{2,1,0:T(8,128)S(1)}) custom-call(f32[1,1]{1,0:T(1,128)} %bitcast.weight, f32[32,2048]{1,0:T(8,128)S(1)} %collective-permute-done.3.above, f32[32,2048]{1,0:T(8,128)S(1)} %get-tuple-element.19.top, f32[64,2048]{1,0:T(8,128)S(1)} %inner_ratio.1.inner, ...), custom_call_target="tpu_custom_call" | custom-call | flops 402653184 | bytes 1572864 | tf_op jit(solution)/shard_map/rim_log/pallas_call | solution.py:183
  37.8 0.7 copy-done.9
  38.5 1.5 %collective-permute-start.5 = (f32[64,1024]{1,0:T(8,128)}, f32[64,1024]{1,0:T(8,128)S(1)}, u32[]{:S(2)}, u32[]{:S(2)}) collective-permute-start(f32[64,1024]{1,0:T(8,128)} %bitcast.3), channel_id=1, source_target_pairs={{0,8},{8,0},{1,9},{9,1},{2,10},{10,2},{3,11},{11,3},{4,12},{12,4},... | collective-permute-start | bytes 786440 | tf_op jit(solution)/shard_map/ppermute | solution.py:216
  40.0 3.4 %collective-permute-done.7 = f32[64,1024]{1,0:T(8,128)} collective-permute-done((f32[64,1024]{1,0:T(8,128)}, f32[64,1024]{1,0:T(8,128)}, u32[]{:S(2)}, u32[]{:S(2)}) %collective-permute-start.7) | collective-permute-done | bytes 262176 | tf_op jit(solution)/shard_map/ppermute | solution.py:216
  43.5 1.0 %bitcast_reduce_fusion.1 = f32[8,1024]{1,0:T(8,128)S(1)} fusion(f32[64,1024]{1,0:T(8,128)} %collective-permute-done.7, f32[64,2048]{1,0:T(8,128)S(1)} %get-tuple-element.23, s32[]{:T(128)S(6)} %select_n.35), kind=kLoop, calls=%fused_computation.10 | loop fusion | flops 122880 | bytes 557060 | tf_op jit(solution)/shard_map/reduce_sum | solution.py:299
  44.5 2.4 %collective-permute-done.5 = f32[64,1024]{1,0:T(8,128)S(1)} collective-permute-done((f32[64,1024]{1,0:T(8,128)}, f32[64,1024]{1,0:T(8,128)S(1)}, u32[]{:S(2)}, u32[]{:S(2)}) %collective-permute-start.5) | collective-permute-done | bytes 262176 | tf_op jit(solution)/shard_map/ppermute | solution.py:216
  46.9 0.1 bitcast_reduce_fusion
  46.9 0.1 collective-permute-start.9
  47.0 1.6 %collective-permute-start.8 = (f32[64,1024]{1,0:T(8,128)S(1)}, f32[64,1024]{1,0:T(8,128)S(1)}, u32[]{:S(2)}, u32[]{:S(2)}) collective-permute-start(f32[64,1024]{1,0:T(8,128)S(1)} %bitcast.31), channel_id=1, source_target_pairs={{0,8},{8,0},{1,9},{9,1},{2,10},{10,2},{3,11},{11,3},{4,12},{12,4},... | collective-permute-start | bytes 786440 | tf_op jit(solution)/shard_map/ppermute | solution.py:216
  48.6 0.5 collective-permute-start.6
  49.1 2.4 %collective-permute-start.10 = (f32[8,128]{1,0:T(8,128)S(1)}, f32[8,128]{1,0:T(8,128)S(1)}, u32[]{:S(2)}, u32[]{:S(2)}) collective-permute-start(f32[8,128]{1,0:T(8,128)S(1)} %add.57), channel_id=1, source_target_pairs={{0,2},{2,0},{4,6},{6,4},{1,3},{3,1},{5,7},{7,5},{8,10},{10,8},{12,... | collective-permute-start | bytes 12296 | tf_op jit(solution)/shard_map/ppermute | solution.py:226
  51.5 1.5 %collective-permute-done.10 = f32[8,128]{1,0:T(8,128)S(1)} collective-permute-done((f32[8,128]{1,0:T(8,128)S(1)}, f32[8,128]{1,0:T(8,128)S(1)}, u32[]{:S(2)}, u32[]{:S(2)}) %collective-permute-start.10) | collective-permute-done | bytes 4128 | tf_op jit(solution)/shard_map/ppermute | solution.py:226
  53.1 3.0 %collective-permute-start.11 = (f32[8,128]{1,0:T(8,128)S(1)}, f32[8,128]{1,0:T(8,128)S(1)}, u32[]{:S(2)}, u32[]{:S(2)}) collective-permute-start(f32[8,128]{1,0:T(8,128)S(1)} %add.58), channel_id=1, source_target_pairs={{0,4},{2,6},{4,0},{6,2},{1,5},{3,7},{5,1},{7,3},{8,12},{10,14},{12... | collective-permute-start | bytes 12296 | tf_op jit(solution)/shard_map/ppermute | solution.py:226
  56.1 0.1 collective-permute-done.8
  56.2 5.2 %collective-permute-done.6 = f32[64,1024]{1,0:T(8,128)S(1)} collective-permute-done((f32[64,1024]{1,0:T(8,128)S(1)}, f32[64,1024]{1,0:T(8,128)S(1)}, u32[]{:S(2)}, u32[]{:S(2)}) %collective-permute-start.6) | collective-permute-done | bytes 262176 | tf_op jit(solution)/shard_map/ppermute | solution.py:216
  61.4 1.3 %fusion.3 = (f32[64,2048]{1,0:T(8,128)S(1)}, f32[64,2048]{1,0:T(8,128)S(1)}) fusion(f32[64,2048]{1,0:T(8,128)S(1)} %get-tuple-element.23, f32[64,1024]{1,0:T(8,128)} %collective-permute-done.7, f32[64,1024]{1,0:T(8,128)S(1)} %collective-permute-done.8, s32[]{:T(128)S(6)} %axis_index.23, s32[2048]{0:T(1024)S(1)} %get-tuple-element.42, ...), kind=kLoop, calls=%fused_computation.7 | loop fusion | flops 1310720 | bytes 3164164 | tf_op jit(solution)/shard_map/add | solution.py:315
  62.7 1.6 %collective-permute-start.12 = (f32[8,128]{1,0:T(8,128)S(1)}, f32[8,128]{1,0:T(8,128)S(1)}, u32[]{:S(2)}, u32[]{:S(2)}) collective-permute-start(f32[8,128]{1,0:T(8,128)S(1)} %add.59), channel_id=1, source_target_pairs={{0,8},{8,0},{1,9},{9,1},{2,10},{10,2},{3,11},{11,3},{4,12},{12,4},... | collective-permute-start | bytes 12296 | tf_op jit(solution)/shard_map/ppermute | solution.py:226
  64.3 0.1 slice_bitcast_fusion.3
  64.4 2.0 %collective-permute-done.12 = f32[8,128]{1,0:T(8,128)S(1)} collective-permute-done((f32[8,128]{1,0:T(8,128)S(1)}, f32[8,128]{1,0:T(8,128)S(1)}, u32[]{:S(2)}, u32[]{:S(2)}) %collective-permute-start.12) | collective-permute-done | bytes 4128 | tf_op jit(solution)/shard_map/ppermute | solution.py:226
  66.4 0.6 add_reduce_fusion
  67.7 1.1 %fusion = f32[128,2048]{1,0:T(8,128)} fusion(f32[32,2048]{1,0:T(8,128)S(1)} %get-tuple-element.38, f32[64,2048]{1,0:T(8,128)S(1)} %get-tuple-element.40, f32[32,2048]{1,0:T(8,128)S(1)} %get-tuple-element.39, f32[]{:T(128)S(6)} %div.20), kind=kLoop, calls=%fused_computation.1 | loop fusion | flops 786432 | bytes 2097156 | tf_op jit(solution)/shard_map/mul | solution.py:331
  68.8 1.1 %fusion.1 = f32[1,128,2048]{2,1,0:T(8,128)} fusion(f32[1,32,2048]{2,1,0:T(8,128)S(1)} %get-tuple-element.37, f32[1,64,2048]{2,1,0:T(8,128)S(1)} %bitcast.33, f32[1,32,2048]{2,1,0:T(8,128)S(1)} %get-tuple-element.36, f32[1,32,2048]{2,1,0:T(8,128)S(1)} %get-tuple-element.35, f32[1,64,2048]{2,1,0:T(8,128)S(1)} %bitcast.30, ...), kind=kLoop, calls=%fused_computation.3 | loop fusion | flops 1572864 | bytes 3145732 | tf_op jit(solution)/shard_map/sub | solution.py:332
  (27 shorter events, 0.1 us)
Async XLA Ops:
  0.6 22.5 %copy-start.4 = (bf16[192,256]{1,0:T(8,128)(2,1)S(1)}, bf16[192,256]{1,0:T(8,128)(2,1)}, u32[]{:S(2)}) copy-start(bf16[192,256]{1,0:T(8,128)(2,1)} %constant.45.clone.band) | copy-start | bytes 294916
  0.6 22.5 %copy-start.6 = (bf16[64,192]{1,0:T(8,128)(2,1)S(1)}, bf16[64,192]{1,0:T(8,128)(2,1)}, u32[]{:S(2)}) copy-start(bf16[64,192]{1,0:T(8,128)(2,1)} %constant.47.clone.rows_band) | copy-start | bytes 73732
  1.7 21.5 %copy-start = (f32[1,128,2048]{2,1,0:T(8,128)S(1)}, f32[1,128,2048]{2,1,0:T(8,128)}, u32[]{:S(2)}) copy-start(f32[1,128,2048]{2,1,0:T(8,128)} %param.6) | copy-start | bytes 3145732
  2.9 1.4 %collective-permute-start = (f32[128,128]{1,0:T(8,128)S(1)}, f32[128,128]{1,0:T(8,128)S(1)}, u32[]{:S(2)}, u32[]{:S(2)}) collective-permute-start(f32[128,128]{1,0:T(8,128)S(1)} %maximum_select_fusion.2), channel_id=1, source_target_pairs={{0,1},{1,0},{2,3},{3,2},{4,5},{5,4},{6,7},{7,6},{8,9},{9,8},{10,11... | collective-permute-start | bytes 196616 | tf_op jit(solution)/shard_map/ppermute | solution.py:199
  4.3 1.2 %copy-start.1 = (f32[1,128,2048]{2,1,0:T(8,128)S(1)}, f32[1,128,2048]{2,1,0:T(8,128)}, u32[]{:S(2)}) copy-start(f32[1,128,2048]{2,1,0:T(8,128)} %param.7) | copy-start | bytes 3145732
  5.6 0.9 %copy-start.3 = (bf16[192,256]{1,0:T(8,128)(2,1)S(1)}, bf16[192,256]{1,0:T(8,128)(2,1)}, u32[]{:S(2)}) copy-start(bf16[192,256]{1,0:T(8,128)(2,1)} %constant.45.clone.band) | copy-start | bytes 294916
  8.0 11.4 %collective-permute-start.1 = (f32[32,2176]{1,0:T(8,128)}, f32[32,2176]{1,0:T(8,128)S(1)}, u32[]{:S(2)}, u32[]{:S(2)}) collective-permute-start(f32[32,2176]{1,0:T(8,128)} %get-tuple-element.16), channel_id=1, source_target_pairs={{0,2},{2,4},{4,6},{1,3},{3,5},{5,7},{8,10},{10,12},{12,14},{9,11},... | collective-permute-start | bytes 835592 | tf_op jit(solution)/shard_map/ppermute | solution.py:210
  12.8 10.3 %collective-permute-start.2 = (f32[32,2176]{1,0:T(8,128)S(1)}, f32[32,2176]{1,0:T(8,128)S(1)}, u32[]{:S(2)}, u32[]{:S(2)}) collective-permute-start(f32[32,2176]{1,0:T(8,128)S(1)} %get-tuple-element.17), channel_id=1, source_target_pairs={{2,0},{4,2},{6,4},{3,1},{5,3},{7,5},{10,8},{12,10},{14,12},{11,9},... | collective-permute-start | bytes 835592 | tf_op jit(solution)/shard_map/ppermute | solution.py:210
  23.1 5.9 %copy-start.11 = (f32[2]{0:T(128)S(1)}, f32[2]{0:T(128)}, u32[]{:S(2)}) copy-start(f32[2]{0:T(128)} %param.8) | copy-start | bytes 28
  23.2 7.9 %copy-start.5 = (bf16[128,256]{1,0:T(8,128)(2,1)S(1)}, bf16[128,256]{1,0:T(8,128)(2,1)}, u32[]{:S(2)}) copy-start(bf16[128,256]{1,0:T(8,128)(2,1)} %constant.46.clone.rows_band) | copy-start | bytes 196612
  24.3 11.3 %collective-permute-start.3 = (f32[32,2048]{1,0:T(8,128)S(1)}, f32[32,2048]{1,0:T(8,128)S(1)}, u32[]{:S(2)}, u32[]{:S(2)}) collective-permute-start(f32[32,2048]{1,0:T(8,128)S(1)} %get-tuple-element.18.bottom), channel_id=1, source_target_pairs={{0,2},{2,4},{4,6},{1,3},{3,5},{5,7},{8,10},{10,12},{12,14},{9,11},... | collective-permute-start | bytes 786440 | tf_op jit(solution)/shard_map/ppermute | solution.py:210
  27.8 8.8 %collective-permute-start.4 = (f32[32,2048]{1,0:T(8,128)S(1)}, f32[32,2048]{1,0:T(8,128)S(1)}, u32[]{:S(2)}, u32[]{:S(2)}) collective-permute-start(f32[32,2048]{1,0:T(8,128)S(1)} %get-tuple-element.19.top), channel_id=1, source_target_pairs={{2,0},{4,2},{6,4},{3,1},{5,3},{7,5},{10,8},{12,10},{14,12},{11,9},... | collective-permute-start | bytes 786440 | tf_op jit(solution)/shard_map/ppermute | solution.py:210
  31.0 1.2 %copy-start.2 = (f32[1,128,2048]{2,1,0:T(8,128)S(1)}, f32[1,128,2048]{2,1,0:T(8,128)}, u32[]{:S(2)}) copy-start(f32[1,128,2048]{2,1,0:T(8,128)} %param.7) | copy-start | bytes 3145732
  33.4 0.7 %copy-start.7 = (f32[1,64,1024]{2,1,0:T(8,128)}, f32[1,64,1024]{2,1,0:T(8,128)S(1)}, u32[]{:S(2)}) copy-start(f32[1,64,1024]{2,1,0:T(8,128)S(1)} %get-tuple-element.25) | copy-start | bytes 786436
  34.1 9.4 %collective-permute-start.7 = (f32[64,1024]{1,0:T(8,128)}, f32[64,1024]{1,0:T(8,128)}, u32[]{:S(2)}, u32[]{:S(2)}) collective-permute-start(f32[64,1024]{1,0:T(8,128)} %bitcast.5), channel_id=1, source_target_pairs={{0,8},{8,0},{1,9},{9,1},{2,10},{10,2},{3,11},{11,3},{4,12},{12,4},... | collective-permute-start | bytes 786440 | tf_op jit(solution)/shard_map/ppermute | solution.py:216
  37.8 0.7 %copy-start.9 = (f32[1,64,1024]{2,1,0:T(8,128)}, f32[1,64,1024]{2,1,0:T(8,128)S(1)}, u32[]{:S(2)}) copy-start(f32[1,64,1024]{2,1,0:T(8,128)S(1)} %get-tuple-element.22) | copy-start | bytes 786436
  38.5 8.5 %copy-start.8 = (f32[1,64,1024]{2,1,0:T(8,128)S(1)}, f32[1,64,1024]{2,1,0:T(8,128)}, u32[]{:S(2)}) copy-start(f32[1,64,1024]{2,1,0:T(8,128)} %copy-done.7) | copy-start | bytes 786436
  38.5 10.1 %copy-start.10 = (f32[1,64,1024]{2,1,0:T(8,128)S(1)}, f32[1,64,1024]{2,1,0:T(8,128)}, u32[]{:S(2)}) copy-start(f32[1,64,1024]{2,1,0:T(8,128)} %copy-done.9) | copy-start | bytes 786436
  38.5 8.4 %collective-permute-start.5 = (f32[64,1024]{1,0:T(8,128)}, f32[64,1024]{1,0:T(8,128)S(1)}, u32[]{:S(2)}, u32[]{:S(2)}) collective-permute-start(f32[64,1024]{1,0:T(8,128)} %bitcast.3), channel_id=1, source_target_pairs={{0,8},{8,0},{1,9},{9,1},{2,10},{10,2},{3,11},{11,3},{4,12},{12,4},... | collective-permute-start | bytes 786440 | tf_op jit(solution)/shard_map/ppermute | solution.py:216
  46.9 2.2 %collective-permute-start.9 = (f32[8,128]{1,0:T(8,128)S(1)}, f32[8,128]{1,0:T(8,128)S(1)}, u32[]{:S(2)}, u32[]{:S(2)}) collective-permute-start(f32[8,128]{1,0:T(8,128)S(1)} %bitcast_reduce_fusion.2), channel_id=1, source_target_pairs={{0,1},{1,0},{2,3},{3,2},{4,5},{5,4},{6,7},{7,6},{8,9},{9,8},{10,11... | collective-permute-start | bytes 12296 | tf_op jit(solution)/shard_map/ppermute | solution.py:226
  47.0 9.2 %collective-permute-start.8 = (f32[64,1024]{1,0:T(8,128)S(1)}, f32[64,1024]{1,0:T(8,128)S(1)}, u32[]{:S(2)}, u32[]{:S(2)}) collective-permute-start(f32[64,1024]{1,0:T(8,128)S(1)} %bitcast.31), channel_id=1, source_target_pairs={{0,8},{8,0},{1,9},{9,1},{2,10},{10,2},{3,11},{11,3},{4,12},{12,4},... | collective-permute-start | bytes 786440 | tf_op jit(solution)/shard_map/ppermute | solution.py:216
  48.6 12.8 %collective-permute-start.6 = (f32[64,1024]{1,0:T(8,128)S(1)}, f32[64,1024]{1,0:T(8,128)S(1)}, u32[]{:S(2)}, u32[]{:S(2)}) collective-permute-start(f32[64,1024]{1,0:T(8,128)S(1)} %bitcast.32), channel_id=1, source_target_pairs={{0,8},{8,0},{1,9},{9,1},{2,10},{10,2},{3,11},{11,3},{4,12},{12,4},... | collective-permute-start | bytes 786440 | tf_op jit(solution)/shard_map/ppermute | solution.py:216
  49.1 3.9 %collective-permute-start.10 = (f32[8,128]{1,0:T(8,128)S(1)}, f32[8,128]{1,0:T(8,128)S(1)}, u32[]{:S(2)}, u32[]{:S(2)}) collective-permute-start(f32[8,128]{1,0:T(8,128)S(1)} %add.57), channel_id=1, source_target_pairs={{0,2},{2,0},{4,6},{6,4},{1,3},{3,1},{5,7},{7,5},{8,10},{10,8},{12,... | collective-permute-start | bytes 12296 | tf_op jit(solution)/shard_map/ppermute | solution.py:226
  53.1 9.6 %collective-permute-start.11 = (f32[8,128]{1,0:T(8,128)S(1)}, f32[8,128]{1,0:T(8,128)S(1)}, u32[]{:S(2)}, u32[]{:S(2)}) collective-permute-start(f32[8,128]{1,0:T(8,128)S(1)} %add.58), channel_id=1, source_target_pairs={{0,4},{2,6},{4,0},{6,2},{1,5},{3,7},{5,1},{7,3},{8,12},{10,14},{12... | collective-permute-start | bytes 12296 | tf_op jit(solution)/shard_map/ppermute | solution.py:226
  62.7 3.7 %collective-permute-start.12 = (f32[8,128]{1,0:T(8,128)S(1)}, f32[8,128]{1,0:T(8,128)S(1)}, u32[]{:S(2)}, u32[]{:S(2)}) collective-permute-start(f32[8,128]{1,0:T(8,128)S(1)} %add.59), channel_id=1, source_target_pairs={{0,8},{8,0},{1,9},{9,1},{2,10},{10,2},{3,11},{11,3},{4,12},{12,4},... | collective-permute-start | bytes 12296 | tf_op jit(solution)/shard_map/ppermute | solution.py:226

commit v2 on v1

v2 whole, which is shorter than its diff:
```python
import functools

import jax
import jax.numpy as jnp
import numpy as np
from jax import lax
from jax.experimental import pallas as pl
from jax.experimental.pallas import tpu as pltpu
from jax.sharding import PartitionSpec as P

HALF = 32
LANES = 128
kernel_sigma = 16.0


def taps_total():
    taps = np.arange(-HALF, HALF + 1).astype(np.float64)
    return float(np.sum(np.exp(-taps * taps / (2.0 * kernel_sigma * kernel_sigma))))


def band_matrix(shape, axis_in):
    places = lax.broadcasted_iota(jnp.int32, shape, axis_in) - lax.broadcasted_iota(jnp.int32, shape, 1 - axis_in)
    offsets = (places - HALF).astype(jnp.float32)
    entries = jnp.exp(-offsets * offsets / (2.0 * kernel_sigma * kernel_sigma)) / taps_total()
    return jnp.where(jnp.abs(offsets) <= HALF, entries, 0.0)


def column_band():
    high, low = split(band_matrix((LANES + 2 * HALF, LANES), 0))
    return jnp.concatenate([high, low], axis=1)


def row_band(rows_out):
    high, low = split(band_matrix((rows_out, rows_out + 2 * HALF), 1))
    return jnp.concatenate(
        [jnp.concatenate([high, high], axis=1), jnp.concatenate([low, jnp.zeros_like(low)], axis=1)], axis=0
    )


def split(values):
    high = values.astype(jnp.bfloat16)
    low = (values - high.astype(jnp.float32)).astype(jnp.bfloat16)
    return high, low


def dot(left, right):
    return jnp.dot(left, right, preferred_element_type=jnp.float32)


def column_block(window, band):
    high, low = split(window)
    depth = window.shape[1]
    both = dot(high, band[:depth])
    return both[:, :LANES] + both[:, LANES:] + dot(low, band[:depth, :LANES])


def row_block(window, band):
    high, low = split(window)
    rows = band.shape[0] // 2
    both = dot(band, jnp.concatenate([high, low], axis=0))
    return both[:rows] + both[rows:]


def edge_flags():
    place = lax.axis_index("cols")
    return (place > 0).astype(jnp.float32), (place < lax.axis_size("cols") - 1).astype(jnp.float32)


def row_parity():
    return lax.rem(lax.axis_index("rows"), 2)


def chunks(width, step):
    return [(start, min(start + step, width)) for start in range(0, width, step)]


def edge_sides():
    return [lax.axis_index("cols") == 0] if lax.axis_size("cols") == 2 else [True, False]


def edge_kernel(function, values, *refs):
    outs = refs[-len(edge_sides()) :]
    width = values.shape[1]
    for out, right in zip(outs, edge_sides()):
        start = pl.multiple_of(jnp.where(right, width - LANES, 0), LANES)
        out[...] = function(values[:, pl.ds(start, LANES)])


def spread_kernel(logs, across, wide):
    width = logs.shape[1]
    edge = 2 * HALF
    taps = column_band()
    wide[:, edge : edge + width] = jnp.exp(logs[...])
    for start in range(LANES, width, LANES):
        across[:, start : start + LANES] = column_block(wide[:, start : start + LANES + 2 * HALF], taps)


def spread_edge_kernel(partial, logs, from_left, from_right, across, first, second):
    has_left, has_right = edge_flags()
    height, width = logs.shape
    edge = 2 * HALF
    taps = column_band()
    across[...] = partial[...]
    left = jnp.concatenate([from_left[:, edge:] * has_left, jnp.exp(logs[:, :LANES])], axis=1)
    right = jnp.concatenate([jnp.exp(logs[:, width - edge :]), from_right[:, :edge] * has_right], axis=1)
    across[:, :LANES] = column_block(left, taps)
    across[:, width : width + LANES] = column_block(right, taps)
    odd = row_parity()
    first[...] = across[pl.ds(pl.multiple_of((1 - odd) * (height - HALF), HALF), HALF), :]
    second[...] = across[pl.ds(pl.multiple_of(odd * (height - HALF), HALF), HALF), :]


def ratio_rows(smooth, masses, from_left, from_right):
    has_left, has_right = edge_flags()
    edge = 2 * HALF
    rows = masses.shape[0]
    wide = jnp.concatenate(
        [
            from_left[:, LANES - HALF :] * has_left,
            masses,
            from_right[:, :HALF] * has_right,
            jnp.zeros((rows, edge), jnp.float32),
        ],
        axis=1,
    )
    return jnp.where(wide > 0.0, wide / smooth, 0.0)


def column_pass(ratios, taps, out):
    for start in range(0, out.shape[1], LANES):
        out[:, start : start + LANES] = column_block(ratios[:, start : start + LANES + 2 * HALF], taps)


def inner_ratio_kernel(across, masses, from_left, from_right, out, smooth, ratios):
    height = masses.shape[0]
    taps = row_band(out.shape[0])
    for start, stop in chunks(across.shape[1], 256):
        smooth[:, start:stop] = row_block(across[:, start:stop], taps)
    inner = slice(HALF, height - HALF)
    ratios[...] = ratio_rows(smooth[...], masses[inner, :], from_left[inner, :], from_right[inner, :])
    column_pass(ratios, column_band(), out)


def rim_ratio_kernel(
    after, across, first, second, masses, from_left, from_right, rims, sent_first, sent_second,
    smooth, ratios,
):
    height = masses.shape[0]
    taps = row_band(HALF)
    odd = row_parity()
    for start, stop in chunks(across.shape[1], 256):
        one, two = first[:, start:stop], second[:, start:stop]
        upper = jnp.concatenate([jnp.where(odd == 1, one, two), across[: 2 * HALF, start:stop]], axis=0)
        lower = jnp.concatenate(
            [across[height - 2 * HALF :, start:stop], jnp.where(odd == 1, two, one)], axis=0
        )
        smooth[:HALF, start:stop] = row_block(upper, taps)
        smooth[HALF:, start:stop] = row_block(lower, taps)
    ends = lambda ref: jnp.concatenate([ref[:HALF, :], ref[height - HALF :, :]], axis=0)
    ratios[...] = ratio_rows(smooth[...], ends(masses), ends(from_left), ends(from_right))
    column_pass(ratios, column_band(), rims)
    sent_first[...] = rims[pl.ds(pl.multiple_of((1 - odd) * HALF, HALF), HALF), :]
    sent_second[...] = rims[pl.ds(pl.multiple_of(odd * HALF, HALF), HALF), :]


def own_weight(weights):
    total = weights[0]
    for k in range(1, weights.shape[0]):
        total += weights[k]
    return jnp.full((1, 1), weights[lax.axis_index("hist")]) / jnp.full((1, 1), total)


def block_of(ref, place, share):
    return ref[:, pl.ds(pl.multiple_of(place * share, LANES), share)]


def others_first(own, first):
    count = lax.axis_size("hist")
    share = own.shape[1] // count
    for shift in range(1, count):
        other = lax.rem(lax.axis_index("hist") + shift, count)
        first[shift - 1] = block_of(own, other, share)


def inner_log_kernel(weights, rims, inner, logs, smooth, own, first):
    height = logs.shape[0]
    taps = row_band(inner.shape[0])
    for start, stop in chunks(inner.shape[1], 256):
        window = jnp.concatenate([rims[:HALF, start:stop], inner[:, start:stop], rims[HALF:, start:stop]], axis=0)
        smooth[:, start:stop] = jnp.log(row_block(window, taps))
    own[...] = own_weight(weights) * (logs[HALF : height - HALF, :] + smooth[...])
    others_first(own, first)


def rim_log_kernel(
    weights, from_first, from_second, rims, inner, logs, smooth, own, first
):
    height = logs.shape[0]
    depth = inner.shape[0]
    taps = row_band(HALF)
    odd = row_parity()
    for start, stop in chunks(inner.shape[1], 256):
        one, two = from_first[:, start:stop], from_second[:, start:stop]
        above, below = jnp.where(odd == 1, one, two), jnp.where(odd == 1, two, one)
        upper = jnp.concatenate([above, rims[:HALF, start:stop], inner[:HALF, start:stop]], axis=0)
        lower = jnp.concatenate([inner[depth - HALF :, start:stop], rims[HALF:, start:stop], below], axis=0)
        smooth[:HALF, start:stop] = jnp.log(row_block(upper, taps))
        smooth[HALF:, start:stop] = jnp.log(row_block(lower, taps))
    log_rows = jnp.concatenate([logs[:HALF, :], logs[height - HALF :, :]], axis=0)
    own[...] = own_weight(weights) * (log_rows + smooth[...])
    others_first(own, first)


def others_later(inner_own, rim_own, later):
    height = later.shape[1]
    count = lax.axis_size("hist")
    share = rim_own.shape[1] // count
    for shift in range(1, count):
        other = lax.rem(lax.axis_index("hist") + shift, count)
        for step in range(1, count):
            block = lax.rem(other + step, count)
            slot = slice((step - 1) * share, step * share)
            rim = block_of(rim_own, block, share)
            later[shift - 1, :HALF, slot] = rim[:HALF]
            later[shift - 1, HALF : height - HALF, slot] = block_of(inner_own, block, share)
            later[shift - 1, height - HALF :, slot] = rim[HALF:]


def folded(values):
    rows, width = values.shape
    total = jnp.sum(values.reshape(rows // 8, 8, width), axis=0)
    return sum(total[:, start : start + LANES] for start in range(0, width, LANES))


def mean_part(own, smooth, arrived, mean, change):
    share = mean.shape[1]
    place = lax.axis_index("hist")
    log_mean = block_of(own, place, share) + sum(ref[...] for ref in arrived)
    values = jnp.exp(log_mean)
    mean[...] = values
    change[...] = log_mean - block_of(smooth, place, share)
    return folded(values)


def inner_mean_kernel(own, smooth, rim_own, *refs):
    arrived, (mean, change, partial, later) = refs[:-4], refs[-4:]
    others_later(own, rim_own, later)
    partial[...] = mean_part(own, smooth, arrived, mean, change)


def rim_mean_kernel(own, smooth, before, *refs):
    arrived, (mean, change, partial) = refs[:-3], refs[-3:]
    partial[...] = before[...] + mean_part(own, smooth, arrived, mean, change)


def later_mean_kernel(rim_own, rim_smooth, inner_own, inner_smooth, *refs):
    arrived, (mean, change) = refs[:-2], refs[-2:]
    count = lax.axis_size("hist")
    height = mean.shape[0]
    share = rim_own.shape[1] // count
    for step in range(1, count):
        block = lax.rem(lax.axis_index("hist") + step, count)
        slot = slice((step - 1) * share, step * share)
        for rows, own, smooth, part in (
            (slice(0, HALF), rim_own, rim_smooth, slice(0, HALF)),
            (slice(HALF, height - HALF), inner_own, inner_smooth, slice(None)),
            (slice(height - HALF, height), rim_own, rim_smooth, slice(HALF, 2 * HALF)),
        ):
            lanes = pl.ds(pl.multiple_of(block * share, LANES), share)
            log_mean = own[part, lanes] + sum(ref[rows, slot] for ref in arrived)
            mean[rows, slot] = jnp.exp(log_mean)
            change[rows, slot] = log_mean - smooth[part, lanes]


def final_kernel(
    cells, total, rim_mean, rim_change, inner_mean, inner_change, later_mean, later_change, barycenter, new_logs,
    stage, sems,
):
    count = lax.axis_size("hist")
    height, width = barycenter.shape
    share = width // count
    scale = cells / jnp.sum(total[...], axis=(0, 1), keepdims=True)
    log_scale = jnp.log(scale)
    copies = []
    for k, (out, rim, inner, later, apply) in enumerate(
        (
            (barycenter, rim_mean, inner_mean, later_mean, lambda x: x * scale),
            (new_logs, rim_change, inner_change, later_change, lambda x: x + log_scale),
        )
    ):
        for step in range(count):
            slot = slice(step * share, (step + 1) * share)
            if step == 0:
                stage[k, :HALF, slot] = apply(rim[:HALF, :])
                stage[k, HALF : height - HALF, slot] = apply(inner[...])
                stage[k, height - HALF :, slot] = apply(rim[HALF:, :])
            else:
                stage[k, :, slot] = apply(later[:, (step - 1) * share : step * share])
            block = lax.rem(lax.axis_index("hist") + step, count)
            lanes = pl.ds(pl.multiple_of(block * share, LANES), share)
            copy = pltpu.make_async_copy(stage.at[k, :, slot], out.at[:, lanes], sems.at[k, step])
            copy.start()
            copies.append(copy)
    for copy in copies:
        copy.wait()


def call(kernel, name, args, outs, scratch=(), scalars=0, cost=0, far_in=(), far_out=False, sems=None,
         room=32):
    f32 = lambda shape: jax.ShapeDtypeStruct(shape, jnp.float32)
    near = pl.BlockSpec(memory_space=pltpu.VMEM)
    far = pl.BlockSpec(memory_space=pltpu.HBM)
    scalar = pl.BlockSpec(memory_space=pltpu.SMEM)
    return pl.pallas_call(
        kernel,
        name=name,
        out_shape=tuple(f32(shape) for shape in outs),
        in_specs=[scalar if k < scalars else far if k in far_in else near for k in range(len(args))],
        out_specs=tuple(far if far_out else near for _ in outs),
        scratch_shapes=[pltpu.VMEM(shape, jnp.float32) for shape in scratch]
        + ([pltpu.SemaphoreType.DMA(sems)] if sems else []),
        compiler_params=pltpu.CompilerParams(vmem_limit_bytes=room * 1024 * 1024),
        cost_estimate=pl.CostEstimate(flops=5 * cost, bytes_accessed=cost // 256, transcendentals=0),
    )(*args)


def swap_columns(edges):
    count = lax.axis_size("cols")
    if count == 2:
        got = lax.ppermute(edges[0], "cols", [(0, 1), (1, 0)])
        return got, got
    steps = [(i, i + 1) for i in range(count - 1)]
    right_edge, left_edge = edges
    return (
        lax.ppermute(right_edge, "cols", steps),
        lax.ppermute(left_edge, "cols", [(b, a) for a, b in steps]),
    )


def swap_rows(first, second):
    count = lax.axis_size("rows")
    pairs = lambda start: [
        pair for i in range(start, count - 1, 2) for pair in ((i, i + 1), (i + 1, i))
    ]
    got_second = lax.ppermute(second, "rows", pairs(1))
    got_first = lax.ppermute(first, "rows", pairs(0))
    return got_first, got_second


def share_over_hist(parts):
    count = lax.axis_size("hist")
    return [
        lax.ppermute(parts[shift - 1], "hist", [(i, (i + shift) % count) for i in range(count)])
        for shift in range(1, count)
    ]


def total_over(values, axes):
    for axis in axes:
        count = lax.axis_size(axis)
        if count & (count - 1):
            values = lax.psum(values, axis)
            continue
        span = 1
        while span < count:
            values = values + lax.ppermute(values, axis, [(i, i ^ span) for i in range(count)])
            span *= 2
    return values


def body(hists, log_scaling_fields, histogram_weight_list):
    masses = hists[0]
    logs = log_scaling_fields[0]
    height, width = masses.shape
    count = lax.axis_size("hist")
    edge = 2 * HALF
    inner = height - edge
    share = width // count
    wide = width + LANES
    matmul = 2 * height * width * 3 * 256

    sides = 1 if lax.axis_size("cols") == 2 else 2
    tiles = [(height, LANES)] * sides
    edges = call(functools.partial(edge_kernel, jnp.exp), "log_edges", (logs,), tiles)
    from_left, from_right = swap_columns(edges)
    (partial,) = call(spread_kernel, "spread", (logs,), [(height, wide)], [(height, width + LANES)], cost=matmul)
    across, first, second = call(
        spread_edge_kernel, "spread_edge", (partial, logs, from_left, from_right),
        [(height, wide), (HALF, wide), (HALF, wide)], cost=matmul // 8,
    )
    edges = call(functools.partial(edge_kernel, lambda x: x), "mass_edges", (masses, first), tiles)
    from_left, from_right = swap_columns(edges)
    first, second = swap_rows(first, second)
    (inside,) = call(
        inner_ratio_kernel, "inner_ratio", (across, masses, from_left, from_right),
        [(inner, width)], [(inner, wide), (inner, wide)], cost=matmul,
    )
    rims, first, second = call(
        rim_ratio_kernel, "rim_ratio",
        (inside, across, first, second, masses, from_left, from_right),
        [(edge, width), (HALF, width), (HALF, width)], [(edge, wide), (edge, wide)], cost=matmul,
    )
    first, second = swap_rows(first, second)

    weights = histogram_weight_list
    inner_smooth, inner_own, inner_first = call(
        inner_log_kernel, "inner_log", (weights, rims, inside, logs),
        [(inner, width), (inner, width), (count - 1, inner, share)], scalars=1, cost=matmul,
    )
    inner_first = share_over_hist(inner_first)
    rim_smooth, rim_own, rim_first = call(
        rim_log_kernel, "rim_log", (weights, first, second, rims, inside, logs),
        [(edge, width), (edge, width), (count - 1, edge, share)], scalars=1, cost=matmul,
    )
    rim_first = share_over_hist(rim_first)
    inner_mean, inner_change, mass, later = call(
        inner_mean_kernel, "inner_mean", (inner_own, inner_smooth, rim_own, *inner_first),
        [(inner, share), (inner, share), (8, LANES), (count - 1, height, width - share)], cost=matmul // 4,
    )
    later = share_over_hist(later)
    rim_mean, rim_change, mass = call(
        rim_mean_kernel, "rim_mean", (rim_own, rim_smooth, mass, *rim_first),
        [(edge, share), (edge, share), (8, LANES)], cost=10 * matmul,
    )
    mass = total_over(mass, ("cols", "rows", "hist"))
    later_mean, later_change = call(
        later_mean_kernel, "later_mean", (rim_own, rim_smooth, inner_own, inner_smooth, *later),
        [(height, width - share), (height, width - share)], cost=matmul // 4,
    )
    cells = height * lax.axis_size("rows") * width * lax.axis_size("cols")
    barycenter, new_logs = call(
        functools.partial(final_kernel, float(cells)), "final",
        (mass, rim_mean, rim_change, inner_mean, inner_change, later_mean, later_change),
        [(height, width), (height, width)], [(2, height, width)], far_out=True, sems=(2, count), cost=matmul // 4,
    )
    return (barycenter, new_logs[None])


def solution(mesh):
    return jax.shard_map(
        body,
        mesh=mesh,
        in_specs=(
            P("hist", ("groups", "rows"), "cols"),
            P("hist", ("groups", "rows"), "cols"),
            P(),
        ),
        out_specs=(P(("groups", "rows"), "cols"), P("hist", ("groups", "rows"), "cols")),
        check_vma=False,
    )
```

time: 70.3 us -> 52.3 us (0.74)
  other arithmetic: 5.86 us -> 0.01 us
  waiting for transfers between devices: 25.6 us -> 20.5 us
  local copies, waits for them, and re-layouts: 6.14 us -> 1.24 us
  between operations: 2.91 us -> 0.77 us
  Pallas kernels: 5.8 us -> 7.09 us
  starting transfers between devices: 23.5 us -> 22.5 us
    ppermute x4 -> x3, waiting for transfers between devices: 11.2 us -> 6.1 us  [share_over_hist(): lax.ppermute(parts[shift - 1], 'hist', [(i, (i + shift) % count) for i in...]
    ppermute x5 -> x6, waiting for transfers between devices: 10.9 us -> 7.96 us  [the longest x2 6.56 us: swap_rows(): got_first = lax.ppermute(first, 'rows', pairs(0))]
    ppermute x4, waiting for transfers between devices: 3.54 us -> 6.48 us  [total_over(): lax.ppermute(values, axis, [(i, i ^ span) for i in range(count)])]
    unnamed x24 -> x8, local copies, waits for them, and re-layouts: 3.89 us -> 1.24 us
    reduce_sum x5 -> x0, other arithmetic: 2.27 us -> none  [the longest x1 1 us: body(): jnp.sum(jnp.exp(own_share(in_own, in_first)).reshape(-1, 8, share), axis=0)]
    ppermute x5 -> x6, starting transfers between devices: 11.4 us -> 9.72 us  [the longest x2 7.8 us: swap_rows(): got_first = lax.ppermute(first, 'rows', pairs(0))]
    pallas_call x5 -> x12, Pallas kernels: 5.8 us -> 7.09 us  [call(): pl.pallas_call(kernel, name=name, out_shape=tuple((f32(shape) for shape i...]
    add x1 -> x0, other arithmetic: 1.26 us -> none  [log_mean(): return own + arrived]
  transfers between devices with their start and end apart: 13 -> 13, of which waited for: 10 -> 10; matrix products, arithmetic and copies ran while one was open for 4% -> 0% of each run, Pallas kernels for 5% -> 8%
where the time goes in v2:
time: 52.3 us; the launch traced here: 52.1 us
  starting transfers between devices  22.5 us (43%)
  waiting for transfers between devices  20.5 us (39%)
  Pallas kernels  7.09 us (14%)
  local copies, waits for them, and re-layouts  1.24 us (2%)
  between operations  0.77 us (1%)
    ppermute x4, starting transfers between devices, total_over(): lax.ppermute(values, axis, [(i, i ^ span) for i in range(count)])  8.08 us
    ppermute x2, starting transfers between devices, swap_rows(): got_first = lax.ppermute(first, 'rows', pairs(0))  7.8 us
    pallas_call x12, Pallas kernels, call(): pl.pallas_call(kernel, name=name, out_shape=tuple((f32(shape) for shape i...  7.09 us
    ppermute x2, waiting for transfers between devices, swap_rows(): got_first = lax.ppermute(first, 'rows', pairs(0))  6.56 us
    ppermute x4, waiting for transfers between devices, total_over(): lax.ppermute(values, axis, [(i, i ^ span) for i in range(count)])  6.48 us
    ppermute x3, waiting for transfers between devices, share_over_hist(): lax.ppermute(parts[shift - 1], 'hist', [(i, (i + shift) % count) for i in...  6.1 us
    ppermute x3, starting transfers between devices, share_over_hist(): lax.ppermute(parts[shift - 1], 'hist', [(i, (i + shift) % count) for i in...  4.66 us
    ppermute x2, waiting for transfers between devices, swap_columns(): got = lax.ppermute(edges[0], 'cols', [(0, 1), (1, 0)])  1.39 us
  transfers between devices with their start and end apart: 13, of which 10 were waited for; matrix products, arithmetic and copies ran while one was open for 0% of the time, Pallas kernels for 8%

profile of v2, /device:TPU:0, one launch (start us, length us, event | category | flops | bytes accessed | tf_op | source)
XLA Modules:
  0.0 52.1 jit_solution(9815915572712788509)
XLA Ops:
  0.6 0.0 copy-start
  0.6 1.2 %copy-done = f32[1,128,2048]{2,1,0:T(8,128)S(1)} copy-done((f32[1,128,2048]{2,1,0:T(8,128)S(1)}, f32[1,128,2048]{2,1,0:T(8,128)}, u32[]{:S(2)}) %copy-start) | copy-done | bytes 1048600
  1.9 0.5 collective-permute-start
  2.4 0.7 %spread.1.partial = f32[128,2176]{1,0:T(8,128)S(1)} custom-call(f32[128,2048]{1,0:T(8,128)S(1)} %bitcast.7), custom_call_target="tpu_custom_call" | custom-call | flops 2013265920 | bytes 1572864 | tf_op jit(solution)/shard_map/spread/pallas_call | solution.py:314
  3.1 0.0 copy-start.2
  3.2 0.1 collective-permute-done.from_left.from_right
  3.3 0.3 spread_edge.1
  3.6 3.0 %collective-permute-start.2 = (f32[32,2176]{1,0:T(8,128)S(1)}, f32[32,2176]{1,0:T(8,128)S(1)}, u32[]{:S(2)}, u32[]{:S(2)}) collective-permute-start(f32[32,2176]{1,0:T(8,128)S(1)} %get-tuple-element.26.refs_0_), channel_id=1, source_target_pairs={{0,2},{2,0},{4,6},{6,4},{1,3},{3,1},{5,7},{7,5},{8,10},{10,8},{12,... | collective-permute-start | bytes 835592 | tf_op jit(solution)/shard_map/ppermute | solution.py:346
  6.6 0.7 %collective-permute-start.3 = (f32[32,2176]{1,0:T(8,128)S(1)}, f32[32,2176]{1,0:T(8,128)S(1)}, u32[]{:S(2)}, u32[]{:S(2)}) collective-permute-start(f32[32,2176]{1,0:T(8,128)S(1)} %get-tuple-element.27), channel_id=1, source_target_pairs={{2,4},{4,2},{3,5},{5,3},{10,12},{12,10},{11,13},{13,11},{18,20},{2... | collective-permute-start | bytes 835592 | tf_op jit(solution)/shard_map/ppermute | solution.py:345
  7.3 0.0 copy-done.2
  7.3 0.1 collective-permute-start.1
  7.4 1.2 %collective-permute-done.1.from_left.from_right = f32[128,128]{1,0:T(8,128)S(1)} collective-permute-done((f32[128,128]{1,0:T(8,128)S(1)}, f32[128,128]{1,0:T(8,128)S(1)}, u32[]{:S(2)}, u32[]{:S(2)}) %collective-permute-start.1) | collective-permute-done | bytes 65568 | tf_op jit(solution)/shard_map/ppermute | solution.py:330
  8.6 0.9 %inner_ratio.1.after.inner = f32[64,2048]{1,0:T(8,128)S(1)} custom-call(f32[128,2176]{1,0:T(8,128)S(1)} %get-tuple-element.25.across, f32[128,2048]{1,0:T(8,128)S(1)} %bitcast.12, f32[128,128]{1,0:T(8,128)S(1)} %collective-permute-done.1.from_left.from_right, f32[128,128]{1,0:T(8,128)S(1)} %collective-permute-done.1.from_left.from_right), custom_call_target="tpu_custom_call" | custom-call | flops 2013265920 | bytes 1572864 | tf_op jit(solution)/shard_map/inner_ratio/pallas_call | solution.py:314
  9.6 0.0 copy-start.1
  9.6 0.0 copy-start.3
  9.6 4.0 %collective-permute-done.2.first = f32[32,2176]{1,0:T(8,128)S(1)} collective-permute-done((f32[32,2176]{1,0:T(8,128)S(1)}, f32[32,2176]{1,0:T(8,128)S(1)}, u32[]{:S(2)}, u32[]{:S(2)}) %collective-permute-start.2) | collective-permute-done | bytes 278560 | tf_op jit(solution)/shard_map/ppermute | solution.py:346
  13.6 0.0 collective-permute-done.3.second
  13.6 1.2 %rim_ratio.1 = (f32[64,2048]{1,0:T(8,128)S(1)}, f32[32,2048]{1,0:T(8,128)S(1)}, f32[32,2048]{1,0:T(8,128)S(1)}) custom-call(f32[64,2048]{1,0:T(8,128)S(1)} %inner_ratio.1.after.inner, f32[128,2176]{1,0:T(8,128)S(1)} %get-tuple-element.25.across, f32[32,2176]{1,0:T(8,128)S(1)} %collective-permute-done.2.first, f32[32,2176]{1,0:T(8,128)S(1)} %collective-permute-done.3.second, ...), custom_call_target="tpu_custom_call" | custom-call | flops 2013265920 | bytes 1572864 | tf_op jit(solution)/shard_map/rim_ratio/pallas_call | solution.py:314
  14.8 4.8 %collective-permute-start.4 = (f32[32,2048]{1,0:T(8,128)S(1)}, f32[32,2048]{1,0:T(8,128)S(1)}, u32[]{:S(2)}, u32[]{:S(2)}) collective-permute-start(f32[32,2048]{1,0:T(8,128)S(1)} %get-tuple-element.28), channel_id=1, source_target_pairs={{0,2},{2,0},{4,6},{6,4},{1,3},{3,1},{5,7},{7,5},{8,10},{10,8},{12,... | collective-permute-start | bytes 786440 | tf_op jit(solution)/shard_map/ppermute | solution.py:346
  19.6 0.7 %collective-permute-start.5 = (f32[32,2048]{1,0:T(8,128)S(1)}, f32[32,2048]{1,0:T(8,128)S(1)}, u32[]{:S(2)}, u32[]{:S(2)}) collective-permute-start(f32[32,2048]{1,0:T(8,128)S(1)} %get-tuple-element.29), channel_id=1, source_target_pairs={{2,4},{4,2},{3,5},{5,3},{10,12},{12,10},{11,13},{13,11},{18,20},{2... | collective-permute-start | bytes 786440 | tf_op jit(solution)/shard_map/ppermute | solution.py:345
  20.3 0.0 copy-done.1
  20.3 0.0 copy-done.3
  20.3 1.0 %inner_log.1 = (f32[64,2048]{1,0:T(8,128)S(1)}, f32[64,2048]{1,0:T(8,128)S(1)}, f32[1,64,1024]{2,1,0:T(8,128)S(1)}) custom-call(f32[2]{0:T(128)S(1)} %copy-done.3, f32[64,2048]{1,0:T(8,128)S(1)} %get-tuple-element.30.rims, f32[64,2048]{1,0:T(8,128)S(1)} %inner_ratio.1.after.inner, f32[128,2048]{1,0:T(8,128)S(1)} %bitcast.9), custom_call_target="tpu_custom_call" | custom-call | flops 2013265920 | bytes 1572864 | tf_op jit(solution)/shard_map/inner_log/pallas_call | solution.py:314
  21.3 1.6 %collective-permute-start.6 = (f32[64,1024]{1,0:T(8,128)S(1)}, f32[64,1024]{1,0:T(8,128)S(1)}, u32[]{:S(2)}, u32[]{:S(2)}) collective-permute-start(f32[64,1024]{1,0:T(8,128)S(1)} %bitcast.15), channel_id=1, source_target_pairs={{0,8},{8,0},{1,9},{9,1},{2,10},{10,2},{3,11},{11,3},{4,12},{12,4},... | collective-permute-start | bytes 786440 | tf_op jit(solution)/shard_map/ppermute | solution.py:353
  22.8 2.6 %collective-permute-done.4.from_first = f32[32,2048]{1,0:T(8,128)S(1)} collective-permute-done((f32[32,2048]{1,0:T(8,128)S(1)}, f32[32,2048]{1,0:T(8,128)S(1)}, u32[]{:S(2)}, u32[]{:S(2)}) %collective-permute-start.4) | collective-permute-done | bytes 262176 | tf_op jit(solution)/shard_map/ppermute | solution.py:346
  25.4 0.0 collective-permute-done.5.from_second
  25.4 1.1 %rim_log.1 = (f32[64,2048]{1,0:T(8,128)S(1)}, f32[64,2048]{1,0:T(8,128)S(1)}, f32[1,64,1024]{2,1,0:T(8,128)S(1)}) custom-call(f32[2]{0:T(128)S(1)} %copy-done.3, f32[32,2048]{1,0:T(8,128)S(1)} %collective-permute-done.4.from_first, f32[32,2048]{1,0:T(8,128)S(1)} %collective-permute-done.5.from_second, f32[64,2048]{1,0:T(8,128)S(1)} %get-tuple-element.30.rims, ...), custom_call_target="tpu_custom_call" | custom-call | flops 2013265920 | bytes 1572864 | tf_op jit(solution)/shard_map/rim_log/pallas_call | solution.py:314
  26.5 1.6 %collective-permute-start.7 = (f32[64,1024]{1,0:T(8,128)S(1)}, f32[64,1024]{1,0:T(8,128)S(1)}, u32[]{:S(2)}, u32[]{:S(2)}) collective-permute-start(f32[64,1024]{1,0:T(8,128)S(1)} %bitcast.16), channel_id=1, source_target_pairs={{0,8},{8,0},{1,9},{9,1},{2,10},{10,2},{3,11},{11,3},{4,12},{12,4},... | collective-permute-start | bytes 786440 | tf_op jit(solution)/shard_map/ppermute | solution.py:353
  28.1 1.2 %collective-permute-done.6.refs_0_ = f32[64,1024]{1,0:T(8,128)S(1)} collective-permute-done((f32[64,1024]{1,0:T(8,128)S(1)}, f32[64,1024]{1,0:T(8,128)S(1)}, u32[]{:S(2)}, u32[]{:S(2)}) %collective-permute-start.6) | collective-permute-done | bytes 262176 | tf_op jit(solution)/shard_map/ppermute | solution.py:353
  29.3 0.1 inner_mean.1
  29.4 1.6 %collective-permute-start.12 = (f32[128,1024]{1,0:T(8,128)S(1)}, f32[128,1024]{1,0:T(8,128)S(1)}, u32[]{:S(2)}, u32[]{:S(2)}) collective-permute-start(f32[128,1024]{1,0:T(8,128)S(1)} %bitcast.14), channel_id=1, source_target_pairs={{0,8},{8,0},{1,9},{9,1},{2,10},{10,2},{3,11},{11,3},{4,12},{12,4},... | collective-permute-start | bytes 1572872 | tf_op jit(solution)/shard_map/ppermute | solution.py:353
  30.9 4.9 %collective-permute-done.7.refs_0_ = f32[64,1024]{1,0:T(8,128)S(1)} collective-permute-done((f32[64,1024]{1,0:T(8,128)S(1)}, f32[64,1024]{1,0:T(8,128)S(1)}, u32[]{:S(2)}, u32[]{:S(2)}) %collective-permute-start.7) | collective-permute-done | bytes 262176 | tf_op jit(solution)/shard_map/ppermute | solution.py:353
  35.8 0.1 rim_mean.1
  35.9 0.1 collective-permute-start.8
  36.0 1.2 %collective-permute-done.8 = f32[8,128]{1,0:T(8,128)S(1)} collective-permute-done((f32[8,128]{1,0:T(8,128)S(1)}, f32[8,128]{1,0:T(8,128)S(1)}, u32[]{:S(2)}, u32[]{:S(2)}) %collective-permute-start.8) | collective-permute-done | bytes 4128 | tf_op jit(solution)/shard_map/ppermute | solution.py:366
  37.1 3.6 %collective-permute-start.9 = (f32[8,128]{1,0:T(8,128)S(1)}, f32[8,128]{1,0:T(8,128)S(1)}, u32[]{:S(2)}, u32[]{:S(2)}) collective-permute-start(f32[8,128]{1,0:T(8,128)S(1)} %add.12), channel_id=1, source_target_pairs={{0,2},{2,0},{4,6},{6,4},{1,3},{3,1},{5,7},{7,5},{8,10},{10,8},{12,... | collective-permute-start | bytes 12296 | tf_op jit(solution)/shard_map/ppermute | solution.py:366
  40.8 1.6 %collective-permute-done.9 = f32[8,128]{1,0:T(8,128)S(1)} collective-permute-done((f32[8,128]{1,0:T(8,128)S(1)}, f32[8,128]{1,0:T(8,128)S(1)}, u32[]{:S(2)}, u32[]{:S(2)}) %collective-permute-start.9) | collective-permute-done | bytes 4128 | tf_op jit(solution)/shard_map/ppermute | solution.py:366
  42.4 2.9 %collective-permute-start.10 = (f32[8,128]{1,0:T(8,128)S(1)}, f32[8,128]{1,0:T(8,128)S(1)}, u32[]{:S(2)}, u32[]{:S(2)}) collective-permute-start(f32[8,128]{1,0:T(8,128)S(1)} %add.13), channel_id=1, source_target_pairs={{0,4},{2,6},{4,0},{6,2},{1,5},{3,7},{5,1},{7,3},{8,12},{10,14},{12... | collective-permute-start | bytes 12296 | tf_op jit(solution)/shard_map/ppermute | solution.py:366
  45.3 1.6 %collective-permute-done.10 = f32[8,128]{1,0:T(8,128)S(1)} collective-permute-done((f32[8,128]{1,0:T(8,128)S(1)}, f32[8,128]{1,0:T(8,128)S(1)}, u32[]{:S(2)}, u32[]{:S(2)}) %collective-permute-start.10) | collective-permute-done | bytes 4128 | tf_op jit(solution)/shard_map/ppermute | solution.py:366
  46.9 1.5 %collective-permute-start.11 = (f32[8,128]{1,0:T(8,128)S(1)}, f32[8,128]{1,0:T(8,128)S(1)}, u32[]{:S(2)}, u32[]{:S(2)}) collective-permute-start(f32[8,128]{1,0:T(8,128)S(1)} %add.14), channel_id=1, source_target_pairs={{0,8},{8,0},{1,9},{9,1},{2,10},{10,2},{3,11},{11,3},{4,12},{12,4},... | collective-permute-start | bytes 12296 | tf_op jit(solution)/shard_map/ppermute | solution.py:366
  48.4 2.1 %collective-permute-done.11 = f32[8,128]{1,0:T(8,128)S(1)} collective-permute-done((f32[8,128]{1,0:T(8,128)S(1)}, f32[8,128]{1,0:T(8,128)S(1)}, u32[]{:S(2)}, u32[]{:S(2)}) %collective-permute-start.11) | collective-permute-done | bytes 4128 | tf_op jit(solution)/shard_map/ppermute | solution.py:366
  50.5 0.0 collective-permute-done.12.refs_0_
  50.5 0.1 later_mean.1
  50.6 1.5 %final.1 = (f32[128,2048]{1,0:T(8,128)}, f32[128,2048]{1,0:T(8,128)}) custom-call(f32[8,128]{1,0:T(8,128)S(1)} %add.15.total, f32[64,1024]{1,0:T(8,128)S(1)} %get-tuple-element.39.rim_mean, f32[64,1024]{1,0:T(8,128)S(1)} %get-tuple-element.40.rim_change, f32[64,1024]{1,0:T(8,128)S(1)} %get-tuple-element.41.inner_mean, ...), custom_call_target="tpu_custom_call" | custom-call | flops 503316480 | bytes 393216 | tf_op jit(solution)/shard_map/final/pallas_call | solution.py:314
  (6 shorter events, 0.0 us)
Async XLA Ops:
  0.6 1.2 %copy-start = (f32[1,128,2048]{2,1,0:T(8,128)S(1)}, f32[1,128,2048]{2,1,0:T(8,128)}, u32[]{:S(2)}) copy-start(f32[1,128,2048]{2,1,0:T(8,128)} %param.4) | copy-start | bytes 3145732
  1.9 1.4 %collective-permute-start = (f32[128,128]{1,0:T(8,128)S(1)}, f32[128,128]{1,0:T(8,128)S(1)}, u32[]{:S(2)}, u32[]{:S(2)}) collective-permute-start(f32[128,128]{1,0:T(8,128)S(1)} %log_edges.1), channel_id=1, source_target_pairs={{0,1},{1,0},{2,3},{3,2},{4,5},{5,4},{6,7},{7,6},{8,9},{9,8},{10,11... | collective-permute-start | bytes 196616 | tf_op jit(solution)/shard_map/ppermute | solution.py:330
  3.1 4.1 %copy-start.2 = (f32[1,128,2048]{2,1,0:T(8,128)S(1)}, f32[1,128,2048]{2,1,0:T(8,128)}, u32[]{:S(2)}) copy-start(f32[1,128,2048]{2,1,0:T(8,128)} %param.3) | copy-start | bytes 3145732
  3.6 10.0 %collective-permute-start.2 = (f32[32,2176]{1,0:T(8,128)S(1)}, f32[32,2176]{1,0:T(8,128)S(1)}, u32[]{:S(2)}, u32[]{:S(2)}) collective-permute-start(f32[32,2176]{1,0:T(8,128)S(1)} %get-tuple-element.26.refs_0_), channel_id=1, source_target_pairs={{0,2},{2,0},{4,6},{6,4},{1,3},{3,1},{5,7},{7,5},{8,10},{10,8},{12,... | collective-permute-start | bytes 835592 | tf_op jit(solution)/shard_map/ppermute | solution.py:346
  6.6 7.0 %collective-permute-start.3 = (f32[32,2176]{1,0:T(8,128)S(1)}, f32[32,2176]{1,0:T(8,128)S(1)}, u32[]{:S(2)}, u32[]{:S(2)}) collective-permute-start(f32[32,2176]{1,0:T(8,128)S(1)} %get-tuple-element.27), channel_id=1, source_target_pairs={{2,4},{4,2},{3,5},{5,3},{10,12},{12,10},{11,13},{13,11},{18,20},{2... | collective-permute-start | bytes 835592 | tf_op jit(solution)/shard_map/ppermute | solution.py:345
  7.3 1.3 %collective-permute-start.1 = (f32[128,128]{1,0:T(8,128)S(1)}, f32[128,128]{1,0:T(8,128)S(1)}, u32[]{:S(2)}, u32[]{:S(2)}) collective-permute-start(f32[128,128]{1,0:T(8,128)S(1)} %mass_edges.1), channel_id=1, source_target_pairs={{0,1},{1,0},{2,3},{3,2},{4,5},{5,4},{6,7},{7,6},{8,9},{9,8},{10,11... | collective-permute-start | bytes 196616 | tf_op jit(solution)/shard_map/ppermute | solution.py:330
  9.6 10.7 %copy-start.1 = (f32[1,128,2048]{2,1,0:T(8,128)S(1)}, f32[1,128,2048]{2,1,0:T(8,128)}, u32[]{:S(2)}) copy-start(f32[1,128,2048]{2,1,0:T(8,128)} %param.4) | copy-start | bytes 3145732
  9.6 10.7 %copy-start.3 = (f32[2]{0:T(128)S(1)}, f32[2]{0:T(128)}, u32[]{:S(2)}) copy-start(f32[2]{0:T(128)} %weights.3) | copy-start | bytes 28
  14.8 10.6 %collective-permute-start.4 = (f32[32,2048]{1,0:T(8,128)S(1)}, f32[32,2048]{1,0:T(8,128)S(1)}, u32[]{:S(2)}, u32[]{:S(2)}) collective-permute-start(f32[32,2048]{1,0:T(8,128)S(1)} %get-tuple-element.28), channel_id=1, source_target_pairs={{0,2},{2,0},{4,6},{6,4},{1,3},{3,1},{5,7},{7,5},{8,10},{10,8},{12,... | collective-permute-start | bytes 786440 | tf_op jit(solution)/shard_map/ppermute | solution.py:346
  19.6 5.8 %collective-permute-start.5 = (f32[32,2048]{1,0:T(8,128)S(1)}, f32[32,2048]{1,0:T(8,128)S(1)}, u32[]{:S(2)}, u32[]{:S(2)}) collective-permute-start(f32[32,2048]{1,0:T(8,128)S(1)} %get-tuple-element.29), channel_id=1, source_target_pairs={{2,4},{4,2},{3,5},{5,3},{10,12},{12,10},{11,13},{13,11},{18,20},{2... | collective-permute-start | bytes 786440 | tf_op jit(solution)/shard_map/ppermute | solution.py:345
  21.3 8.0 %collective-permute-start.6 = (f32[64,1024]{1,0:T(8,128)S(1)}, f32[64,1024]{1,0:T(8,128)S(1)}, u32[]{:S(2)}, u32[]{:S(2)}) collective-permute-start(f32[64,1024]{1,0:T(8,128)S(1)} %bitcast.15), channel_id=1, source_target_pairs={{0,8},{8,0},{1,9},{9,1},{2,10},{10,2},{3,11},{11,3},{4,12},{12,4},... | collective-permute-start | bytes 786440 | tf_op jit(solution)/shard_map/ppermute | solution.py:353
  26.5 9.3 %collective-permute-start.7 = (f32[64,1024]{1,0:T(8,128)S(1)}, f32[64,1024]{1,0:T(8,128)S(1)}, u32[]{:S(2)}, u32[]{:S(2)}) collective-permute-start(f32[64,1024]{1,0:T(8,128)S(1)} %bitcast.16), channel_id=1, source_target_pairs={{0,8},{8,0},{1,9},{9,1},{2,10},{10,2},{3,11},{11,3},{4,12},{12,4},... | collective-permute-start | bytes 786440 | tf_op jit(solution)/shard_map/ppermute | solution.py:353
  29.4 21.1 %collective-permute-start.12 = (f32[128,1024]{1,0:T(8,128)S(1)}, f32[128,1024]{1,0:T(8,128)S(1)}, u32[]{:S(2)}, u32[]{:S(2)}) collective-permute-start(f32[128,1024]{1,0:T(8,128)S(1)} %bitcast.14), channel_id=1, source_target_pairs={{0,8},{8,0},{1,9},{9,1},{2,10},{10,2},{3,11},{11,3},{4,12},{12,4},... | collective-permute-start | bytes 1572872 | tf_op jit(solution)/shard_map/ppermute | solution.py:353
  35.9 1.2 %collective-permute-start.8 = (f32[8,128]{1,0:T(8,128)S(1)}, f32[8,128]{1,0:T(8,128)S(1)}, u32[]{:S(2)}, u32[]{:S(2)}) collective-permute-start(f32[8,128]{1,0:T(8,128)S(1)} %get-tuple-element.38), channel_id=1, source_target_pairs={{0,1},{1,0},{2,3},{3,2},{4,5},{5,4},{6,7},{7,6},{8,9},{9,8},{10,11... | collective-permute-start | bytes 12296 | tf_op jit(solution)/shard_map/ppermute | solution.py:366
  37.1 5.2 %collective-permute-start.9 = (f32[8,128]{1,0:T(8,128)S(1)}, f32[8,128]{1,0:T(8,128)S(1)}, u32[]{:S(2)}, u32[]{:S(2)}) collective-permute-start(f32[8,128]{1,0:T(8,128)S(1)} %add.12), channel_id=1, source_target_pairs={{0,2},{2,0},{4,6},{6,4},{1,3},{3,1},{5,7},{7,5},{8,10},{10,8},{12,... | collective-permute-start | bytes 12296 | tf_op jit(solution)/shard_map/ppermute | solution.py:366
  42.4 4.5 %collective-permute-start.10 = (f32[8,128]{1,0:T(8,128)S(1)}, f32[8,128]{1,0:T(8,128)S(1)}, u32[]{:S(2)}, u32[]{:S(2)}) collective-permute-start(f32[8,128]{1,0:T(8,128)S(1)} %add.13), channel_id=1, source_target_pairs={{0,4},{2,6},{4,0},{6,2},{1,5},{3,7},{5,1},{7,3},{8,12},{10,14},{12... | collective-permute-start | bytes 12296 | tf_op jit(solution)/shard_map/ppermute | solution.py:366
  46.9 3.6 %collective-permute-start.11 = (f32[8,128]{1,0:T(8,128)S(1)}, f32[8,128]{1,0:T(8,128)S(1)}, u32[]{:S(2)}, u32[]{:S(2)}) collective-permute-start(f32[8,128]{1,0:T(8,128)S(1)} %add.14), channel_id=1, source_target_pairs={{0,8},{8,0},{1,9},{9,1},{2,10},{10,2},{3,11},{11,3},{4,12},{12,4},... | collective-permute-start | bytes 12296 | tf_op jit(solution)/shard_map/ppermute | solution.py:366

commit v3 on v2

v3 whole, which is shorter than its diff:
```python
import functools

import jax
import jax.numpy as jnp
import numpy as np
from jax import lax
from jax.experimental import pallas as pl
from jax.experimental.pallas import tpu as pltpu
from jax.sharding import PartitionSpec as P

HALF = 32
LANES = 128
kernel_sigma = 16.0


def taps_total():
    taps = np.arange(-HALF, HALF + 1).astype(np.float64)
    return float(np.sum(np.exp(-taps * taps / (2.0 * kernel_sigma * kernel_sigma))))


def band_matrix(shape, axis_in):
    places = lax.broadcasted_iota(jnp.int32, shape, axis_in) - lax.broadcasted_iota(jnp.int32, shape, 1 - axis_in)
    offsets = (places - HALF).astype(jnp.float32)
    entries = jnp.exp(-offsets * offsets / (2.0 * kernel_sigma * kernel_sigma)) / taps_total()
    return jnp.where(jnp.abs(offsets) <= HALF, entries, 0.0)


def bands_kernel(columns, inner, rim):
    high, low = split(band_matrix((LANES + 2 * HALF, LANES), 0))
    columns[...] = jnp.concatenate([high, low], axis=1)
    for rows in (inner, rim):
        count = rows.shape[0] // 2
        high, low = split(band_matrix((count, count + 2 * HALF), 1))
        rows[...] = jnp.concatenate(
            [jnp.concatenate([high, high], axis=1), jnp.concatenate([low, jnp.zeros_like(low)], axis=1)], axis=0
        )


def split(values):
    high = values.astype(jnp.bfloat16)
    low = (values - high.astype(jnp.float32)).astype(jnp.bfloat16)
    return high, low


def dot(left, right):
    return jnp.dot(left, right, preferred_element_type=jnp.float32)


def column_block(window, band):
    high, low = split(window)
    depth = window.shape[1]
    both = dot(high, band[:depth])
    return both[:, :LANES] + both[:, LANES:] + dot(low, band[:depth, :LANES])


def row_block(window, band):
    high, low = split(window)
    rows = band.shape[0] // 2
    both = dot(band, jnp.concatenate([high, low], axis=0))
    return both[:rows] + both[rows:]


def edge_flags():
    place = lax.axis_index("cols")
    return (place > 0).astype(jnp.float32), (place < lax.axis_size("cols") - 1).astype(jnp.float32)


def row_parity():
    return lax.rem(lax.axis_index("rows"), 2)


def chunks(width, step):
    return [(start, min(start + step, width)) for start in range(0, width, step)]


def edge_sides():
    return [lax.axis_index("cols") == 0] if lax.axis_size("cols") == 2 else [True, False]


def edge_tiles(values, outs):
    width = values.shape[1]
    for out, right in zip(outs, edge_sides()):
        start = pl.multiple_of(jnp.where(right, width - LANES, 0), LANES)
        out[...] = values[:, pl.ds(start, LANES)]


def log_edge_kernel(logs, taps, kept, *outs):
    edge_tiles(logs, outs)
    for out in outs:
        out[...] = jnp.exp(out[...])
    kept[...] = logs[...]


def half_sends(which, across, first, second):
    height, share = across.shape[0], first.shape[1] - LANES
    odd = row_parity()
    lanes = pl.ds(pl.multiple_of(half_place(which) * share, LANES), share + LANES)
    first[...] = across[pl.ds(pl.multiple_of((1 - odd) * (height - HALF), HALF), HALF), lanes]
    second[...] = across[pl.ds(pl.multiple_of(odd * (height - HALF), HALF), HALF), lanes]


def mass_edge_kernel(masses, across, after, first, second, *outs):
    half_sends("own", across, first, second)
    edge_tiles(masses, outs)


def spread_kernel(logs, taps, across, wide):
    width = logs.shape[1]
    edge = 2 * HALF
    wide[:, edge : edge + width] = jnp.exp(logs[...])
    for start in range(LANES, width, LANES):
        across[:, start : start + LANES] = column_block(wide[:, start : start + LANES + 2 * HALF], taps[...])


def spread_edge_kernel(partial, logs, from_left, from_right, taps, across, first, second):
    has_left, has_right = edge_flags()
    height, width = logs.shape
    edge = 2 * HALF
    across[...] = partial[...]
    left = jnp.concatenate([from_left[:, edge:] * has_left, jnp.exp(logs[:, :LANES])], axis=1)
    right = jnp.concatenate([jnp.exp(logs[:, width - edge :]), from_right[:, :edge] * has_right], axis=1)
    across[:, :LANES] = column_block(left, taps[...])
    across[:, width : width + LANES] = column_block(right, taps[...])
    half_sends("other", across, first, second)


def ratio_of(masses, smooth):
    return jnp.where(masses > 0.0, masses / smooth, 0.0)


def column_pass(ratios, taps, out):
    for start in range(0, out.shape[1], LANES):
        out[:, start : start + LANES] = column_block(ratios[:, start : start + LANES + 2 * HALF], taps[...])


def own_weight(weights):
    mine = lax.broadcasted_iota(jnp.int32, weights.shape, 1) == lax.axis_index("hist")
    own = jnp.sum(jnp.where(mine, weights[...], 0.0), axis=1, keepdims=True)
    return own / jnp.sum(weights[...], axis=1, keepdims=True)


def inner_ratio_kernel(
    across, masses, from_left, from_right, weights, taps, row_taps, out, wide, weight, smooth, ratios
):
    weight[...] = jnp.broadcast_to(own_weight(weights), weight.shape)
    has_left, has_right = edge_flags()
    height = masses.shape[0]
    wide[...] = jnp.concatenate(
        [
            from_left[:, LANES - HALF :] * has_left,
            masses[...],
            from_right[:, :HALF] * has_right,
            jnp.zeros((height, 2 * HALF), jnp.float32),
        ],
        axis=1,
    )
    for start, stop in chunks(across.shape[1], 256):
        smooth[:, start:stop] = row_block(across[:, start:stop], row_taps[...])
    ratios[...] = ratio_of(wide[HALF : height - HALF, :], smooth[...])
    column_pass(ratios, taps, out)


def half_place(which):
    place = lax.axis_index("hist") if lax.axis_size("hist") == 2 else 0
    return 1 - place if which == "other" else place


def rim_ratio_kernel(
    which, across, first, second, wide, taps, row_taps, after, rims, sent_first, sent_second, smooth, ratios
):
    height = across.shape[0]
    share = rims.shape[1]
    odd = row_parity()
    offset = half_place(which) * share
    for start, stop in chunks(share + LANES, 256):
        lanes = pl.ds(pl.multiple_of(offset + start, LANES), stop - start)
        one, two = first[:, start:stop], second[:, start:stop]
        upper = jnp.concatenate([jnp.where(odd == 1, one, two), across[: 2 * HALF, lanes]], axis=0)
        lower = jnp.concatenate([across[height - 2 * HALF :, lanes], jnp.where(odd == 1, two, one)], axis=0)
        smooth[:HALF, start:stop] = row_block(upper, row_taps[...])
        smooth[HALF:, start:stop] = row_block(lower, row_taps[...])
    lanes = pl.ds(pl.multiple_of(offset, LANES), share + LANES)
    masses = jnp.concatenate([wide[:HALF, lanes], wide[height - HALF :, lanes]], axis=0)
    ratios[...] = ratio_of(masses, smooth[...])
    column_pass(ratios, taps, rims)
    sent_first[...] = rims[pl.ds(pl.multiple_of((1 - odd) * HALF, HALF), HALF), :]
    sent_second[...] = rims[pl.ds(pl.multiple_of(odd * HALF, HALF), HALF), :]


def inner_log_kernel(which, weight, rims, inner, logs, row_taps, smooth, own):
    height = logs.shape[0]
    share = rims.shape[1]
    offset = half_place(which) * share
    for start, stop in chunks(share, 256):
        lanes = pl.ds(pl.multiple_of(offset + start, LANES), stop - start)
        window = jnp.concatenate([rims[:HALF, start:stop], inner[:, lanes], rims[HALF:, start:stop]], axis=0)
        smooth[:, start:stop] = jnp.log(row_block(window, row_taps[...]))
    lanes = pl.ds(pl.multiple_of(offset, LANES), share)
    own[...] = weight[:1, :1] * (logs[HALF : height - HALF, lanes] + smooth[...])


def rim_log_kernel(which, weight, from_first, from_second, rims, inner, logs, row_taps, after, smooth, own):
    height = logs.shape[0]
    depth = inner.shape[0]
    share = rims.shape[1]
    odd = row_parity()
    offset = half_place(which) * share
    for start, stop in chunks(share, 256):
        lanes = pl.ds(pl.multiple_of(offset + start, LANES), stop - start)
        one, two = from_first[:, start:stop], from_second[:, start:stop]
        above, below = jnp.where(odd == 1, one, two), jnp.where(odd == 1, two, one)
        upper = jnp.concatenate([above, rims[:HALF, start:stop], inner[:HALF, lanes]], axis=0)
        lower = jnp.concatenate([inner[depth - HALF :, lanes], rims[HALF:, start:stop], below], axis=0)
        smooth[:HALF, start:stop] = jnp.log(row_block(upper, row_taps[...]))
        smooth[HALF:, start:stop] = jnp.log(row_block(lower, row_taps[...]))
    lanes = pl.ds(pl.multiple_of(offset, LANES), share)
    log_rows = jnp.concatenate([logs[:HALF, lanes], logs[height - HALF :, lanes]], axis=0)
    own[...] = weight[:1, :1] * (log_rows + smooth[...])


def folded(values):
    rows, width = values.shape
    total = jnp.sum(values.reshape(rows // 8, 8, width), axis=0)
    return sum(total[:, start : start + LANES] for start in range(0, width, LANES))


def mean_part(own, smooth, arrived, mean, change):
    log_mean = own[...] + arrived[...]
    values = jnp.exp(log_mean)
    mean[...] = values
    change[...] = log_mean - smooth[...]
    return folded(values)


def inner_mean_kernel(own, smooth, arrived, mean, change, partial):
    partial[...] = mean_part(own, smooth, arrived, mean, change)


def rim_mean_kernel(own, smooth, arrived, inner_own, before, mean, change, partial, later):
    partial[...] = before[...] + mean_part(own, smooth, arrived, mean, change)
    height = later.shape[0]
    later[:HALF, :] = own[:HALF, :]
    later[HALF : height - HALF, :] = inner_own[...]
    later[height - HALF :, :] = own[HALF:, :]


def later_mean_kernel(rim_own, rim_smooth, inner_own, inner_smooth, arrived, mean, change):
    height = mean.shape[0]
    for rows, own, smooth, part in (
        (slice(0, HALF), rim_own, rim_smooth, slice(0, HALF)),
        (slice(HALF, height - HALF), inner_own, inner_smooth, slice(None)),
        (slice(height - HALF, height), rim_own, rim_smooth, slice(HALF, 2 * HALF)),
    ):
        log_mean = own[part, :] + arrived[rows, :]
        mean[rows, :] = jnp.exp(log_mean)
        change[rows, :] = log_mean - smooth[part, :]


def final_kernel(
    cells, total, rim_mean, rim_change, inner_mean, inner_change, later_mean, later_change, barycenter, new_logs,
    stage, sems,
):
    height, width = barycenter.shape
    share = width // 2
    scale = cells / jnp.sum(total[...], axis=(0, 1), keepdims=True)
    log_scale = jnp.log(scale)
    copies = []
    for k, (out, rim, inner, later, apply) in enumerate(
        (
            (barycenter, rim_mean, inner_mean, later_mean, lambda x: x * scale),
            (new_logs, rim_change, inner_change, later_change, lambda x: x + log_scale),
        )
    ):
        for step, which in enumerate(("own", "other")):
            slot = slice(step * share, (step + 1) * share)
            if which == "own":
                stage[k, :HALF, slot] = apply(rim[:HALF, :])
                stage[k, HALF : height - HALF, slot] = apply(inner[...])
                stage[k, height - HALF :, slot] = apply(rim[HALF:, :])
            else:
                stage[k, :, slot] = apply(later[...])
            lanes = pl.ds(pl.multiple_of(half_place(which) * share, LANES), share)
            copy = pltpu.make_async_copy(stage.at[k, :, slot], out.at[:, lanes], sems.at[k, step])
            copy.start()
            copies.append(copy)
    for copy in copies:
        copy.wait()


def call(kernel, name, args, outs, scratch=(), cost=0, far_out=False, sems=None):
    shaped = lambda shape: shape if isinstance(shape, jax.ShapeDtypeStruct) else jax.ShapeDtypeStruct(shape, jnp.float32)
    near = pl.BlockSpec(memory_space=pltpu.VMEM)
    far = pl.BlockSpec(memory_space=pl.ANY)
    return pl.pallas_call(
        kernel,
        name=name,
        out_shape=tuple(shaped(shape) for shape in outs),
        in_specs=[near for _ in args],
        out_specs=tuple(far if far_out else near for _ in outs),
        scratch_shapes=[pltpu.VMEM(shape, jnp.float32) for shape in scratch]
        + ([pltpu.SemaphoreType.DMA(sems)] if sems else []),
        compiler_params=pltpu.CompilerParams(vmem_limit_bytes=32 * 1024 * 1024),
        cost_estimate=pl.CostEstimate(flops=5 * cost, bytes_accessed=cost // 256, transcendentals=0),
    )(*args)


def swap_columns(edges):
    count = lax.axis_size("cols")
    if count == 2:
        got = lax.ppermute(edges[0], "cols", [(0, 1), (1, 0)])
        return got, got
    steps = [(i, i + 1) for i in range(count - 1)]
    right_edge, left_edge = edges
    return (
        lax.ppermute(right_edge, "cols", steps),
        lax.ppermute(left_edge, "cols", [(b, a) for a, b in steps]),
    )


def swap_rows(first, second):
    count = lax.axis_size("rows")
    pairs = lambda start: [
        pair for i in range(start, count - 1, 2) for pair in ((i, i + 1), (i + 1, i))
    ]
    got_second = lax.ppermute(second, "rows", pairs(1))
    got_first = lax.ppermute(first, "rows", pairs(0))
    return got_first, got_second


def swap_hist(values):
    return lax.ppermute(values, "hist", [(0, 1), (1, 0)])


def total_over(values, axes):
    for axis in axes:
        count = lax.axis_size(axis)
        if count & (count - 1):
            values = lax.psum(values, axis)
            continue
        span = 1
        while span < count:
            values = values + lax.ppermute(values, axis, [(i, i ^ span) for i in range(count)])
            span *= 2
    return values


def body(hists, log_scaling_fields, histogram_weight_list):
    masses = hists[0]
    logs = log_scaling_fields[0]
    weights = histogram_weight_list
    height, width = masses.shape
    count = lax.axis_size("hist")
    edge = 2 * HALF
    inner = height - edge
    share = width // 2
    wide_width = width + LANES
    matmul = 2 * height * width * 3 * 256
    cells = height * lax.axis_size("rows") * width * lax.axis_size("cols")

    half = lambda *shape: jax.ShapeDtypeStruct(shape, jnp.bfloat16)
    taps, inner_taps, rim_taps = call(
        bands_kernel, "bands", (),
        [half(LANES + edge, 2 * LANES), half(2 * inner, 2 * height), half(edge, 2 * (HALF + edge))],
    )
    sides = 1 if lax.axis_size("cols") == 2 else 2
    tiles = [(height, LANES)] * sides
    logs, *edges = call(log_edge_kernel, "log_edges", (logs, taps), [(height, width)] + tiles)
    from_left, from_right = swap_columns(edges)
    (partial,) = call(
        spread_kernel, "spread", (logs, taps), [(height, wide_width)], [(height, wide_width)], cost=matmul
    )
    across, *other_sent = call(
        spread_edge_kernel, "spread_edge", (partial, logs, from_left, from_right, taps),
        [(height, wide_width)] + [(HALF, share + LANES)] * 2, cost=matmul // 8,
    )
    first, second, *edges = call(
        mass_edge_kernel, "mass_edges", (masses, across, other_sent[0]), [(HALF, share + LANES)] * 2 + tiles,
        cost=20 * matmul,
    )
    own_sent = (first, second)
    from_left, from_right = swap_columns(edges)
    other_arrived = swap_rows(*other_sent)
    own_arrived = swap_rows(*own_sent)
    inside, masses, weight = call(
        inner_ratio_kernel, "inner_ratio",
        (across, masses, from_left, from_right, weights.reshape(1, count), taps, inner_taps),
        [(inner, width), (height, wide_width), (8, LANES)], [(inner, wide_width), (inner, wide_width)],
    )

    def rim_ratio(which, arrived, after):
        return call(
            functools.partial(rim_ratio_kernel, which), which + "_rim_ratio",
            (across, *arrived, masses, taps, rim_taps, after),
            [(edge, share), (HALF, share), (HALF, share)], [(edge, share + LANES)] * 2, cost=matmul,
        )

    def inner_log(which, rims):
        return call(
            functools.partial(inner_log_kernel, which), which + "_inner_log",
            (weight, rims, inside, logs, inner_taps), [(inner, share)] * 2, cost=matmul,
        )

    def rim_log(which, rims, arrived, after):
        return call(
            functools.partial(rim_log_kernel, which), which + "_rim_log",
            (weight, *arrived, rims, inside, logs, rim_taps, after), [(edge, share)] * 2, cost=matmul,
        )

    other_rims, *sent = rim_ratio("other", other_arrived, inside)
    other_arrived = swap_rows(*sent)
    other_inner_smooth, other_inner_own = inner_log("other", other_rims)
    own_rims, *sent = rim_ratio("own", own_arrived, other_inner_own)
    own_arrived = swap_rows(*sent)
    other_rim_smooth, other_rim_own = rim_log("other", other_rims, other_arrived, own_rims)
    inner_smooth, inner_own = inner_log("own", own_rims)
    rim_smooth, rim_own = rim_log("own", own_rims, own_arrived, other_rim_own)

    if count != 2:
        joined = lambda rim, inside: jnp.concatenate([rim[:HALF], inside, rim[HALF:]], axis=0)
        both = lambda *parts: jnp.concatenate([joined(*parts[:2]), joined(*parts[2:])], axis=1)
        log_mean = lax.psum(both(rim_own, inner_own, other_rim_own, other_inner_own), "hist")
        log_smooth = both(rim_smooth, inner_smooth, other_rim_smooth, other_inner_smooth)
        mean = jnp.exp(log_mean)
        scale = cells / lax.psum(jnp.sum(mean), ("rows", "cols"))
        return (mean * scale, (log_mean + jnp.log(scale) - log_smooth)[None])

    inner_arrived = swap_hist(other_inner_own)
    rim_arrived = swap_hist(other_rim_own)
    inner_mean, inner_change, mass = call(
        inner_mean_kernel, "inner_mean", (inner_own, inner_smooth, inner_arrived),
        [(inner, share), (inner, share), (8, LANES)], cost=matmul // 4,
    )
    rim_mean, rim_change, mass, later = call(
        rim_mean_kernel, "rim_mean", (rim_own, rim_smooth, rim_arrived, inner_own, mass),
        [(edge, share), (edge, share), (8, LANES), (height, share)], cost=matmul // 4,
    )
    later_arrived = swap_hist(later)
    mass = total_over(mass, ("cols", "rows", "hist"))
    later_mean, later_change = call(
        later_mean_kernel, "later_mean",
        (other_rim_own, other_rim_smooth, other_inner_own, other_inner_smooth, later_arrived),
        [(height, share)] * 2, cost=matmul // 4,
    )
    barycenter, new_logs = call(
        functools.partial(final_kernel, float(cells)), "final",
        (mass, rim_mean, rim_change, inner_mean, inner_change, later_mean, later_change),
        [(height, width)] * 2, [(2, height, width)], far_out=True, sems=(2, 2), cost=matmul // 4,
    )
    return (barycenter, new_logs[None])


def solution(mesh):
    return jax.shard_map(
        body,
        mesh=mesh,
        in_specs=(
            P("hist", ("groups", "rows"), "cols"),
            P("hist", ("groups", "rows"), "cols"),
            P(),
        ),
        out_specs=(P(("groups", "rows"), "cols"), P("hist", ("groups", "rows"), "cols")),
        check_vma=False,
    )
```

time: 52.3 us -> 48.2 us (0.922)
  waiting for transfers between devices: 20.5 us -> 17.3 us
  Pallas kernels: 7.09 us -> 6.34 us
    ppermute x2 -> x4, waiting for transfers between devices: 6.56 us -> 3.58 us  [swap_rows(): got_first = lax.ppermute(first, 'rows', pairs(0))]
    ppermute x4, starting transfers between devices: 8.08 us -> 5.29 us  [total_over(): lax.ppermute(values, axis, [(i, i ^ span) for i in range(count)])]
    ppermute x2 -> x4, starting transfers between devices: 7.8 us -> 10 us  [swap_rows(): got_first = lax.ppermute(first, 'rows', pairs(0))]
    ppermute x4, waiting for transfers between devices: 6.48 us -> 8.42 us  [total_over(): lax.ppermute(values, axis, [(i, i ^ span) for i in range(count)])]
    ppermute x3, waiting for transfers between devices: 6.1 us -> 4.7 us  [swap_hist(): return lax.ppermute(values, 'hist', [(0, 1), (1, 0)])]
    ppermute x2 -> x4, starting transfers between devices: 1.33 us -> 2.64 us  [swap_rows(): got_second = lax.ppermute(second, 'rows', pairs(1))]
    ppermute x3, starting transfers between devices: 4.66 us -> 3.7 us  [swap_hist(): return lax.ppermute(values, 'hist', [(0, 1), (1, 0)])]
    ppermute x2, waiting for transfers between devices: 1.39 us -> 0.59 us  [swap_columns(): got = lax.ppermute(edges[0], 'cols', [(0, 1), (1, 0)])]
  transfers between devices with their start and end apart: 13 -> 17, of which waited for: 10 -> 9; matrix products, arithmetic and copies ran while one was open for 0% -> 0% of each run, Pallas kernels for 8% -> 9%
where the time goes in v3:
time: 48.2 us; the launch traced here: 47.9 us
  starting transfers between devices  22.2 us (46%)
  waiting for transfers between devices  17.3 us (36%)
  Pallas kernels  6.34 us (13%)
  local copies, waits for them, and re-layouts  1.23 us (3%)
  between operations  0.81 us (2%)
    ppermute x4, starting transfers between devices, swap_rows(): got_first = lax.ppermute(first, 'rows', pairs(0))  10 us
    ppermute x4, waiting for transfers between devices, total_over(): lax.ppermute(values, axis, [(i, i ^ span) for i in range(count)])  8.42 us
    pallas_call x16, Pallas kernels, call(): pl.pallas_call(kernel, name=name, out_shape=tuple((shaped(shape) for shap...  6.34 us
    ppermute x4, starting transfers between devices, total_over(): lax.ppermute(values, axis, [(i, i ^ span) for i in range(count)])  5.29 us
    ppermute x3, waiting for transfers between devices, swap_hist(): return lax.ppermute(values, 'hist', [(0, 1), (1, 0)])  4.7 us
    ppermute x3, starting transfers between devices, swap_hist(): return lax.ppermute(values, 'hist', [(0, 1), (1, 0)])  3.7 us
    ppermute x4, waiting for transfers between devices, swap_rows(): got_first = lax.ppermute(first, 'rows', pairs(0))  3.58 us
    ppermute x4, starting transfers between devices, swap_rows(): got_second = lax.ppermute(second, 'rows', pairs(1))  2.64 us
  transfers between devices with their start and end apart: 17, of which 9 were waited for; matrix products, arithmetic and copies ran while one was open for 0% of the time, Pallas kernels for 9%

profile of v3, /device:TPU:0, one launch (start us, length us, event | category | flops | bytes accessed | tf_op | source)
XLA Modules:
  0.0 47.9 jit_solution(6208188585191687067)
XLA Ops:
  0.6 0.1 bands.1
  0.7 0.0 copy-start
  0.7 1.2 %copy-done = f32[1,128,2048]{2,1,0:T(8,128)S(1)} copy-done((f32[1,128,2048]{2,1,0:T(8,128)S(1)}, f32[1,128,2048]{2,1,0:T(8,128)}, u32[]{:S(2)}) %copy-start) | copy-done | bytes 1048600
  2.0 0.1 log_edges.1
  2.0 0.5 %collective-permute-start = (f32[128,128]{1,0:T(8,128)S(1)}, f32[128,128]{1,0:T(8,128)S(1)}, u32[]{:S(2)}, u32[]{:S(2)}) collective-permute-start(f32[128,128]{1,0:T(8,128)S(1)} %get-tuple-element.43), channel_id=1, source_target_pairs={{0,1},{1,0},{2,3},{3,2},{4,5},{5,4},{6,7},{7,6},{8,9},{9,8},{10,11... | collective-permute-start | bytes 196616 | tf_op jit(solution)/shard_map/ppermute | solution.py:310
  2.5 0.8 %spread.1.partial = f32[128,2176]{1,0:T(8,128)S(1)} custom-call(f32[128,2048]{1,0:T(8,128)S(1)} %get-tuple-element.42.logs, bf16[192,256]{1,0:T(8,128)(2,1)S(1)} %get-tuple-element.41.taps), custom_call_target="tpu_custom_call" | custom-call | flops 2013265920 | bytes 1572864 | tf_op jit(solution)/shard_map/spread/pallas_call | solution.py:294
  3.3 0.0 copy-start.1
  3.3 0.1 collective-permute-done.from_left.from_right
  3.5 0.3 spread_edge.1
  3.8 0.7 %collective-permute-start.5 = (f32[32,1152]{1,0:T(8,128)S(1)}, f32[32,1152]{1,0:T(8,128)S(1)}, u32[]{:S(2)}, u32[]{:S(2)}) collective-permute-start(f32[32,1152]{1,0:T(8,128)S(1)} %get-tuple-element.53), channel_id=1, source_target_pairs={{2,4},{4,2},{3,5},{5,3},{10,12},{12,10},{11,13},{13,11},{18,20},{2... | collective-permute-start | bytes 442376 | tf_op jit(solution)/shard_map/ppermute | solution.py:325
  4.4 5.8 %collective-permute-start.4 = (f32[32,1152]{1,0:T(8,128)S(1)}, f32[32,1152]{1,0:T(8,128)S(1)}, u32[]{:S(2)}, u32[]{:S(2)}) collective-permute-start(f32[32,1152]{1,0:T(8,128)S(1)} %get-tuple-element.45.after), channel_id=1, source_target_pairs={{0,2},{2,0},{4,6},{6,4},{1,3},{3,1},{5,7},{7,5},{8,10},{10,8},{12,... | collective-permute-start | bytes 442376 | tf_op jit(solution)/shard_map/ppermute | solution.py:326
  10.3 0.1 collective-permute-start.1
  10.4 0.1 collective-permute-start.2
  10.5 0.7 %collective-permute-start.3 = (f32[32,1152]{1,0:T(8,128)S(1)}, f32[32,1152]{1,0:T(8,128)S(1)}, u32[]{:S(2)}, u32[]{:S(2)}) collective-permute-start(f32[32,1152]{1,0:T(8,128)S(1)} %get-tuple-element.50), channel_id=1, source_target_pairs={{2,4},{4,2},{3,5},{5,3},{10,12},{12,10},{11,13},{13,11},{18,20},{2... | collective-permute-start | bytes 442376 | tf_op jit(solution)/shard_map/ppermute | solution.py:325
  11.1 0.5 collective-permute-done.1.from_left.from_right
  11.6 0.9 %inner_ratio.1 = (f32[64,2048]{1,0:T(8,128)S(1)}, f32[128,2176]{1,0:T(8,128)S(1)}, f32[8,128]{1,0:T(8,128)S(1)}) custom-call(f32[128,2176]{1,0:T(8,128)S(1)} %get-tuple-element.44.across, f32[128,2048]{1,0:T(8,128)S(1)} %bitcast.6, f32[128,128]{1,0:T(8,128)S(1)} %collective-permute-done.1.from_left.from_right, ...), custom_call_target="tpu_custom_call" | custom-call | tf_op jit(solution)/shard_map/inner_ratio/pallas_call | solution.py:294
  12.6 2.2 %collective-permute-done.4.first = f32[32,1152]{1,0:T(8,128)S(1)} collective-permute-done((f32[32,1152]{1,0:T(8,128)S(1)}, f32[32,1152]{1,0:T(8,128)S(1)}, u32[]{:S(2)}, u32[]{:S(2)}) %collective-permute-start.4) | collective-permute-done | bytes 147488 | tf_op jit(solution)/shard_map/ppermute | solution.py:326
  14.7 0.6 %other_rim_ratio.1 = (f32[64,1024]{1,0:T(8,128)S(1)}, f32[32,1024]{1,0:T(8,128)S(1)}, f32[32,1024]{1,0:T(8,128)S(1)}) custom-call(f32[128,2176]{1,0:T(8,128)S(1)} %get-tuple-element.44.across, f32[32,1152]{1,0:T(8,128)S(1)} %collective-permute-done.4.first, f32[32,1152]{1,0:T(8,128)S(1)} %collective-permute-done.5.second, ...), custom_call_target="tpu_custom_call" | custom-call | flops 2013265920 | bytes 1572864 | tf_op jit(solution)/shard_map/other_rim_ratio/pallas_call | solution.py:294
  15.4 2.3 %collective-permute-start.8 = (f32[32,1024]{1,0:T(8,128)S(1)}, f32[32,1024]{1,0:T(8,128)S(1)}, u32[]{:S(2)}, u32[]{:S(2)}) collective-permute-start(f32[32,1024]{1,0:T(8,128)S(1)} %get-tuple-element.60), channel_id=1, source_target_pairs={{0,2},{2,0},{4,6},{6,4},{1,3},{3,1},{5,7},{7,5},{8,10},{10,8},{12,... | collective-permute-start | bytes 393224 | tf_op jit(solution)/shard_map/ppermute | solution.py:326
  17.7 0.7 %collective-permute-start.9 = (f32[32,1024]{1,0:T(8,128)S(1)}, f32[32,1024]{1,0:T(8,128)S(1)}, u32[]{:S(2)}, u32[]{:S(2)}) collective-permute-start(f32[32,1024]{1,0:T(8,128)S(1)} %get-tuple-element.61), channel_id=1, source_target_pairs={{2,4},{4,2},{3,5},{5,3},{10,12},{12,10},{11,13},{13,11},{18,20},{2... | collective-permute-start | bytes 393224 | tf_op jit(solution)/shard_map/ppermute | solution.py:325
  18.3 0.3 other_inner_log.1
  18.6 1.5 %collective-permute-start.11 = (f32[64,1024]{1,0:T(8,128)S(1)}, f32[64,1024]{1,0:T(8,128)S(1)}, u32[]{:S(2)}, u32[]{:S(2)}) collective-permute-start(f32[64,1024]{1,0:T(8,128)S(1)} %get-tuple-element.56.after.inner_own), channel_id=1, source_target_pairs={{0,8},{8,0},{1,9},{9,1},{2,10},{10,2},{3,11},{11,3},{4,12},{12,4},... | collective-permute-start | bytes 786440 | tf_op jit(solution)/shard_map/ppermute | solution.py:331
  20.2 0.0 collective-permute-done.2.first
  20.2 0.0 collective-permute-done.3.second
  20.2 0.6 %own_rim_ratio.1 = (f32[64,1024]{1,0:T(8,128)S(1)}, f32[32,1024]{1,0:T(8,128)S(1)}, f32[32,1024]{1,0:T(8,128)S(1)}) custom-call(f32[128,2176]{1,0:T(8,128)S(1)} %get-tuple-element.44.across, f32[32,1152]{1,0:T(8,128)S(1)} %collective-permute-done.2.first, f32[32,1152]{1,0:T(8,128)S(1)} %collective-permute-done.3.second, ...), custom_call_target="tpu_custom_call" | custom-call | flops 2013265920 | bytes 1572864 | tf_op jit(solution)/shard_map/own_rim_ratio/pallas_call | solution.py:294
  20.8 1.8 %collective-permute-start.6 = (f32[32,1024]{1,0:T(8,128)S(1)}, f32[32,1024]{1,0:T(8,128)S(1)}, u32[]{:S(2)}, u32[]{:S(2)}) collective-permute-start(f32[32,1024]{1,0:T(8,128)S(1)} %get-tuple-element.57), channel_id=1, source_target_pairs={{0,2},{2,0},{4,6},{6,4},{1,3},{3,1},{5,7},{7,5},{8,10},{10,8},{12,... | collective-permute-start | bytes 393224 | tf_op jit(solution)/shard_map/ppermute | solution.py:326
  22.6 0.7 %collective-permute-start.7 = (f32[32,1024]{1,0:T(8,128)S(1)}, f32[32,1024]{1,0:T(8,128)S(1)}, u32[]{:S(2)}, u32[]{:S(2)}) collective-permute-start(f32[32,1024]{1,0:T(8,128)S(1)} %get-tuple-element.58), channel_id=1, source_target_pairs={{2,4},{4,2},{3,5},{5,3},{10,12},{12,10},{11,13},{13,11},{18,20},{2... | collective-permute-start | bytes 393224 | tf_op jit(solution)/shard_map/ppermute | solution.py:325
  23.2 0.0 collective-permute-done.8.from_first
  23.2 0.0 collective-permute-done.9.from_second
  23.3 0.3 other_rim_log.1
  23.6 0.6 %collective-permute-start.10 = (f32[64,1024]{1,0:T(8,128)S(1)}, f32[64,1024]{1,0:T(8,128)S(1)}, u32[]{:S(2)}, u32[]{:S(2)}) collective-permute-start(f32[64,1024]{1,0:T(8,128)S(1)} %get-tuple-element.62.after.rim_own), channel_id=1, source_target_pairs={{0,8},{8,0},{1,9},{9,1},{2,10},{10,2},{3,11},{11,3},{4,12},{12,4},... | collective-permute-start | bytes 786440 | tf_op jit(solution)/shard_map/ppermute | solution.py:331
  24.2 0.3 own_inner_log.1
  24.4 1.4 %collective-permute-done.6.from_first = f32[32,1024]{1,0:T(8,128)S(1)} collective-permute-done((f32[32,1024]{1,0:T(8,128)S(1)}, f32[32,1024]{1,0:T(8,128)S(1)}, u32[]{:S(2)}, u32[]{:S(2)}) %collective-permute-start.6) | collective-permute-done | bytes 131104 | tf_op jit(solution)/shard_map/ppermute | solution.py:326
  25.8 0.0 collective-permute-done.7.from_second
  25.8 0.3 own_rim_log.1
  26.1 0.1 inner_mean.1
  26.2 4.7 %collective-permute-done.10.arrived = f32[64,1024]{1,0:T(8,128)S(1)} collective-permute-done((f32[64,1024]{1,0:T(8,128)S(1)}, f32[64,1024]{1,0:T(8,128)S(1)}, u32[]{:S(2)}, u32[]{:S(2)}) %collective-permute-start.10) | collective-permute-done | bytes 262176 | tf_op jit(solution)/shard_map/ppermute | solution.py:331
  30.9 0.1 rim_mean.1
  31.0 1.6 %collective-permute-start.16 = (f32[128,1024]{1,0:T(8,128)S(1)}, f32[128,1024]{1,0:T(8,128)S(1)}, u32[]{:S(2)}, u32[]{:S(2)}) collective-permute-start(f32[128,1024]{1,0:T(8,128)S(1)} %get-tuple-element.75), channel_id=1, source_target_pairs={{0,8},{8,0},{1,9},{9,1},{2,10},{10,2},{3,11},{11,3},{4,12},{12,4},... | collective-permute-start | bytes 1572872 | tf_op jit(solution)/shard_map/ppermute | solution.py:331
  32.6 1.2 %collective-permute-done.12 = f32[8,128]{1,0:T(8,128)S(1)} collective-permute-done((f32[8,128]{1,0:T(8,128)S(1)}, f32[8,128]{1,0:T(8,128)S(1)}, u32[]{:S(2)}, u32[]{:S(2)}) %collective-permute-start.12) | collective-permute-done | bytes 4128 | tf_op jit(solution)/shard_map/ppermute | solution.py:342
  33.7 2.8 %collective-permute-start.13 = (f32[8,128]{1,0:T(8,128)S(1)}, f32[8,128]{1,0:T(8,128)S(1)}, u32[]{:S(2)}, u32[]{:S(2)}) collective-permute-start(f32[8,128]{1,0:T(8,128)S(1)} %add.12), channel_id=1, source_target_pairs={{0,2},{2,0},{4,6},{6,4},{1,3},{3,1},{5,7},{7,5},{8,10},{10,8},{12,... | collective-permute-start | bytes 12296 | tf_op jit(solution)/shard_map/ppermute | solution.py:342
  36.6 1.6 %collective-permute-done.13 = f32[8,128]{1,0:T(8,128)S(1)} collective-permute-done((f32[8,128]{1,0:T(8,128)S(1)}, f32[8,128]{1,0:T(8,128)S(1)}, u32[]{:S(2)}, u32[]{:S(2)}) %collective-permute-start.13) | collective-permute-done | bytes 4128 | tf_op jit(solution)/shard_map/ppermute | solution.py:342
  38.2 1.9 %collective-permute-start.14 = (f32[8,128]{1,0:T(8,128)S(1)}, f32[8,128]{1,0:T(8,128)S(1)}, u32[]{:S(2)}, u32[]{:S(2)}) collective-permute-start(f32[8,128]{1,0:T(8,128)S(1)} %add.13), channel_id=1, source_target_pairs={{0,4},{2,6},{4,0},{6,2},{1,5},{3,7},{5,1},{7,3},{8,12},{10,14},{12... | collective-permute-start | bytes 12296 | tf_op jit(solution)/shard_map/ppermute | solution.py:342
  40.1 2.6 %collective-permute-done.14 = f32[8,128]{1,0:T(8,128)S(1)} collective-permute-done((f32[8,128]{1,0:T(8,128)S(1)}, f32[8,128]{1,0:T(8,128)S(1)}, u32[]{:S(2)}, u32[]{:S(2)}) %collective-permute-start.14) | collective-permute-done | bytes 4128 | tf_op jit(solution)/shard_map/ppermute | solution.py:342
  42.7 0.5 %collective-permute-start.15 = (f32[8,128]{1,0:T(8,128)S(1)}, f32[8,128]{1,0:T(8,128)S(1)}, u32[]{:S(2)}, u32[]{:S(2)}) collective-permute-start(f32[8,128]{1,0:T(8,128)S(1)} %add.14), channel_id=1, source_target_pairs={{0,8},{8,0},{1,9},{9,1},{2,10},{10,2},{3,11},{11,3},{4,12},{12,4},... | collective-permute-start | bytes 12296 | tf_op jit(solution)/shard_map/ppermute | solution.py:342
  43.2 3.1 %collective-permute-done.15 = f32[8,128]{1,0:T(8,128)S(1)} collective-permute-done((f32[8,128]{1,0:T(8,128)S(1)}, f32[8,128]{1,0:T(8,128)S(1)}, u32[]{:S(2)}, u32[]{:S(2)}) %collective-permute-start.15) | collective-permute-done | bytes 4128 | tf_op jit(solution)/shard_map/ppermute | solution.py:342
  46.3 0.1 later_mean.1
  46.4 1.5 %final.1 = (f32[128,2048]{1,0:T(8,128)}, f32[128,2048]{1,0:T(8,128)}) custom-call(f32[8,128]{1,0:T(8,128)S(1)} %add.15.total, f32[64,1024]{1,0:T(8,128)S(1)} %get-tuple-element.69.rim_mean, f32[64,1024]{1,0:T(8,128)S(1)} %get-tuple-element.70.rim_change, f32[64,1024]{1,0:T(8,128)S(1)} %get-tuple-element.71.inner_mean, ...), custom_call_target="tpu_custom_call" | custom-call | flops 503316480 | bytes 393216 | tf_op jit(solution)/shard_map/final/pallas_call | solution.py:294
  (12 shorter events, 0.1 us)
Async XLA Ops:
  0.7 1.2 %copy-start = (f32[1,128,2048]{2,1,0:T(8,128)S(1)}, f32[1,128,2048]{2,1,0:T(8,128)}, u32[]{:S(2)}) copy-start(f32[1,128,2048]{2,1,0:T(8,128)} %param.4) | copy-start | bytes 3145732
  2.0 1.4 %collective-permute-start = (f32[128,128]{1,0:T(8,128)S(1)}, f32[128,128]{1,0:T(8,128)S(1)}, u32[]{:S(2)}, u32[]{:S(2)}) collective-permute-start(f32[128,128]{1,0:T(8,128)S(1)} %get-tuple-element.43), channel_id=1, source_target_pairs={{0,1},{1,0},{2,3},{3,2},{4,5},{5,4},{6,7},{7,6},{8,9},{9,8},{10,11... | collective-permute-start | bytes 196616 | tf_op jit(solution)/shard_map/ppermute | solution.py:310
  3.3 6.9 %copy-start.1 = (f32[1,128,2048]{2,1,0:T(8,128)S(1)}, f32[1,128,2048]{2,1,0:T(8,128)}, u32[]{:S(2)}) copy-start(f32[1,128,2048]{2,1,0:T(8,128)} %param.3) | copy-start | bytes 3145732
  3.8 8.8 %collective-permute-start.5 = (f32[32,1152]{1,0:T(8,128)S(1)}, f32[32,1152]{1,0:T(8,128)S(1)}, u32[]{:S(2)}, u32[]{:S(2)}) collective-permute-start(f32[32,1152]{1,0:T(8,128)S(1)} %get-tuple-element.53), channel_id=1, source_target_pairs={{2,4},{4,2},{3,5},{5,3},{10,12},{12,10},{11,13},{13,11},{18,20},{2... | collective-permute-start | bytes 442376 | tf_op jit(solution)/shard_map/ppermute | solution.py:325
  4.4 10.3 %collective-permute-start.4 = (f32[32,1152]{1,0:T(8,128)S(1)}, f32[32,1152]{1,0:T(8,128)S(1)}, u32[]{:S(2)}, u32[]{:S(2)}) collective-permute-start(f32[32,1152]{1,0:T(8,128)S(1)} %get-tuple-element.45.after), channel_id=1, source_target_pairs={{0,2},{2,0},{4,6},{6,4},{1,3},{3,1},{5,7},{7,5},{8,10},{10,8},{12,... | collective-permute-start | bytes 442376 | tf_op jit(solution)/shard_map/ppermute | solution.py:326
  10.3 1.4 %copy-start.2 = (f32[2]{0:T(128)S(1)}, f32[2]{0:T(128)}, u32[]{:S(2)}) copy-start(f32[2]{0:T(128)} %param.5) | copy-start | bytes 28
  10.3 1.3 %collective-permute-start.1 = (f32[128,128]{1,0:T(8,128)S(1)}, f32[128,128]{1,0:T(8,128)S(1)}, u32[]{:S(2)}, u32[]{:S(2)}) collective-permute-start(f32[128,128]{1,0:T(8,128)S(1)} %get-tuple-element.46), channel_id=1, source_target_pairs={{0,1},{1,0},{2,3},{3,2},{4,5},{5,4},{6,7},{7,6},{8,9},{9,8},{10,11... | collective-permute-start | bytes 196616 | tf_op jit(solution)/shard_map/ppermute | solution.py:310
  10.4 9.8 %collective-permute-start.2 = (f32[32,1152]{1,0:T(8,128)S(1)}, f32[32,1152]{1,0:T(8,128)S(1)}, u32[]{:S(2)}, u32[]{:S(2)}) collective-permute-start(f32[32,1152]{1,0:T(8,128)S(1)} %get-tuple-element.49), channel_id=1, source_target_pairs={{0,2},{2,0},{4,6},{6,4},{1,3},{3,1},{5,7},{7,5},{8,10},{10,8},{12,... | collective-permute-start | bytes 442376 | tf_op jit(solution)/shard_map/ppermute | solution.py:326
  10.5 9.7 %collective-permute-start.3 = (f32[32,1152]{1,0:T(8,128)S(1)}, f32[32,1152]{1,0:T(8,128)S(1)}, u32[]{:S(2)}, u32[]{:S(2)}) collective-permute-start(f32[32,1152]{1,0:T(8,128)S(1)} %get-tuple-element.50), channel_id=1, source_target_pairs={{2,4},{4,2},{3,5},{5,3},{10,12},{12,10},{11,13},{13,11},{18,20},{2... | collective-permute-start | bytes 442376 | tf_op jit(solution)/shard_map/ppermute | solution.py:325
  15.4 7.9 %collective-permute-start.8 = (f32[32,1024]{1,0:T(8,128)S(1)}, f32[32,1024]{1,0:T(8,128)S(1)}, u32[]{:S(2)}, u32[]{:S(2)}) collective-permute-start(f32[32,1024]{1,0:T(8,128)S(1)} %get-tuple-element.60), channel_id=1, source_target_pairs={{0,2},{2,0},{4,6},{6,4},{1,3},{3,1},{5,7},{7,5},{8,10},{10,8},{12,... | collective-permute-start | bytes 393224 | tf_op jit(solution)/shard_map/ppermute | solution.py:326
  17.7 5.6 %collective-permute-start.9 = (f32[32,1024]{1,0:T(8,128)S(1)}, f32[32,1024]{1,0:T(8,128)S(1)}, u32[]{:S(2)}, u32[]{:S(2)}) collective-permute-start(f32[32,1024]{1,0:T(8,128)S(1)} %get-tuple-element.61), channel_id=1, source_target_pairs={{2,4},{4,2},{3,5},{5,3},{10,12},{12,10},{11,13},{13,11},{18,20},{2... | collective-permute-start | bytes 393224 | tf_op jit(solution)/shard_map/ppermute | solution.py:325
  18.6 7.5 %collective-permute-start.11 = (f32[64,1024]{1,0:T(8,128)S(1)}, f32[64,1024]{1,0:T(8,128)S(1)}, u32[]{:S(2)}, u32[]{:S(2)}) collective-permute-start(f32[64,1024]{1,0:T(8,128)S(1)} %get-tuple-element.56.after.inner_own), channel_id=1, source_target_pairs={{0,8},{8,0},{1,9},{9,1},{2,10},{10,2},{3,11},{11,3},{4,12},{12,4},... | collective-permute-start | bytes 786440 | tf_op jit(solution)/shard_map/ppermute | solution.py:331
  20.8 5.0 %collective-permute-start.6 = (f32[32,1024]{1,0:T(8,128)S(1)}, f32[32,1024]{1,0:T(8,128)S(1)}, u32[]{:S(2)}, u32[]{:S(2)}) collective-permute-start(f32[32,1024]{1,0:T(8,128)S(1)} %get-tuple-element.57), channel_id=1, source_target_pairs={{0,2},{2,0},{4,6},{6,4},{1,3},{3,1},{5,7},{7,5},{8,10},{10,8},{12,... | collective-permute-start | bytes 393224 | tf_op jit(solution)/shard_map/ppermute | solution.py:326
  22.6 3.3 %collective-permute-start.7 = (f32[32,1024]{1,0:T(8,128)S(1)}, f32[32,1024]{1,0:T(8,128)S(1)}, u32[]{:S(2)}, u32[]{:S(2)}) collective-permute-start(f32[32,1024]{1,0:T(8,128)S(1)} %get-tuple-element.58), channel_id=1, source_target_pairs={{2,4},{4,2},{3,5},{5,3},{10,12},{12,10},{11,13},{13,11},{18,20},{2... | collective-permute-start | bytes 393224 | tf_op jit(solution)/shard_map/ppermute | solution.py:325
  23.6 7.3 %collective-permute-start.10 = (f32[64,1024]{1,0:T(8,128)S(1)}, f32[64,1024]{1,0:T(8,128)S(1)}, u32[]{:S(2)}, u32[]{:S(2)}) collective-permute-start(f32[64,1024]{1,0:T(8,128)S(1)} %get-tuple-element.62.after.rim_own), channel_id=1, source_target_pairs={{0,8},{8,0},{1,9},{9,1},{2,10},{10,2},{3,11},{11,3},{4,12},{12,4},... | collective-permute-start | bytes 786440 | tf_op jit(solution)/shard_map/ppermute | solution.py:331
  31.0 15.3 %collective-permute-start.16 = (f32[128,1024]{1,0:T(8,128)S(1)}, f32[128,1024]{1,0:T(8,128)S(1)}, u32[]{:S(2)}, u32[]{:S(2)}) collective-permute-start(f32[128,1024]{1,0:T(8,128)S(1)} %get-tuple-element.75), channel_id=1, source_target_pairs={{0,8},{8,0},{1,9},{9,1},{2,10},{10,2},{3,11},{11,3},{4,12},{12,4},... | collective-permute-start | bytes 1572872 | tf_op jit(solution)/shard_map/ppermute | solution.py:331
  32.6 1.2 %collective-permute-start.12 = (f32[8,128]{1,0:T(8,128)S(1)}, f32[8,128]{1,0:T(8,128)S(1)}, u32[]{:S(2)}, u32[]{:S(2)}) collective-permute-start(f32[8,128]{1,0:T(8,128)S(1)} %get-tuple-element.68), channel_id=1, source_target_pairs={{0,1},{1,0},{2,3},{3,2},{4,5},{5,4},{6,7},{7,6},{8,9},{9,8},{10,11... | collective-permute-start | bytes 12296 | tf_op jit(solution)/shard_map/ppermute | solution.py:342
  33.7 4.4 %collective-permute-start.13 = (f32[8,128]{1,0:T(8,128)S(1)}, f32[8,128]{1,0:T(8,128)S(1)}, u32[]{:S(2)}, u32[]{:S(2)}) collective-permute-start(f32[8,128]{1,0:T(8,128)S(1)} %add.12), channel_id=1, source_target_pairs={{0,2},{2,0},{4,6},{6,4},{1,3},{3,1},{5,7},{7,5},{8,10},{10,8},{12,... | collective-permute-start | bytes 12296 | tf_op jit(solution)/shard_map/ppermute | solution.py:342
  38.2 4.5 %collective-permute-start.14 = (f32[8,128]{1,0:T(8,128)S(1)}, f32[8,128]{1,0:T(8,128)S(1)}, u32[]{:S(2)}, u32[]{:S(2)}) collective-permute-start(f32[8,128]{1,0:T(8,128)S(1)} %add.13), channel_id=1, source_target_pairs={{0,4},{2,6},{4,0},{6,2},{1,5},{3,7},{5,1},{7,3},{8,12},{10,14},{12... | collective-permute-start | bytes 12296 | tf_op jit(solution)/shard_map/ppermute | solution.py:342
  42.7 3.6 %collective-permute-start.15 = (f32[8,128]{1,0:T(8,128)S(1)}, f32[8,128]{1,0:T(8,128)S(1)}, u32[]{:S(2)}, u32[]{:S(2)}) collective-permute-start(f32[8,128]{1,0:T(8,128)S(1)} %add.14), channel_id=1, source_target_pairs={{0,8},{8,0},{1,9},{9,1},{2,10},{10,2},{3,11},{11,3},{4,12},{12,4},... | collective-permute-start | bytes 12296 | tf_op jit(solution)/shard_map/ppermute | solution.py:342

commit v4 on v3

--- a/solution.py
+++ b/solution.py
@@ -65,8 +65,8 @@
     return (place > 0).astype(jnp.float32), (place < lax.axis_size("cols") - 1).astype(jnp.float32)
 
 
-def row_parity():
-    return lax.rem(lax.axis_index("rows"), 2)
+def row_parity(flip):
+    return lax.rem(lax.axis_index("rows") + flip, 2)
 
 
 def chunks(width, step):
@@ -91,16 +91,16 @@
     kept[...] = logs[...]
 
 
-def half_sends(which, across, first, second):
+def half_sends(which, flip, across, first, second):
     height, share = across.shape[0], first.shape[1] - LANES
-    odd = row_parity()
+    odd = row_parity(flip)
     lanes = pl.ds(pl.multiple_of(half_place(which) * share, LANES), share + LANES)
     first[...] = across[pl.ds(pl.multiple_of((1 - odd) * (height - HALF), HALF), HALF), lanes]
     second[...] = across[pl.ds(pl.multiple_of(odd * (height - HALF), HALF), HALF), lanes]
 
 
 def mass_edge_kernel(masses, across, after, first, second, *outs):
-    half_sends("own", across, first, second)
+    half_sends("own", 1, across, first, second)
     edge_tiles(masses, outs)
 
 
@@ -121,7 +121,7 @@
     right = jnp.concatenate([jnp.exp(logs[:, width - edge :]), from_right[:, :edge] * has_right], axis=1)
     across[:, :LANES] = column_block(left, taps[...])
     across[:, width : width + LANES] = column_block(right, taps[...])
-    half_sends("other", across, first, second)
+    half_sends("other", 0, across, first, second)
 
 
 def ratio_of(masses, smooth):
@@ -166,11 +166,11 @@
 
 
 def rim_ratio_kernel(
-    which, across, first, second, wide, taps, row_taps, after, rims, sent_first, sent_second, smooth, ratios
+    which, came, goes, across, first, second, wide, taps, row_taps, after, rims, sent_first, sent_second, smooth, ratios
 ):
     height = across.shape[0]
     share = rims.shape[1]
-    odd = row_parity()
+    odd = row_parity(came)
     offset = half_place(which) * share
     for start, stop in chunks(share + LANES, 256):
         lanes = pl.ds(pl.multiple_of(offset + start, LANES), stop - start)
@@ -183,6 +183,7 @@
     masses = jnp.concatenate([wide[:HALF, lanes], wide[height - HALF :, lanes]], axis=0)
     ratios[...] = ratio_of(masses, smooth[...])
     column_pass(ratios, taps, rims)
+    odd = row_parity(goes)
     sent_first[...] = rims[pl.ds(pl.multiple_of((1 - odd) * HALF, HALF), HALF), :]
     sent_second[...] = rims[pl.ds(pl.multiple_of(odd * HALF, HALF), HALF), :]
 
@@ -199,11 +200,11 @@
     own[...] = weight[:1, :1] * (logs[HALF : height - HALF, lanes] + smooth[...])
 
 
-def rim_log_kernel(which, weight, from_first, from_second, rims, inner, logs, row_taps, after, smooth, own):
+def rim_log_kernel(which, came, weight, from_first, from_second, rims, inner, logs, row_taps, after, smooth, own):
     height = logs.shape[0]
     depth = inner.shape[0]
     share = rims.shape[1]
-    odd = row_parity()
+    odd = row_parity(came)
     offset = half_place(which) * share
     for start, stop in chunks(share, 256):
         lanes = pl.ds(pl.multiple_of(offset + start, LANES), stop - start)
@@ -317,14 +318,12 @@
     )
 
 
-def swap_rows(first, second):
+def swap_rows(flip, first, second):
     count = lax.axis_size("rows")
     pairs = lambda start: [
         pair for i in range(start, count - 1, 2) for pair in ((i, i + 1), (i + 1, i))
     ]
-    got_second = lax.ppermute(second, "rows", pairs(1))
-    got_first = lax.ppermute(first, "rows", pairs(0))
-    return got_first, got_second
+    return lax.ppermute(first, "rows", pairs(flip)), lax.ppermute(second, "rows", pairs(1 - flip))
 
 
 def swap_hist(values):
@@ -332,16 +331,11 @@
 
 
 def total_over(values, axes):
-    for axis in axes:
-        count = lax.axis_size(axis)
-        if count & (count - 1):
-            values = lax.psum(values, axis)
-            continue
-        span = 1
-        while span < count:
-            values = values + lax.ppermute(values, axis, [(i, i ^ span) for i in range(count)])
-            span *= 2
-    return values
+    count = lax.axis_size(axes)
+    if count & (count - 1):
+        return lax.psum(values, axes)
+    arrived = [lax.ppermute(values, axes, [(i, i ^ mask) for i in range(count)]) for mask in range(1, count)]
+    return values + sum(arrived)
 
 
 def body(hists, log_scaling_fields, histogram_weight_list):
@@ -362,6 +356,7 @@
         bands_kernel, "bands", (),
         [half(LANES + edge, 2 * LANES), half(2 * inner, 2 * height), half(edge, 2 * (HALF + edge))],
     )
+    flips = {"other": (0, 0), "own": (1, 0)}
     sides = 1 if lax.axis_size("cols") == 2 else 2
     tiles = [(height, LANES)] * sides
     logs, *edges = call(log_edge_kernel, "log_edges", (logs, taps), [(height, width)] + tiles)
@@ -379,8 +374,8 @@
     )
     own_sent = (first, second)
     from_left, from_right = swap_columns(edges)
-    other_arrived = swap_rows(*other_sent)
-    own_arrived = swap_rows(*own_sent)
+    other_arrived = swap_rows(0, *other_sent)
+    own_arrived = swap_rows(1, *own_sent)
     inside, masses, weight = call(
         inner_ratio_kernel, "inner_ratio",
         (across, masses, from_left, from_right, weights.reshape(1, count), taps, inner_taps),
@@ -389,7 +384,7 @@
 
     def rim_ratio(which, arrived, after):
         return call(
-            functools.partial(rim_ratio_kernel, which), which + "_rim_ratio",
+            functools.partial(rim_ratio_kernel, which, *flips[which]), which + "_rim_ratio",
             (across, *arrived, masses, taps, rim_taps, after),
             [(edge, share), (HALF, share), (HALF, share)], [(edge, share + LANES)] * 2, cost=matmul,
         )
@@ -402,15 +397,15 @@
 
     def rim_log(which, rims, arrived, after):
         return call(
-            functools.partial(rim_log_kernel, which), which + "_rim_log",
+            functools.partial(rim_log_kernel, which, flips[which][1]), which + "_rim_log",
             (weight, *arrived, rims, inside, logs, rim_taps, after), [(edge, share)] * 2, cost=matmul,
         )
 
     other_rims, *sent = rim_ratio("other", other_arrived, inside)
-    other_arrived = swap_rows(*sent)
+    other_arrived = swap_rows(0, *sent)
     other_inner_smooth, other_inner_own = inner_log("other", other_rims)
     own_rims, *sent = rim_ratio("own", own_arrived, other_inner_own)
-    own_arrived = swap_rows(*sent)
+    own_arrived = swap_rows(0, *sent)
     other_rim_smooth, other_rim_own = rim_log("other", other_rims, other_arrived, own_rims)
     inner_smooth, inner_own = inner_log("own", own_rims)
     rim_smooth, rim_own = rim_log("own", own_rims, own_arrived, other_rim_own)
@@ -435,7 +430,8 @@
         [(edge, share), (edge, share), (8, LANES), (height, share)], cost=matmul // 4,
     )
     later_arrived = swap_hist(later)
-    mass = total_over(mass, ("cols", "rows", "hist"))
+    mass = total_over(mass, ("rows",))
+    mass = total_over(mass, ("hist", "cols"))
     later_mean, later_change = call(
         later_mean_kernel, "later_mean",
         (other_rim_own, other_rim_smooth, other_inner_own, other_inner_smooth, later_arrived),

time: 48.2 us -> 45.8 us (0.950)
  waiting for transfers between devices: 17.3 us -> 11.7 us
  starting transfers between devices: 22.2 us -> 25.5 us
    ppermute x12 -> x14, waiting for transfers between devices: 12 us -> 6.86 us  [the longest x6 5.42 us: total_over(): lax.ppermute(values, axes, [(i, i ^ mask) for i in range(count)])]
    ppermute x12 -> x14, starting transfers between devices: 17.9 us -> 21.7 us  [the longest x4 11.1 us: swap_rows(): lax.ppermute(first, 'rows', pairs(flip))]
  transfers between devices with their start and end apart: 17 -> 19, of which waited for: 9 -> 9; matrix products, arithmetic and copies ran while one was open for 0% -> 0% of each run, Pallas kernels for 9% -> 9%
where the time goes in v4:
time: 45.8 us; the launch traced here: 45.6 us
  starting transfers between devices  25.5 us (56%)
  waiting for transfers between devices  11.7 us (26%)
  Pallas kernels  6.34 us (14%)
  local copies, waits for them, and re-layouts  1.23 us (3%)
  between operations  0.82 us (2%)
    ppermute x4, starting transfers between devices, swap_rows(): lax.ppermute(first, 'rows', pairs(flip))  11.1 us
    ppermute x6, starting transfers between devices, total_over(): lax.ppermute(values, axes, [(i, i ^ mask) for i in range(count)])  6.74 us
    pallas_call x16, Pallas kernels, call(): pl.pallas_call(kernel, name=name, out_shape=tuple((shaped(shape) for shap...  6.34 us
    ppermute x6, waiting for transfers between devices, total_over(): lax.ppermute(values, axes, [(i, i ^ mask) for i in range(count)])  5.42 us
    ppermute x3, waiting for transfers between devices, swap_hist(): return lax.ppermute(values, 'hist', [(0, 1), (1, 0)])  4.73 us
    ppermute x4, starting transfers between devices, swap_rows(): lax.ppermute(second, 'rows', pairs(1 - flip))  3.79 us
    ppermute x3, starting transfers between devices, swap_hist(): return lax.ppermute(values, 'hist', [(0, 1), (1, 0)])  3.23 us
    ppermute x4, waiting for transfers between devices, swap_rows(): lax.ppermute(first, 'rows', pairs(flip))  1.43 us
  transfers between devices with their start and end apart: 19, of which 9 were waited for; matrix products, arithmetic and copies ran while one was open for 0% of the time, Pallas kernels for 9%

profile of v4, /device:TPU:0, one launch (start us, length us, event | category | flops | bytes accessed | tf_op | source)
XLA Modules:
  0.0 45.6 jit_solution(15422052731596926994)
XLA Ops:
  0.6 0.1 bands.1
  0.7 0.0 copy-start
  0.7 1.2 %copy-done = f32[1,128,2048]{2,1,0:T(8,128)S(1)} copy-done((f32[1,128,2048]{2,1,0:T(8,128)S(1)}, f32[1,128,2048]{2,1,0:T(8,128)}, u32[]{:S(2)}) %copy-start) | copy-done | bytes 1048600
  2.0 0.1 log_edges.1
  2.0 0.5 %collective-permute-start = (f32[128,128]{1,0:T(8,128)S(1)}, f32[128,128]{1,0:T(8,128)S(1)}, u32[]{:S(2)}, u32[]{:S(2)}) collective-permute-start(f32[128,128]{1,0:T(8,128)S(1)} %get-tuple-element.43), channel_id=1, source_target_pairs={{0,1},{1,0},{2,3},{3,2},{4,5},{5,4},{6,7},{7,6},{8,9},{9,8},{10,11... | collective-permute-start | bytes 196616 | tf_op jit(solution)/shard_map/ppermute | solution.py:311
  2.5 0.8 %spread.1.partial = f32[128,2176]{1,0:T(8,128)S(1)} custom-call(f32[128,2048]{1,0:T(8,128)S(1)} %get-tuple-element.42.logs, bf16[192,256]{1,0:T(8,128)(2,1)S(1)} %get-tuple-element.41.taps), custom_call_target="tpu_custom_call" | custom-call | flops 2013265920 | bytes 1572864 | tf_op jit(solution)/shard_map/spread/pallas_call | solution.py:295
  3.3 0.0 copy-start.1
  3.3 0.1 collective-permute-done.from_left.from_right
  3.5 0.3 spread_edge.1
  3.8 0.7 %collective-permute-start.5 = (f32[32,1152]{1,0:T(8,128)S(1)}, f32[32,1152]{1,0:T(8,128)S(1)}, u32[]{:S(2)}, u32[]{:S(2)}) collective-permute-start(f32[32,1152]{1,0:T(8,128)S(1)} %get-tuple-element.53), channel_id=1, source_target_pairs={{2,4},{4,2},{3,5},{5,3},{10,12},{12,10},{11,13},{13,11},{18,20},{2... | collective-permute-start | bytes 442376 | tf_op jit(solution)/shard_map/ppermute | solution.py:326
  4.4 5.8 %collective-permute-start.4 = (f32[32,1152]{1,0:T(8,128)S(1)}, f32[32,1152]{1,0:T(8,128)S(1)}, u32[]{:S(2)}, u32[]{:S(2)}) collective-permute-start(f32[32,1152]{1,0:T(8,128)S(1)} %get-tuple-element.45.after), channel_id=1, source_target_pairs={{0,2},{2,0},{4,6},{6,4},{1,3},{3,1},{5,7},{7,5},{8,10},{10,8},{12,... | collective-permute-start | bytes 442376 | tf_op jit(solution)/shard_map/ppermute | solution.py:326
  10.3 0.1 collective-permute-start.1
  10.4 0.7 %collective-permute-start.2 = (f32[32,1152]{1,0:T(8,128)S(1)}, f32[32,1152]{1,0:T(8,128)S(1)}, u32[]{:S(2)}, u32[]{:S(2)}) collective-permute-start(f32[32,1152]{1,0:T(8,128)S(1)} %get-tuple-element.49), channel_id=1, source_target_pairs={{2,4},{4,2},{3,5},{5,3},{10,12},{12,10},{11,13},{13,11},{18,20},{2... | collective-permute-start | bytes 442376 | tf_op jit(solution)/shard_map/ppermute | solution.py:326
  11.0 1.8 %collective-permute-start.3 = (f32[32,1152]{1,0:T(8,128)S(1)}, f32[32,1152]{1,0:T(8,128)S(1)}, u32[]{:S(2)}, u32[]{:S(2)}) collective-permute-start(f32[32,1152]{1,0:T(8,128)S(1)} %get-tuple-element.50), channel_id=1, source_target_pairs={{0,2},{2,0},{4,6},{6,4},{1,3},{3,1},{5,7},{7,5},{8,10},{10,8},{12,... | collective-permute-start | bytes 442376 | tf_op jit(solution)/shard_map/ppermute | solution.py:326
  12.9 0.9 %inner_ratio.1 = (f32[64,2048]{1,0:T(8,128)S(1)}, f32[128,2176]{1,0:T(8,128)S(1)}, f32[8,128]{1,0:T(8,128)S(1)}) custom-call(f32[128,2176]{1,0:T(8,128)S(1)} %get-tuple-element.44.across, f32[128,2048]{1,0:T(8,128)S(1)} %bitcast.6, f32[128,128]{1,0:T(8,128)S(1)} %collective-permute-done.1.from_left.from_right, ...), custom_call_target="tpu_custom_call" | custom-call | tf_op jit(solution)/shard_map/inner_ratio/pallas_call | solution.py:295
  13.8 0.0 collective-permute-done.5.second
  13.8 0.3 collective-permute-done.4.first
  14.1 0.6 %other_rim_ratio.1 = (f32[64,1024]{1,0:T(8,128)S(1)}, f32[32,1024]{1,0:T(8,128)S(1)}, f32[32,1024]{1,0:T(8,128)S(1)}) custom-call(f32[128,2176]{1,0:T(8,128)S(1)} %get-tuple-element.44.across, f32[32,1152]{1,0:T(8,128)S(1)} %collective-permute-done.4.first, f32[32,1152]{1,0:T(8,128)S(1)} %collective-permute-done.5.second, ...), custom_call_target="tpu_custom_call" | custom-call | flops 2013265920 | bytes 1572864 | tf_op jit(solution)/shard_map/other_rim_ratio/pallas_call | solution.py:295
  14.8 2.0 %collective-permute-start.8 = (f32[32,1024]{1,0:T(8,128)S(1)}, f32[32,1024]{1,0:T(8,128)S(1)}, u32[]{:S(2)}, u32[]{:S(2)}) collective-permute-start(f32[32,1024]{1,0:T(8,128)S(1)} %get-tuple-element.60), channel_id=1, source_target_pairs={{0,2},{2,0},{4,6},{6,4},{1,3},{3,1},{5,7},{7,5},{8,10},{10,8},{12,... | collective-permute-start | bytes 393224 | tf_op jit(solution)/shard_map/ppermute | solution.py:326
  16.7 0.7 %collective-permute-start.9 = (f32[32,1024]{1,0:T(8,128)S(1)}, f32[32,1024]{1,0:T(8,128)S(1)}, u32[]{:S(2)}, u32[]{:S(2)}) collective-permute-start(f32[32,1024]{1,0:T(8,128)S(1)} %get-tuple-element.61), channel_id=1, source_target_pairs={{2,4},{4,2},{3,5},{5,3},{10,12},{12,10},{11,13},{13,11},{18,20},{2... | collective-permute-start | bytes 393224 | tf_op jit(solution)/shard_map/ppermute | solution.py:326
  17.4 0.3 other_inner_log.1
  17.7 1.6 %collective-permute-start.11 = (f32[64,1024]{1,0:T(8,128)S(1)}, f32[64,1024]{1,0:T(8,128)S(1)}, u32[]{:S(2)}, u32[]{:S(2)}) collective-permute-start(f32[64,1024]{1,0:T(8,128)S(1)} %get-tuple-element.56.after.inner_own), channel_id=1, source_target_pairs={{0,8},{8,0},{1,9},{9,1},{2,10},{10,2},{3,11},{11,3},{4,12},{12,4},... | collective-permute-start | bytes 786440 | tf_op jit(solution)/shard_map/ppermute | solution.py:330
  19.2 0.6 %own_rim_ratio.1 = (f32[64,1024]{1,0:T(8,128)S(1)}, f32[32,1024]{1,0:T(8,128)S(1)}, f32[32,1024]{1,0:T(8,128)S(1)}) custom-call(f32[128,2176]{1,0:T(8,128)S(1)} %get-tuple-element.44.across, f32[32,1152]{1,0:T(8,128)S(1)} %collective-permute-done.2.first, f32[32,1152]{1,0:T(8,128)S(1)} %collective-permute-done.3.second, ...), custom_call_target="tpu_custom_call" | custom-call | flops 2013265920 | bytes 1572864 | tf_op jit(solution)/shard_map/own_rim_ratio/pallas_call | solution.py:295
  19.9 2.7 %collective-permute-start.6 = (f32[32,1024]{1,0:T(8,128)S(1)}, f32[32,1024]{1,0:T(8,128)S(1)}, u32[]{:S(2)}, u32[]{:S(2)}) collective-permute-start(f32[32,1024]{1,0:T(8,128)S(1)} %get-tuple-element.57), channel_id=1, source_target_pairs={{0,2},{2,0},{4,6},{6,4},{1,3},{3,1},{5,7},{7,5},{8,10},{10,8},{12,... | collective-permute-start | bytes 393224 | tf_op jit(solution)/shard_map/ppermute | solution.py:326
  22.5 0.7 %collective-permute-start.7 = (f32[32,1024]{1,0:T(8,128)S(1)}, f32[32,1024]{1,0:T(8,128)S(1)}, u32[]{:S(2)}, u32[]{:S(2)}) collective-permute-start(f32[32,1024]{1,0:T(8,128)S(1)} %get-tuple-element.58), channel_id=1, source_target_pairs={{2,4},{4,2},{3,5},{5,3},{10,12},{12,10},{11,13},{13,11},{18,20},{2... | collective-permute-start | bytes 393224 | tf_op jit(solution)/shard_map/ppermute | solution.py:326
  23.2 0.0 collective-permute-done.8.from_first
  23.2 0.0 collective-permute-done.9.from_second
  23.2 0.3 other_rim_log.1
  23.5 0.6 %collective-permute-start.10 = (f32[64,1024]{1,0:T(8,128)S(1)}, f32[64,1024]{1,0:T(8,128)S(1)}, u32[]{:S(2)}, u32[]{:S(2)}) collective-permute-start(f32[64,1024]{1,0:T(8,128)S(1)} %get-tuple-element.62.after.rim_own), channel_id=1, source_target_pairs={{0,8},{8,0},{1,9},{9,1},{2,10},{10,2},{3,11},{11,3},{4,12},{12,4},... | collective-permute-start | bytes 786440 | tf_op jit(solution)/shard_map/ppermute | solution.py:330
  24.1 0.3 own_inner_log.1
  24.4 1.1 %collective-permute-done.6.from_first = f32[32,1024]{1,0:T(8,128)S(1)} collective-permute-done((f32[32,1024]{1,0:T(8,128)S(1)}, f32[32,1024]{1,0:T(8,128)S(1)}, u32[]{:S(2)}, u32[]{:S(2)}) %collective-permute-start.6) | collective-permute-done | bytes 131104 | tf_op jit(solution)/shard_map/ppermute | solution.py:326
  25.5 0.3 own_rim_log.1
  25.8 0.1 inner_mean.1
  25.9 4.7 %collective-permute-done.10.arrived = f32[64,1024]{1,0:T(8,128)S(1)} collective-permute-done((f32[64,1024]{1,0:T(8,128)S(1)}, f32[64,1024]{1,0:T(8,128)S(1)}, u32[]{:S(2)}, u32[]{:S(2)}) %collective-permute-start.10) | collective-permute-done | bytes 262176 | tf_op jit(solution)/shard_map/ppermute | solution.py:330
  30.6 0.1 rim_mean.1
  30.7 1.1 %collective-permute-start.18 = (f32[128,1024]{1,0:T(8,128)S(1)}, f32[128,1024]{1,0:T(8,128)S(1)}, u32[]{:S(2)}, u32[]{:S(2)}) collective-permute-start(f32[128,1024]{1,0:T(8,128)S(1)} %get-tuple-element.75), channel_id=1, source_target_pairs={{0,8},{8,0},{1,9},{9,1},{2,10},{10,2},{3,11},{11,3},{4,12},{12,4},... | collective-permute-start | bytes 1572872 | tf_op jit(solution)/shard_map/ppermute | solution.py:330
  31.8 1.6 %collective-permute-start.14 = (f32[8,128]{1,0:T(8,128)S(1)}, f32[8,128]{1,0:T(8,128)S(1)}, u32[]{:S(2)}, u32[]{:S(2)}) collective-permute-start(f32[8,128]{1,0:T(8,128)S(1)} %get-tuple-element.68), channel_id=1, source_target_pairs={{0,6},{2,4},{4,2},{6,0},{1,7},{3,5},{5,3},{7,1},{8,14},{10,12},{12... | collective-permute-start | bytes 12296 | tf_op jit(solution)/shard_map/ppermute | solution.py:337
  33.4 3.2 %collective-permute-start.13 = (f32[8,128]{1,0:T(8,128)S(1)}, f32[8,128]{1,0:T(8,128)S(1)}, u32[]{:S(2)}, u32[]{:S(2)}) collective-permute-start(f32[8,128]{1,0:T(8,128)S(1)} %get-tuple-element.68), channel_id=1, source_target_pairs={{0,4},{2,6},{4,0},{6,2},{1,5},{3,7},{5,1},{7,3},{8,12},{10,14},{12... | collective-permute-start | bytes 12296 | tf_op jit(solution)/shard_map/ppermute | solution.py:337
  36.7 0.5 %collective-permute-done.14 = f32[8,128]{1,0:T(8,128)S(1)} collective-permute-done((f32[8,128]{1,0:T(8,128)S(1)}, f32[8,128]{1,0:T(8,128)S(1)}, u32[]{:S(2)}, u32[]{:S(2)}) %collective-permute-start.14) | collective-permute-done | bytes 4128 | tf_op jit(solution)/shard_map/ppermute | solution.py:337
  37.2 1.1 %collective-permute-done.13 = f32[8,128]{1,0:T(8,128)S(1)} collective-permute-done((f32[8,128]{1,0:T(8,128)S(1)}, f32[8,128]{1,0:T(8,128)S(1)}, u32[]{:S(2)}, u32[]{:S(2)}) %collective-permute-start.13) | collective-permute-done | bytes 4128 | tf_op jit(solution)/shard_map/ppermute | solution.py:337
  38.3 2.0 %collective-permute-done.12 = f32[8,128]{1,0:T(8,128)S(1)} collective-permute-done((f32[8,128]{1,0:T(8,128)S(1)}, f32[8,128]{1,0:T(8,128)S(1)}, u32[]{:S(2)}, u32[]{:S(2)}) %collective-permute-start.12) | collective-permute-done | bytes 4128 | tf_op jit(solution)/shard_map/ppermute | solution.py:337
  40.3 0.6 %collective-permute-start.16 = (f32[8,128]{1,0:T(8,128)S(1)}, f32[8,128]{1,0:T(8,128)S(1)}, u32[]{:S(2)}, u32[]{:S(2)}) collective-permute-start(f32[8,128]{1,0:T(8,128)S(1)} %add_add_fusion.1), channel_id=1, source_target_pairs={{0,8},{1,9},{8,0},{9,1},{2,10},{3,11},{10,2},{11,3},{4,12},{5,13},... | collective-permute-start | bytes 12296 | tf_op jit(solution)/shard_map/ppermute | solution.py:337
  40.9 1.3 %collective-permute-start.15 = (f32[8,128]{1,0:T(8,128)S(1)}, f32[8,128]{1,0:T(8,128)S(1)}, u32[]{:S(2)}, u32[]{:S(2)}) collective-permute-start(f32[8,128]{1,0:T(8,128)S(1)} %add_add_fusion.1), channel_id=1, source_target_pairs={{0,1},{1,0},{8,9},{9,8},{2,3},{3,2},{10,11},{11,10},{4,5},{5,4},{1... | collective-permute-start | bytes 12296 | tf_op jit(solution)/shard_map/ppermute | solution.py:337
  42.1 1.2 %collective-permute-done.17 = f32[8,128]{1,0:T(8,128)S(1)} collective-permute-done((f32[8,128]{1,0:T(8,128)S(1)}, f32[8,128]{1,0:T(8,128)S(1)}, u32[]{:S(2)}, u32[]{:S(2)}) %collective-permute-start.17) | collective-permute-done | bytes 4128 | tf_op jit(solution)/shard_map/ppermute | solution.py:337
  43.3 0.6 %collective-permute-done.16 = f32[8,128]{1,0:T(8,128)S(1)} collective-permute-done((f32[8,128]{1,0:T(8,128)S(1)}, f32[8,128]{1,0:T(8,128)S(1)}, u32[]{:S(2)}, u32[]{:S(2)}) %collective-permute-start.16) | collective-permute-done | bytes 4128 | tf_op jit(solution)/shard_map/ppermute | solution.py:337
  44.0 0.0 collective-permute-done.15
  44.0 0.1 later_mean.1
  44.1 1.5 %final.1 = (f32[128,2048]{1,0:T(8,128)}, f32[128,2048]{1,0:T(8,128)}) custom-call(f32[8,128]{1,0:T(8,128)S(1)} %add_add_fusion.total, f32[64,1024]{1,0:T(8,128)S(1)} %get-tuple-element.69.rim_mean, f32[64,1024]{1,0:T(8,128)S(1)} %get-tuple-element.70.rim_change, f32[64,1024]{1,0:T(8,128)S(1)} %get-tuple-element.71.inner_mean, ...), custom_call_target="tpu_custom_call" | custom-call | flops 503316480 | bytes 393216 | tf_op jit(solution)/shard_map/final/pallas_call | solution.py:295
  (14 shorter events, 0.1 us)
Async XLA Ops:
  0.7 1.2 %copy-start = (f32[1,128,2048]{2,1,0:T(8,128)S(1)}, f32[1,128,2048]{2,1,0:T(8,128)}, u32[]{:S(2)}) copy-start(f32[1,128,2048]{2,1,0:T(8,128)} %param.4) | copy-start | bytes 3145732
  2.0 1.4 %collective-permute-start = (f32[128,128]{1,0:T(8,128)S(1)}, f32[128,128]{1,0:T(8,128)S(1)}, u32[]{:S(2)}, u32[]{:S(2)}) collective-permute-start(f32[128,128]{1,0:T(8,128)S(1)} %get-tuple-element.43), channel_id=1, source_target_pairs={{0,1},{1,0},{2,3},{3,2},{4,5},{5,4},{6,7},{7,6},{8,9},{9,8},{10,11... | collective-permute-start | bytes 196616 | tf_op jit(solution)/shard_map/ppermute | solution.py:311
  3.3 6.9 %copy-start.1 = (f32[1,128,2048]{2,1,0:T(8,128)S(1)}, f32[1,128,2048]{2,1,0:T(8,128)}, u32[]{:S(2)}) copy-start(f32[1,128,2048]{2,1,0:T(8,128)} %param.3) | copy-start | bytes 3145732
  3.8 10.0 %collective-permute-start.5 = (f32[32,1152]{1,0:T(8,128)S(1)}, f32[32,1152]{1,0:T(8,128)S(1)}, u32[]{:S(2)}, u32[]{:S(2)}) collective-permute-start(f32[32,1152]{1,0:T(8,128)S(1)} %get-tuple-element.53), channel_id=1, source_target_pairs={{2,4},{4,2},{3,5},{5,3},{10,12},{12,10},{11,13},{13,11},{18,20},{2... | collective-permute-start | bytes 442376 | tf_op jit(solution)/shard_map/ppermute | solution.py:326
  4.4 9.7 %collective-permute-start.4 = (f32[32,1152]{1,0:T(8,128)S(1)}, f32[32,1152]{1,0:T(8,128)S(1)}, u32[]{:S(2)}, u32[]{:S(2)}) collective-permute-start(f32[32,1152]{1,0:T(8,128)S(1)} %get-tuple-element.45.after), channel_id=1, source_target_pairs={{0,2},{2,0},{4,6},{6,4},{1,3},{3,1},{5,7},{7,5},{8,10},{10,8},{12,... | collective-permute-start | bytes 442376 | tf_op jit(solution)/shard_map/ppermute | solution.py:326
  10.3 2.6 %copy-start.2 = (f32[2]{0:T(128)S(1)}, f32[2]{0:T(128)}, u32[]{:S(2)}) copy-start(f32[2]{0:T(128)} %param.5) | copy-start | bytes 28
  10.3 2.6 %collective-permute-start.1 = (f32[128,128]{1,0:T(8,128)S(1)}, f32[128,128]{1,0:T(8,128)S(1)}, u32[]{:S(2)}, u32[]{:S(2)}) collective-permute-start(f32[128,128]{1,0:T(8,128)S(1)} %get-tuple-element.46), channel_id=1, source_target_pairs={{0,1},{1,0},{2,3},{3,2},{4,5},{5,4},{6,7},{7,6},{8,9},{9,8},{10,11... | collective-permute-start | bytes 196616 | tf_op jit(solution)/shard_map/ppermute | solution.py:311
  10.4 8.9 %collective-permute-start.2 = (f32[32,1152]{1,0:T(8,128)S(1)}, f32[32,1152]{1,0:T(8,128)S(1)}, u32[]{:S(2)}, u32[]{:S(2)}) collective-permute-start(f32[32,1152]{1,0:T(8,128)S(1)} %get-tuple-element.49), channel_id=1, source_target_pairs={{2,4},{4,2},{3,5},{5,3},{10,12},{12,10},{11,13},{13,11},{18,20},{2... | collective-permute-start | bytes 442376 | tf_op jit(solution)/shard_map/ppermute | solution.py:326
  11.0 8.2 %collective-permute-start.3 = (f32[32,1152]{1,0:T(8,128)S(1)}, f32[32,1152]{1,0:T(8,128)S(1)}, u32[]{:S(2)}, u32[]{:S(2)}) collective-permute-start(f32[32,1152]{1,0:T(8,128)S(1)} %get-tuple-element.50), channel_id=1, source_target_pairs={{0,2},{2,0},{4,6},{6,4},{1,3},{3,1},{5,7},{7,5},{8,10},{10,8},{12,... | collective-permute-start | bytes 442376 | tf_op jit(solution)/shard_map/ppermute | solution.py:326
  14.8 8.4 %collective-permute-start.8 = (f32[32,1024]{1,0:T(8,128)S(1)}, f32[32,1024]{1,0:T(8,128)S(1)}, u32[]{:S(2)}, u32[]{:S(2)}) collective-permute-start(f32[32,1024]{1,0:T(8,128)S(1)} %get-tuple-element.60), channel_id=1, source_target_pairs={{0,2},{2,0},{4,6},{6,4},{1,3},{3,1},{5,7},{7,5},{8,10},{10,8},{12,... | collective-permute-start | bytes 393224 | tf_op jit(solution)/shard_map/ppermute | solution.py:326
  16.7 6.5 %collective-permute-start.9 = (f32[32,1024]{1,0:T(8,128)S(1)}, f32[32,1024]{1,0:T(8,128)S(1)}, u32[]{:S(2)}, u32[]{:S(2)}) collective-permute-start(f32[32,1024]{1,0:T(8,128)S(1)} %get-tuple-element.61), channel_id=1, source_target_pairs={{2,4},{4,2},{3,5},{5,3},{10,12},{12,10},{11,13},{13,11},{18,20},{2... | collective-permute-start | bytes 393224 | tf_op jit(solution)/shard_map/ppermute | solution.py:326
  17.7 8.1 %collective-permute-start.11 = (f32[64,1024]{1,0:T(8,128)S(1)}, f32[64,1024]{1,0:T(8,128)S(1)}, u32[]{:S(2)}, u32[]{:S(2)}) collective-permute-start(f32[64,1024]{1,0:T(8,128)S(1)} %get-tuple-element.56.after.inner_own), channel_id=1, source_target_pairs={{0,8},{8,0},{1,9},{9,1},{2,10},{10,2},{3,11},{11,3},{4,12},{12,4},... | collective-permute-start | bytes 786440 | tf_op jit(solution)/shard_map/ppermute | solution.py:330
  19.9 5.6 %collective-permute-start.6 = (f32[32,1024]{1,0:T(8,128)S(1)}, f32[32,1024]{1,0:T(8,128)S(1)}, u32[]{:S(2)}, u32[]{:S(2)}) collective-permute-start(f32[32,1024]{1,0:T(8,128)S(1)} %get-tuple-element.57), channel_id=1, source_target_pairs={{0,2},{2,0},{4,6},{6,4},{1,3},{3,1},{5,7},{7,5},{8,10},{10,8},{12,... | collective-permute-start | bytes 393224 | tf_op jit(solution)/shard_map/ppermute | solution.py:326
  22.5 3.0 %collective-permute-start.7 = (f32[32,1024]{1,0:T(8,128)S(1)}, f32[32,1024]{1,0:T(8,128)S(1)}, u32[]{:S(2)}, u32[]{:S(2)}) collective-permute-start(f32[32,1024]{1,0:T(8,128)S(1)} %get-tuple-element.58), channel_id=1, source_target_pairs={{2,4},{4,2},{3,5},{5,3},{10,12},{12,10},{11,13},{13,11},{18,20},{2... | collective-permute-start | bytes 393224 | tf_op jit(solution)/shard_map/ppermute | solution.py:326
  23.5 7.1 %collective-permute-start.10 = (f32[64,1024]{1,0:T(8,128)S(1)}, f32[64,1024]{1,0:T(8,128)S(1)}, u32[]{:S(2)}, u32[]{:S(2)}) collective-permute-start(f32[64,1024]{1,0:T(8,128)S(1)} %get-tuple-element.62.after.rim_own), channel_id=1, source_target_pairs={{0,8},{8,0},{1,9},{9,1},{2,10},{10,2},{3,11},{11,3},{4,12},{12,4},... | collective-permute-start | bytes 786440 | tf_op jit(solution)/shard_map/ppermute | solution.py:330
  30.7 13.3 %collective-permute-start.18 = (f32[128,1024]{1,0:T(8,128)S(1)}, f32[128,1024]{1,0:T(8,128)S(1)}, u32[]{:S(2)}, u32[]{:S(2)}) collective-permute-start(f32[128,1024]{1,0:T(8,128)S(1)} %get-tuple-element.75), channel_id=1, source_target_pairs={{0,8},{8,0},{1,9},{9,1},{2,10},{10,2},{3,11},{11,3},{4,12},{12,4},... | collective-permute-start | bytes 1572872 | tf_op jit(solution)/shard_map/ppermute | solution.py:330
  31.8 5.4 %collective-permute-start.14 = (f32[8,128]{1,0:T(8,128)S(1)}, f32[8,128]{1,0:T(8,128)S(1)}, u32[]{:S(2)}, u32[]{:S(2)}) collective-permute-start(f32[8,128]{1,0:T(8,128)S(1)} %get-tuple-element.68), channel_id=1, source_target_pairs={{0,6},{2,4},{4,2},{6,0},{1,7},{3,5},{5,3},{7,1},{8,14},{10,12},{12... | collective-permute-start | bytes 12296 | tf_op jit(solution)/shard_map/ppermute | solution.py:337
  33.4 4.9 %collective-permute-start.13 = (f32[8,128]{1,0:T(8,128)S(1)}, f32[8,128]{1,0:T(8,128)S(1)}, u32[]{:S(2)}, u32[]{:S(2)}) collective-permute-start(f32[8,128]{1,0:T(8,128)S(1)} %get-tuple-element.68), channel_id=1, source_target_pairs={{0,4},{2,6},{4,0},{6,2},{1,5},{3,7},{5,1},{7,3},{8,12},{10,14},{12... | collective-permute-start | bytes 12296 | tf_op jit(solution)/shard_map/ppermute | solution.py:337
  36.7 3.6 %collective-permute-start.12 = (f32[8,128]{1,0:T(8,128)S(1)}, f32[8,128]{1,0:T(8,128)S(1)}, u32[]{:S(2)}, u32[]{:S(2)}) collective-permute-start(f32[8,128]{1,0:T(8,128)S(1)} %get-tuple-element.68), channel_id=1, source_target_pairs={{0,2},{2,0},{4,6},{6,4},{1,3},{3,1},{5,7},{7,5},{8,10},{10,8},{12,... | collective-permute-start | bytes 12296 | tf_op jit(solution)/shard_map/ppermute | solution.py:337
  40.3 3.0 %collective-permute-start.17 = (f32[8,128]{1,0:T(8,128)S(1)}, f32[8,128]{1,0:T(8,128)S(1)}, u32[]{:S(2)}, u32[]{:S(2)}) collective-permute-start(f32[8,128]{1,0:T(8,128)S(1)} %add_add_fusion.1), channel_id=1, source_target_pairs={{0,9},{1,8},{8,1},{9,0},{2,11},{3,10},{10,3},{11,2},{4,13},{5,12},... | collective-permute-start | bytes 12296 | tf_op jit(solution)/shard_map/ppermute | solution.py:337
  40.3 3.7 %collective-permute-start.16 = (f32[8,128]{1,0:T(8,128)S(1)}, f32[8,128]{1,0:T(8,128)S(1)}, u32[]{:S(2)}, u32[]{:S(2)}) collective-permute-start(f32[8,128]{1,0:T(8,128)S(1)} %add_add_fusion.1), channel_id=1, source_target_pairs={{0,8},{1,9},{8,0},{9,1},{2,10},{3,11},{10,2},{11,3},{4,12},{5,13},... | collective-permute-start | bytes 12296 | tf_op jit(solution)/shard_map/ppermute | solution.py:337
  40.9 3.1 %collective-permute-start.15 = (f32[8,128]{1,0:T(8,128)S(1)}, f32[8,128]{1,0:T(8,128)S(1)}, u32[]{:S(2)}, u32[]{:S(2)}) collective-permute-start(f32[8,128]{1,0:T(8,128)S(1)} %add_add_fusion.1), channel_id=1, source_target_pairs={{0,1},{1,0},{8,9},{9,8},{2,3},{3,2},{10,11},{11,10},{4,5},{5,4},{1... | collective-permute-start | bytes 12296 | tf_op jit(solution)/shard_map/ppermute | solution.py:337

commit v5 on v4

--- a/solution.py
+++ b/solution.py
@@ -166,7 +166,7 @@
 
 
 def rim_ratio_kernel(
-    which, came, goes, across, first, second, wide, taps, row_taps, after, rims, sent_first, sent_second, smooth, ratios
+    which, came, across, first, second, wide, taps, row_taps, after, rims, smooth, ratios
 ):
     height = across.shape[0]
     share = rims.shape[1]
@@ -183,9 +183,6 @@
     masses = jnp.concatenate([wide[:HALF, lanes], wide[height - HALF :, lanes]], axis=0)
     ratios[...] = ratio_of(masses, smooth[...])
     column_pass(ratios, taps, rims)
-    odd = row_parity(goes)
-    sent_first[...] = rims[pl.ds(pl.multiple_of((1 - odd) * HALF, HALF), HALF), :]
-    sent_second[...] = rims[pl.ds(pl.multiple_of(odd * HALF, HALF), HALF), :]
 
 
 def inner_log_kernel(which, weight, rims, inner, logs, row_taps, smooth, own):
@@ -198,6 +195,12 @@
         smooth[:, start:stop] = jnp.log(row_block(window, row_taps[...]))
     lanes = pl.ds(pl.multiple_of(offset, LANES), share)
     own[...] = weight[:1, :1] * (logs[HALF : height - HALF, lanes] + smooth[...])
+
+
+def rim_sends_kernel(goes, rims, after, sent_first, sent_second):
+    odd = row_parity(goes)
+    sent_first[...] = rims[pl.ds(pl.multiple_of((1 - odd) * HALF, HALF), HALF), :]
+    sent_second[...] = rims[pl.ds(pl.multiple_of(odd * HALF, HALF), HALF), :]
 
 
 def rim_log_kernel(which, came, weight, from_first, from_second, rims, inner, logs, row_taps, after, smooth, own):
@@ -239,22 +242,22 @@
 
 def rim_mean_kernel(own, smooth, arrived, inner_own, before, mean, change, partial, later):
     partial[...] = before[...] + mean_part(own, smooth, arrived, mean, change)
-    height = later.shape[0]
+    rest = later.shape[0] - HALF
     later[:HALF, :] = own[:HALF, :]
-    later[HALF : height - HALF, :] = inner_own[...]
-    later[height - HALF :, :] = own[HALF:, :]
-
-
-def later_mean_kernel(rim_own, rim_smooth, inner_own, inner_smooth, arrived, mean, change):
-    height = mean.shape[0]
-    for rows, own, smooth, part in (
-        (slice(0, HALF), rim_own, rim_smooth, slice(0, HALF)),
-        (slice(HALF, height - HALF), inner_own, inner_smooth, slice(None)),
-        (slice(height - HALF, height), rim_own, rim_smooth, slice(HALF, 2 * HALF)),
+    later[HALF:rest, :] = inner_own[...]
+    later[rest:, :] = own[HALF:, :]
+
+
+def later_mean_kernel(rim_own, rim_smooth, inner_own, inner_smooth, later, mean, change):
+    rest = mean.shape[0] - HALF
+    for rows, own, smooth in (
+        (slice(0, HALF), rim_own[:HALF, :], rim_smooth[:HALF, :]),
+        (slice(HALF, rest), inner_own[...], inner_smooth[...]),
+        (slice(rest, rest + HALF), rim_own[HALF:, :], rim_smooth[HALF:, :]),
     ):
-        log_mean = own[part, :] + arrived[rows, :]
+        log_mean = own + later[rows, :]
         mean[rows, :] = jnp.exp(log_mean)
-        change[rows, :] = log_mean - smooth[part, :]
+        change[rows, :] = log_mean - smooth
 
 
 def final_kernel(
@@ -384,10 +387,10 @@
 
     def rim_ratio(which, arrived, after):
         return call(
-            functools.partial(rim_ratio_kernel, which, *flips[which]), which + "_rim_ratio",
+            functools.partial(rim_ratio_kernel, which, flips[which][0]), which + "_rim_ratio",
             (across, *arrived, masses, taps, rim_taps, after),
-            [(edge, share), (HALF, share), (HALF, share)], [(edge, share + LANES)] * 2, cost=matmul,
-        )
+            [(edge, share)], [(edge, share + LANES)] * 2, cost=matmul,
+        )[0]
 
     def inner_log(which, rims):
         return call(
@@ -401,13 +404,21 @@
             (weight, *arrived, rims, inside, logs, rim_taps, after), [(edge, share)] * 2, cost=matmul,
         )
 
-    other_rims, *sent = rim_ratio("other", other_arrived, inside)
-    other_arrived = swap_rows(0, *sent)
+    def rim_exchange(which, rims, after):
+        goes = flips[which][1]
+        sent = call(
+            functools.partial(rim_sends_kernel, goes), which + "_rim_sends", (rims, after), [(HALF, share)] * 2,
+            cost=0 * matmul,
+        )
+        return swap_rows(goes, *sent)
+
+    other_rims = rim_ratio("other", other_arrived, inside)
     other_inner_smooth, other_inner_own = inner_log("other", other_rims)
-    own_rims, *sent = rim_ratio("own", own_arrived, other_inner_own)
-    own_arrived = swap_rows(0, *sent)
-    other_rim_smooth, other_rim_own = rim_log("other", other_rims, other_arrived, own_rims)
+    other_arrived = rim_exchange("other", other_rims, other_inner_own)
+    own_rims = rim_ratio("own", own_arrived, other_inner_own)
     inner_smooth, inner_own = inner_log("own", own_rims)
+    own_arrived = rim_exchange("own", own_rims, inner_own)
+    other_rim_smooth, other_rim_own = rim_log("other", other_rims, other_arrived, inner_own)
     rim_smooth, rim_own = rim_log("own", own_rims, own_arrived, other_rim_own)
 
     if count != 2:

time: 45.8 us -> 44.8 us (0.978)
  starting transfers between devices: 25.5 us -> 24.5 us
    ppermute x6, starting transfers between devices: 6.74 us -> 6.25 us  [total_over(): lax.ppermute(values, axes, [(i, i ^ mask) for i in range(count)])]
    ppermute x3, starting transfers between devices: 3.23 us -> 2.76 us  [swap_hist(): return lax.ppermute(values, 'hist', [(0, 1), (1, 0)])]
    pallas_call x16 -> x18, Pallas kernels: 6.34 us -> 6.39 us  [call(): pl.pallas_call(kernel, name=name, out_shape=tuple((shaped(shape) for shap...]
where the time goes in v5:
time: 44.8 us; the launch traced here: 44.6 us
  starting transfers between devices  24.5 us (55%)
  waiting for transfers between devices  11.7 us (26%)
  Pallas kernels  6.39 us (14%)
  local copies, waits for them, and re-layouts  1.23 us (3%)
  between operations  0.86 us (2%)
    ppermute x4, starting transfers between devices, swap_rows(): lax.ppermute(first, 'rows', pairs(flip))  11.1 us
    pallas_call x18, Pallas kernels, call(): pl.pallas_call(kernel, name=name, out_shape=tuple((shaped(shape) for shap...  6.39 us
    ppermute x6, starting transfers between devices, total_over(): lax.ppermute(values, axes, [(i, i ^ mask) for i in range(count)])  6.25 us
    ppermute x6, waiting for transfers between devices, total_over(): lax.ppermute(values, axes, [(i, i ^ mask) for i in range(count)])  5.08 us
    ppermute x3, waiting for transfers between devices, swap_hist(): return lax.ppermute(values, 'hist', [(0, 1), (1, 0)])  4.73 us
    ppermute x4, starting transfers between devices, swap_rows(): lax.ppermute(second, 'rows', pairs(1 - flip))  3.79 us
    ppermute x3, starting transfers between devices, swap_hist(): return lax.ppermute(values, 'hist', [(0, 1), (1, 0)])  2.76 us
    ppermute x4, waiting for transfers between devices, swap_rows(): lax.ppermute(first, 'rows', pairs(flip))  1.71 us
  transfers between devices with their start and end apart: 19, of which 9 were waited for; matrix products, arithmetic and copies ran while one was open for 0% of the time, Pallas kernels for 9%

profile of v5, /device:TPU:0, one launch (start us, length us, event | category | flops | bytes accessed | tf_op | source)
XLA Modules:
  0.0 44.6 jit_solution(15646265394334664000)
XLA Ops:
  0.6 0.1 bands.1
  0.7 0.0 copy-start
  0.7 1.2 %copy-done = f32[1,128,2048]{2,1,0:T(8,128)S(1)} copy-done((f32[1,128,2048]{2,1,0:T(8,128)S(1)}, f32[1,128,2048]{2,1,0:T(8,128)}, u32[]{:S(2)}) %copy-start) | copy-done | bytes 1048600
  2.0 0.1 log_edges.1
  2.0 0.5 %collective-permute-start = (f32[128,128]{1,0:T(8,128)S(1)}, f32[128,128]{1,0:T(8,128)S(1)}, u32[]{:S(2)}, u32[]{:S(2)}) collective-permute-start(f32[128,128]{1,0:T(8,128)S(1)} %get-tuple-element.41), channel_id=1, source_target_pairs={{0,1},{1,0},{2,3},{3,2},{4,5},{5,4},{6,7},{7,6},{8,9},{9,8},{10,11... | collective-permute-start | bytes 196616 | tf_op jit(solution)/shard_map/ppermute | solution.py:314
  2.5 0.8 %spread.1.partial = f32[128,2176]{1,0:T(8,128)S(1)} custom-call(f32[128,2048]{1,0:T(8,128)S(1)} %get-tuple-element.40.logs, bf16[192,256]{1,0:T(8,128)(2,1)S(1)} %get-tuple-element.39.taps), custom_call_target="tpu_custom_call" | custom-call | flops 2013265920 | bytes 1572864 | tf_op jit(solution)/shard_map/spread/pallas_call | solution.py:298
  3.3 0.0 copy-start.1
  3.3 0.1 collective-permute-done.from_left.from_right
  3.5 0.3 spread_edge.1
  3.8 0.7 %collective-permute-start.5 = (f32[32,1152]{1,0:T(8,128)S(1)}, f32[32,1152]{1,0:T(8,128)S(1)}, u32[]{:S(2)}, u32[]{:S(2)}) collective-permute-start(f32[32,1152]{1,0:T(8,128)S(1)} %get-tuple-element.51), channel_id=1, source_target_pairs={{2,4},{4,2},{3,5},{5,3},{10,12},{12,10},{11,13},{13,11},{18,20},{2... | collective-permute-start | bytes 442376 | tf_op jit(solution)/shard_map/ppermute | solution.py:329
  4.4 5.8 %collective-permute-start.4 = (f32[32,1152]{1,0:T(8,128)S(1)}, f32[32,1152]{1,0:T(8,128)S(1)}, u32[]{:S(2)}, u32[]{:S(2)}) collective-permute-start(f32[32,1152]{1,0:T(8,128)S(1)} %get-tuple-element.43.after), channel_id=1, source_target_pairs={{0,2},{2,0},{4,6},{6,4},{1,3},{3,1},{5,7},{7,5},{8,10},{10,8},{12,... | collective-permute-start | bytes 442376 | tf_op jit(solution)/shard_map/ppermute | solution.py:329
  10.3 0.1 collective-permute-start.1
  10.4 0.7 %collective-permute-start.2 = (f32[32,1152]{1,0:T(8,128)S(1)}, f32[32,1152]{1,0:T(8,128)S(1)}, u32[]{:S(2)}, u32[]{:S(2)}) collective-permute-start(f32[32,1152]{1,0:T(8,128)S(1)} %get-tuple-element.47), channel_id=1, source_target_pairs={{2,4},{4,2},{3,5},{5,3},{10,12},{12,10},{11,13},{13,11},{18,20},{2... | collective-permute-start | bytes 442376 | tf_op jit(solution)/shard_map/ppermute | solution.py:329
  11.0 1.8 %collective-permute-start.3 = (f32[32,1152]{1,0:T(8,128)S(1)}, f32[32,1152]{1,0:T(8,128)S(1)}, u32[]{:S(2)}, u32[]{:S(2)}) collective-permute-start(f32[32,1152]{1,0:T(8,128)S(1)} %get-tuple-element.48), channel_id=1, source_target_pairs={{0,2},{2,0},{4,6},{6,4},{1,3},{3,1},{5,7},{7,5},{8,10},{10,8},{12,... | collective-permute-start | bytes 442376 | tf_op jit(solution)/shard_map/ppermute | solution.py:329
  12.8 0.0 collective-permute-done.1.from_left.from_right
  12.9 0.9 %inner_ratio.1 = (f32[64,2048]{1,0:T(8,128)S(1)}, f32[128,2176]{1,0:T(8,128)S(1)}, f32[8,128]{1,0:T(8,128)S(1)}) custom-call(f32[128,2176]{1,0:T(8,128)S(1)} %get-tuple-element.42.across, f32[128,2048]{1,0:T(8,128)S(1)} %bitcast.6, f32[128,128]{1,0:T(8,128)S(1)} %collective-permute-done.1.from_left.from_right, ...), custom_call_target="tpu_custom_call" | custom-call | tf_op jit(solution)/shard_map/inner_ratio/pallas_call | solution.py:298
  13.8 0.3 collective-permute-done.4.first
  14.1 0.6 %other_rim_ratio.1.rims = f32[64,1024]{1,0:T(8,128)S(1)} custom-call(f32[128,2176]{1,0:T(8,128)S(1)} %get-tuple-element.42.across, f32[32,1152]{1,0:T(8,128)S(1)} %collective-permute-done.4.first, f32[32,1152]{1,0:T(8,128)S(1)} %collective-permute-done.5.second, f32[128,2176]{1,0:T(8,128)S(1)} %get-tuple-element.49.wide, ...), custom_call_target="tpu_custom_call" | custom-call | flops 2013265920 | bytes 1572864 | tf_op jit(solution)/shard_map/other_rim_ratio/pallas_call | solution.py:298
  14.8 0.3 other_inner_log.1
  15.1 1.6 %collective-permute-start.11 = (f32[64,1024]{1,0:T(8,128)S(1)}, f32[64,1024]{1,0:T(8,128)S(1)}, u32[]{:S(2)}, u32[]{:S(2)}) collective-permute-start(f32[64,1024]{1,0:T(8,128)S(1)} %get-tuple-element.53.after.inner_own), channel_id=1, source_target_pairs={{0,8},{8,0},{1,9},{9,1},{2,10},{10,2},{3,11},{11,3},{4,12},{12,4},... | collective-permute-start | bytes 786440 | tf_op jit(solution)/shard_map/ppermute | solution.py:333
  16.6 1.9 %collective-permute-start.8 = (f32[32,1024]{1,0:T(8,128)S(1)}, f32[32,1024]{1,0:T(8,128)S(1)}, u32[]{:S(2)}, u32[]{:S(2)}) collective-permute-start(f32[32,1024]{1,0:T(8,128)S(1)} %get-tuple-element.57), channel_id=1, source_target_pairs={{0,2},{2,0},{4,6},{6,4},{1,3},{3,1},{5,7},{7,5},{8,10},{10,8},{12,... | collective-permute-start | bytes 393224 | tf_op jit(solution)/shard_map/ppermute | solution.py:329
  18.5 0.7 %collective-permute-start.9 = (f32[32,1024]{1,0:T(8,128)S(1)}, f32[32,1024]{1,0:T(8,128)S(1)}, u32[]{:S(2)}, u32[]{:S(2)}) collective-permute-start(f32[32,1024]{1,0:T(8,128)S(1)} %get-tuple-element.58), channel_id=1, source_target_pairs={{2,4},{4,2},{3,5},{5,3},{10,12},{12,10},{11,13},{13,11},{18,20},{2... | collective-permute-start | bytes 393224 | tf_op jit(solution)/shard_map/ppermute | solution.py:329
  19.2 0.0 collective-permute-done.2.first
  19.2 0.0 collective-permute-done.3.second
  19.2 0.6 %own_rim_ratio.1.rims = f32[64,1024]{1,0:T(8,128)S(1)} custom-call(f32[128,2176]{1,0:T(8,128)S(1)} %get-tuple-element.42.across, f32[32,1152]{1,0:T(8,128)S(1)} %collective-permute-done.2.first, f32[32,1152]{1,0:T(8,128)S(1)} %collective-permute-done.3.second, f32[128,2176]{1,0:T(8,128)S(1)} %get-tuple-element.49.wide, ...), custom_call_target="tpu_custom_call" | custom-call | flops 2013265920 | bytes 1572864 | tf_op jit(solution)/shard_map/own_rim_ratio/pallas_call | solution.py:298
  19.9 0.3 own_inner_log.1
  20.2 2.7 %collective-permute-start.6 = (f32[32,1024]{1,0:T(8,128)S(1)}, f32[32,1024]{1,0:T(8,128)S(1)}, u32[]{:S(2)}, u32[]{:S(2)}) collective-permute-start(f32[32,1024]{1,0:T(8,128)S(1)} %get-tuple-element.55), channel_id=1, source_target_pairs={{0,2},{2,0},{4,6},{6,4},{1,3},{3,1},{5,7},{7,5},{8,10},{10,8},{12,... | collective-permute-start | bytes 393224 | tf_op jit(solution)/shard_map/ppermute | solution.py:329
  22.9 0.7 %collective-permute-start.7 = (f32[32,1024]{1,0:T(8,128)S(1)}, f32[32,1024]{1,0:T(8,128)S(1)}, u32[]{:S(2)}, u32[]{:S(2)}) collective-permute-start(f32[32,1024]{1,0:T(8,128)S(1)} %get-tuple-element.56), channel_id=1, source_target_pairs={{2,4},{4,2},{3,5},{5,3},{10,12},{12,10},{11,13},{13,11},{18,20},{2... | collective-permute-start | bytes 393224 | tf_op jit(solution)/shard_map/ppermute | solution.py:329
  23.6 0.3 other_rim_log.1
  23.8 0.6 %collective-permute-start.10 = (f32[64,1024]{1,0:T(8,128)S(1)}, f32[64,1024]{1,0:T(8,128)S(1)}, u32[]{:S(2)}, u32[]{:S(2)}) collective-permute-start(f32[64,1024]{1,0:T(8,128)S(1)} %get-tuple-element.59.after.rim_own), channel_id=1, source_target_pairs={{0,8},{8,0},{1,9},{9,1},{2,10},{10,2},{3,11},{11,3},{4,12},{12,4},... | collective-permute-start | bytes 786440 | tf_op jit(solution)/shard_map/ppermute | solution.py:333
  24.4 1.4 %collective-permute-done.6.from_first = f32[32,1024]{1,0:T(8,128)S(1)} collective-permute-done((f32[32,1024]{1,0:T(8,128)S(1)}, f32[32,1024]{1,0:T(8,128)S(1)}, u32[]{:S(2)}, u32[]{:S(2)}) %collective-permute-start.6) | collective-permute-done | bytes 131104 | tf_op jit(solution)/shard_map/ppermute | solution.py:329
  25.8 0.3 own_rim_log.1
  26.1 0.1 inner_mean.1
  26.2 4.7 %collective-permute-done.10.arrived = f32[64,1024]{1,0:T(8,128)S(1)} collective-permute-done((f32[64,1024]{1,0:T(8,128)S(1)}, f32[64,1024]{1,0:T(8,128)S(1)}, u32[]{:S(2)}, u32[]{:S(2)}) %collective-permute-start.10) | collective-permute-done | bytes 262176 | tf_op jit(solution)/shard_map/ppermute | solution.py:333
  30.9 0.1 rim_mean.1
  31.0 0.6 %collective-permute-start.18 = (f32[128,1024]{1,0:T(8,128)S(1)}, f32[128,1024]{1,0:T(8,128)S(1)}, u32[]{:S(2)}, u32[]{:S(2)}) collective-permute-start(f32[128,1024]{1,0:T(8,128)S(1)} %get-tuple-element.71), channel_id=1, source_target_pairs={{0,8},{8,0},{1,9},{9,1},{2,10},{10,2},{3,11},{11,3},{4,12},{12,4},... | collective-permute-start | bytes 1572872 | tf_op jit(solution)/shard_map/ppermute | solution.py:333
  31.6 1.3 %collective-permute-start.14 = (f32[8,128]{1,0:T(8,128)S(1)}, f32[8,128]{1,0:T(8,128)S(1)}, u32[]{:S(2)}, u32[]{:S(2)}) collective-permute-start(f32[8,128]{1,0:T(8,128)S(1)} %get-tuple-element.64), channel_id=1, source_target_pairs={{0,6},{2,4},{4,2},{6,0},{1,7},{3,5},{5,3},{7,1},{8,14},{10,12},{12... | collective-permute-start | bytes 12296 | tf_op jit(solution)/shard_map/ppermute | solution.py:340
  33.0 1.8 %collective-permute-start.13 = (f32[8,128]{1,0:T(8,128)S(1)}, f32[8,128]{1,0:T(8,128)S(1)}, u32[]{:S(2)}, u32[]{:S(2)}) collective-permute-start(f32[8,128]{1,0:T(8,128)S(1)} %get-tuple-element.64), channel_id=1, source_target_pairs={{0,4},{2,6},{4,0},{6,2},{1,5},{3,7},{5,1},{7,3},{8,12},{10,14},{12... | collective-permute-start | bytes 12296 | tf_op jit(solution)/shard_map/ppermute | solution.py:340
  34.8 1.2 %collective-permute-start.12 = (f32[8,128]{1,0:T(8,128)S(1)}, f32[8,128]{1,0:T(8,128)S(1)}, u32[]{:S(2)}, u32[]{:S(2)}) collective-permute-start(f32[8,128]{1,0:T(8,128)S(1)} %get-tuple-element.64), channel_id=1, source_target_pairs={{0,2},{2,0},{4,6},{6,4},{1,3},{3,1},{5,7},{7,5},{8,10},{10,8},{12,... | collective-permute-start | bytes 12296 | tf_op jit(solution)/shard_map/ppermute | solution.py:340
  36.0 1.0 %collective-permute-done.14 = f32[8,128]{1,0:T(8,128)S(1)} collective-permute-done((f32[8,128]{1,0:T(8,128)S(1)}, f32[8,128]{1,0:T(8,128)S(1)}, u32[]{:S(2)}, u32[]{:S(2)}) %collective-permute-start.14) | collective-permute-done | bytes 4128 | tf_op jit(solution)/shard_map/ppermute | solution.py:340
  37.0 0.4 %collective-permute-done.13 = f32[8,128]{1,0:T(8,128)S(1)} collective-permute-done((f32[8,128]{1,0:T(8,128)S(1)}, f32[8,128]{1,0:T(8,128)S(1)}, u32[]{:S(2)}, u32[]{:S(2)}) %collective-permute-start.13) | collective-permute-done | bytes 4128 | tf_op jit(solution)/shard_map/ppermute | solution.py:340
  37.5 0.9 %collective-permute-done.12 = f32[8,128]{1,0:T(8,128)S(1)} collective-permute-done((f32[8,128]{1,0:T(8,128)S(1)}, f32[8,128]{1,0:T(8,128)S(1)}, u32[]{:S(2)}, u32[]{:S(2)}) %collective-permute-start.12) | collective-permute-done | bytes 4128 | tf_op jit(solution)/shard_map/ppermute | solution.py:340
  38.4 1.6 %collective-permute-start.16 = (f32[8,128]{1,0:T(8,128)S(1)}, f32[8,128]{1,0:T(8,128)S(1)}, u32[]{:S(2)}, u32[]{:S(2)}) collective-permute-start(f32[8,128]{1,0:T(8,128)S(1)} %add_add_fusion.1), channel_id=1, source_target_pairs={{0,8},{1,9},{8,0},{9,1},{2,10},{3,11},{10,2},{11,3},{4,12},{5,13},... | collective-permute-start | bytes 12296 | tf_op jit(solution)/shard_map/ppermute | solution.py:340
  40.0 0.3 collective-permute-start.15
  40.3 1.3 %collective-permute-done.17 = f32[8,128]{1,0:T(8,128)S(1)} collective-permute-done((f32[8,128]{1,0:T(8,128)S(1)}, f32[8,128]{1,0:T(8,128)S(1)}, u32[]{:S(2)}, u32[]{:S(2)}) %collective-permute-start.17) | collective-permute-done | bytes 4128 | tf_op jit(solution)/shard_map/ppermute | solution.py:340
  41.6 1.4 %collective-permute-done.16 = f32[8,128]{1,0:T(8,128)S(1)} collective-permute-done((f32[8,128]{1,0:T(8,128)S(1)}, f32[8,128]{1,0:T(8,128)S(1)}, u32[]{:S(2)}, u32[]{:S(2)}) %collective-permute-start.16) | collective-permute-done | bytes 4128 | tf_op jit(solution)/shard_map/ppermute | solution.py:340
  43.0 0.1 later_mean.1
  43.1 1.5 %final.1 = (f32[128,2048]{1,0:T(8,128)}, f32[128,2048]{1,0:T(8,128)}) custom-call(f32[8,128]{1,0:T(8,128)S(1)} %add_add_fusion.total, f32[64,1024]{1,0:T(8,128)S(1)} %get-tuple-element.65.rim_mean, f32[64,1024]{1,0:T(8,128)S(1)} %get-tuple-element.66.rim_change, f32[64,1024]{1,0:T(8,128)S(1)} %get-tuple-element.67.inner_mean, ...), custom_call_target="tpu_custom_call" | custom-call | flops 503316480 | bytes 393216 | tf_op jit(solution)/shard_map/final/pallas_call | solution.py:298
  (16 shorter events, 0.1 us)
Async XLA Ops:
  0.7 1.2 %copy-start = (f32[1,128,2048]{2,1,0:T(8,128)S(1)}, f32[1,128,2048]{2,1,0:T(8,128)}, u32[]{:S(2)}) copy-start(f32[1,128,2048]{2,1,0:T(8,128)} %param.4) | copy-start | bytes 3145732
  2.0 1.4 %collective-permute-start = (f32[128,128]{1,0:T(8,128)S(1)}, f32[128,128]{1,0:T(8,128)S(1)}, u32[]{:S(2)}, u32[]{:S(2)}) collective-permute-start(f32[128,128]{1,0:T(8,128)S(1)} %get-tuple-element.41), channel_id=1, source_target_pairs={{0,1},{1,0},{2,3},{3,2},{4,5},{5,4},{6,7},{7,6},{8,9},{9,8},{10,11... | collective-permute-start | bytes 196616 | tf_op jit(solution)/shard_map/ppermute | solution.py:314
  3.3 6.9 %copy-start.1 = (f32[1,128,2048]{2,1,0:T(8,128)S(1)}, f32[1,128,2048]{2,1,0:T(8,128)}, u32[]{:S(2)}) copy-start(f32[1,128,2048]{2,1,0:T(8,128)} %param.3) | copy-start | bytes 3145732
  3.8 10.0 %collective-permute-start.5 = (f32[32,1152]{1,0:T(8,128)S(1)}, f32[32,1152]{1,0:T(8,128)S(1)}, u32[]{:S(2)}, u32[]{:S(2)}) collective-permute-start(f32[32,1152]{1,0:T(8,128)S(1)} %get-tuple-element.51), channel_id=1, source_target_pairs={{2,4},{4,2},{3,5},{5,3},{10,12},{12,10},{11,13},{13,11},{18,20},{2... | collective-permute-start | bytes 442376 | tf_op jit(solution)/shard_map/ppermute | solution.py:329
  4.4 9.7 %collective-permute-start.4 = (f32[32,1152]{1,0:T(8,128)S(1)}, f32[32,1152]{1,0:T(8,128)S(1)}, u32[]{:S(2)}, u32[]{:S(2)}) collective-permute-start(f32[32,1152]{1,0:T(8,128)S(1)} %get-tuple-element.43.after), channel_id=1, source_target_pairs={{0,2},{2,0},{4,6},{6,4},{1,3},{3,1},{5,7},{7,5},{8,10},{10,8},{12,... | collective-permute-start | bytes 442376 | tf_op jit(solution)/shard_map/ppermute | solution.py:329
  10.3 2.6 %copy-start.2 = (f32[2]{0:T(128)S(1)}, f32[2]{0:T(128)}, u32[]{:S(2)}) copy-start(f32[2]{0:T(128)} %param.5) | copy-start | bytes 28
  10.3 2.6 %collective-permute-start.1 = (f32[128,128]{1,0:T(8,128)S(1)}, f32[128,128]{1,0:T(8,128)S(1)}, u32[]{:S(2)}, u32[]{:S(2)}) collective-permute-start(f32[128,128]{1,0:T(8,128)S(1)} %get-tuple-element.44), channel_id=1, source_target_pairs={{0,1},{1,0},{2,3},{3,2},{4,5},{5,4},{6,7},{7,6},{8,9},{9,8},{10,11... | collective-permute-start | bytes 196616 | tf_op jit(solution)/shard_map/ppermute | solution.py:314
  10.4 8.8 %collective-permute-start.2 = (f32[32,1152]{1,0:T(8,128)S(1)}, f32[32,1152]{1,0:T(8,128)S(1)}, u32[]{:S(2)}, u32[]{:S(2)}) collective-permute-start(f32[32,1152]{1,0:T(8,128)S(1)} %get-tuple-element.47), channel_id=1, source_target_pairs={{2,4},{4,2},{3,5},{5,3},{10,12},{12,10},{11,13},{13,11},{18,20},{2... | collective-permute-start | bytes 442376 | tf_op jit(solution)/shard_map/ppermute | solution.py:329
  11.0 8.2 %collective-permute-start.3 = (f32[32,1152]{1,0:T(8,128)S(1)}, f32[32,1152]{1,0:T(8,128)S(1)}, u32[]{:S(2)}, u32[]{:S(2)}) collective-permute-start(f32[32,1152]{1,0:T(8,128)S(1)} %get-tuple-element.48), channel_id=1, source_target_pairs={{0,2},{2,0},{4,6},{6,4},{1,3},{3,1},{5,7},{7,5},{8,10},{10,8},{12,... | collective-permute-start | bytes 442376 | tf_op jit(solution)/shard_map/ppermute | solution.py:329
  15.1 11.0 %collective-permute-start.11 = (f32[64,1024]{1,0:T(8,128)S(1)}, f32[64,1024]{1,0:T(8,128)S(1)}, u32[]{:S(2)}, u32[]{:S(2)}) collective-permute-start(f32[64,1024]{1,0:T(8,128)S(1)} %get-tuple-element.53.after.inner_own), channel_id=1, source_target_pairs={{0,8},{8,0},{1,9},{9,1},{2,10},{10,2},{3,11},{11,3},{4,12},{12,4},... | collective-permute-start | bytes 786440 | tf_op jit(solution)/shard_map/ppermute | solution.py:333
  16.6 6.9 %collective-permute-start.8 = (f32[32,1024]{1,0:T(8,128)S(1)}, f32[32,1024]{1,0:T(8,128)S(1)}, u32[]{:S(2)}, u32[]{:S(2)}) collective-permute-start(f32[32,1024]{1,0:T(8,128)S(1)} %get-tuple-element.57), channel_id=1, source_target_pairs={{0,2},{2,0},{4,6},{6,4},{1,3},{3,1},{5,7},{7,5},{8,10},{10,8},{12,... | collective-permute-start | bytes 393224 | tf_op jit(solution)/shard_map/ppermute | solution.py:329
  18.5 5.0 %collective-permute-start.9 = (f32[32,1024]{1,0:T(8,128)S(1)}, f32[32,1024]{1,0:T(8,128)S(1)}, u32[]{:S(2)}, u32[]{:S(2)}) collective-permute-start(f32[32,1024]{1,0:T(8,128)S(1)} %get-tuple-element.58), channel_id=1, source_target_pairs={{2,4},{4,2},{3,5},{5,3},{10,12},{12,10},{11,13},{13,11},{18,20},{2... | collective-permute-start | bytes 393224 | tf_op jit(solution)/shard_map/ppermute | solution.py:329
  20.2 5.6 %collective-permute-start.6 = (f32[32,1024]{1,0:T(8,128)S(1)}, f32[32,1024]{1,0:T(8,128)S(1)}, u32[]{:S(2)}, u32[]{:S(2)}) collective-permute-start(f32[32,1024]{1,0:T(8,128)S(1)} %get-tuple-element.55), channel_id=1, source_target_pairs={{0,2},{2,0},{4,6},{6,4},{1,3},{3,1},{5,7},{7,5},{8,10},{10,8},{12,... | collective-permute-start | bytes 393224 | tf_op jit(solution)/shard_map/ppermute | solution.py:329
  22.9 3.0 %collective-permute-start.7 = (f32[32,1024]{1,0:T(8,128)S(1)}, f32[32,1024]{1,0:T(8,128)S(1)}, u32[]{:S(2)}, u32[]{:S(2)}) collective-permute-start(f32[32,1024]{1,0:T(8,128)S(1)} %get-tuple-element.56), channel_id=1, source_target_pairs={{2,4},{4,2},{3,5},{5,3},{10,12},{12,10},{11,13},{13,11},{18,20},{2... | collective-permute-start | bytes 393224 | tf_op jit(solution)/shard_map/ppermute | solution.py:329
  23.8 7.1 %collective-permute-start.10 = (f32[64,1024]{1,0:T(8,128)S(1)}, f32[64,1024]{1,0:T(8,128)S(1)}, u32[]{:S(2)}, u32[]{:S(2)}) collective-permute-start(f32[64,1024]{1,0:T(8,128)S(1)} %get-tuple-element.59.after.rim_own), channel_id=1, source_target_pairs={{0,8},{8,0},{1,9},{9,1},{2,10},{10,2},{3,11},{11,3},{4,12},{12,4},... | collective-permute-start | bytes 786440 | tf_op jit(solution)/shard_map/ppermute | solution.py:333
  31.0 12.0 %collective-permute-start.18 = (f32[128,1024]{1,0:T(8,128)S(1)}, f32[128,1024]{1,0:T(8,128)S(1)}, u32[]{:S(2)}, u32[]{:S(2)}) collective-permute-start(f32[128,1024]{1,0:T(8,128)S(1)} %get-tuple-element.71), channel_id=1, source_target_pairs={{0,8},{8,0},{1,9},{9,1},{2,10},{10,2},{3,11},{11,3},{4,12},{12,4},... | collective-permute-start | bytes 1572872 | tf_op jit(solution)/shard_map/ppermute | solution.py:333
  31.6 5.4 %collective-permute-start.14 = (f32[8,128]{1,0:T(8,128)S(1)}, f32[8,128]{1,0:T(8,128)S(1)}, u32[]{:S(2)}, u32[]{:S(2)}) collective-permute-start(f32[8,128]{1,0:T(8,128)S(1)} %get-tuple-element.64), channel_id=1, source_target_pairs={{0,6},{2,4},{4,2},{6,0},{1,7},{3,5},{5,3},{7,1},{8,14},{10,12},{12... | collective-permute-start | bytes 12296 | tf_op jit(solution)/shard_map/ppermute | solution.py:340
  33.0 4.5 %collective-permute-start.13 = (f32[8,128]{1,0:T(8,128)S(1)}, f32[8,128]{1,0:T(8,128)S(1)}, u32[]{:S(2)}, u32[]{:S(2)}) collective-permute-start(f32[8,128]{1,0:T(8,128)S(1)} %get-tuple-element.64), channel_id=1, source_target_pairs={{0,4},{2,6},{4,0},{6,2},{1,5},{3,7},{5,1},{7,3},{8,12},{10,14},{12... | collective-permute-start | bytes 12296 | tf_op jit(solution)/shard_map/ppermute | solution.py:340
  34.8 3.6 %collective-permute-start.12 = (f32[8,128]{1,0:T(8,128)S(1)}, f32[8,128]{1,0:T(8,128)S(1)}, u32[]{:S(2)}, u32[]{:S(2)}) collective-permute-start(f32[8,128]{1,0:T(8,128)S(1)} %get-tuple-element.64), channel_id=1, source_target_pairs={{0,2},{2,0},{4,6},{6,4},{1,3},{3,1},{5,7},{7,5},{8,10},{10,8},{12,... | collective-permute-start | bytes 12296 | tf_op jit(solution)/shard_map/ppermute | solution.py:340
  38.4 3.1 %collective-permute-start.17 = (f32[8,128]{1,0:T(8,128)S(1)}, f32[8,128]{1,0:T(8,128)S(1)}, u32[]{:S(2)}, u32[]{:S(2)}) collective-permute-start(f32[8,128]{1,0:T(8,128)S(1)} %add_add_fusion.1), channel_id=1, source_target_pairs={{0,9},{1,8},{8,1},{9,0},{2,11},{3,10},{10,3},{11,2},{4,13},{5,12},... | collective-permute-start | bytes 12296 | tf_op jit(solution)/shard_map/ppermute | solution.py:340
  38.4 4.5 %collective-permute-start.16 = (f32[8,128]{1,0:T(8,128)S(1)}, f32[8,128]{1,0:T(8,128)S(1)}, u32[]{:S(2)}, u32[]{:S(2)}) collective-permute-start(f32[8,128]{1,0:T(8,128)S(1)} %add_add_fusion.1), channel_id=1, source_target_pairs={{0,8},{1,9},{8,0},{9,1},{2,10},{3,11},{10,2},{11,3},{4,12},{5,13},... | collective-permute-start | bytes 12296 | tf_op jit(solution)/shard_map/ppermute | solution.py:340
  40.0 3.0 %collective-permute-start.15 = (f32[8,128]{1,0:T(8,128)S(1)}, f32[8,128]{1,0:T(8,128)S(1)}, u32[]{:S(2)}, u32[]{:S(2)}) collective-permute-start(f32[8,128]{1,0:T(8,128)S(1)} %add_add_fusion.1), channel_id=1, source_target_pairs={{0,1},{1,0},{8,9},{9,8},{2,3},{3,2},{10,11},{11,10},{4,5},{5,4},{1... | collective-permute-start | bytes 12296 | tf_op jit(solution)/shard_map/ppermute | solution.py:340

commit v6 on v5

--- a/solution.py
+++ b/solution.py
@@ -116,7 +116,6 @@
     has_left, has_right = edge_flags()
     height, width = logs.shape
     edge = 2 * HALF
-    across[...] = partial[...]
     left = jnp.concatenate([from_left[:, edge:] * has_left, jnp.exp(logs[:, :LANES])], axis=1)
     right = jnp.concatenate([jnp.exp(logs[:, width - edge :]), from_right[:, :edge] * has_right], axis=1)
     across[:, :LANES] = column_block(left, taps[...])
@@ -236,16 +235,19 @@
     return folded(values)
 
 
-def inner_mean_kernel(own, smooth, arrived, mean, change, partial):
+def inner_mean_kernel(own, smooth, arrived, after, mean, change, partial):
     partial[...] = mean_part(own, smooth, arrived, mean, change)
 
 
-def rim_mean_kernel(own, smooth, arrived, inner_own, before, mean, change, partial, later):
+def later_kernel(rim_own, inner_own, after, later):
+    rest = later.shape[0] - HALF
+    later[:HALF, :] = rim_own[:HALF, :]
+    later[HALF:rest, :] = inner_own[...]
+    later[rest:, :] = rim_own[HALF:, :]
+
+
+def rim_mean_kernel(own, smooth, arrived, before, mean, change, partial):
     partial[...] = before[...] + mean_part(own, smooth, arrived, mean, change)
-    rest = later.shape[0] - HALF
-    later[:HALF, :] = own[:HALF, :]
-    later[HALF:rest, :] = inner_own[...]
-    later[rest:, :] = own[HALF:, :]
 
 
 def later_mean_kernel(rim_own, rim_smooth, inner_own, inner_smooth, later, mean, change):
@@ -291,13 +293,14 @@
         copy.wait()
 
 
-def call(kernel, name, args, outs, scratch=(), cost=0, far_out=False, sems=None):
+def call(kernel, name, args, outs, scratch=(), cost=0, aliases={}, far_out=False, sems=None):
     shaped = lambda shape: shape if isinstance(shape, jax.ShapeDtypeStruct) else jax.ShapeDtypeStruct(shape, jnp.float32)
     near = pl.BlockSpec(memory_space=pltpu.VMEM)
     far = pl.BlockSpec(memory_space=pl.ANY)
     return pl.pallas_call(
         kernel,
         name=name,
+        input_output_aliases=aliases,
         out_shape=tuple(shaped(shape) for shape in outs),
         in_specs=[near for _ in args],
         out_specs=tuple(far if far_out else near for _ in outs),
@@ -339,6 +342,26 @@
         return lax.psum(values, axes)
     arrived = [lax.ppermute(values, axes, [(i, i ^ mask) for i in range(count)]) for mask in range(1, count)]
     return values + sum(arrived)
+
+
+def apart(index, mask, span):
+    return (index // span ^ mask // span) * span + (index % span ^ mask % span)
+
+
+def total_aside(values):
+    hist, rows, cols = (lax.axis_size(axis) for axis in ("hist", "rows", "cols"))
+    if hist & (hist - 1) or cols & (cols - 1):
+        return lax.psum(values, ("hist", "cols"))
+    aside = cols if rows % 2 == 0 else 0
+    total = values
+    for k in range(hist):
+        for m in range(cols):
+            if k or m:
+                mask = k * rows * cols + (aside if k else 0) + m
+                total = total + lax.ppermute(
+                    values, ("hist", "rows", "cols"), [(i, apart(i, mask, rows * cols)) for i in range(hist * rows * cols)]
+                )
+    return total
 
 
 def body(hists, log_scaling_fields, histogram_weight_list):
@@ -369,7 +392,7 @@
     )
     across, *other_sent = call(
         spread_edge_kernel, "spread_edge", (partial, logs, from_left, from_right, taps),
-        [(height, wide_width)] + [(HALF, share + LANES)] * 2, cost=matmul // 8,
+        [(height, wide_width)] + [(HALF, share + LANES)] * 2, cost=matmul // 8, aliases={0: 0},
     )
     first, second, *edges = call(
         mass_edge_kernel, "mass_edges", (masses, across, other_sent[0]), [(HALF, share + LANES)] * 2 + tiles,
@@ -433,16 +456,18 @@
     inner_arrived = swap_hist(other_inner_own)
     rim_arrived = swap_hist(other_rim_own)
     inner_mean, inner_change, mass = call(
-        inner_mean_kernel, "inner_mean", (inner_own, inner_smooth, inner_arrived),
+        inner_mean_kernel, "inner_mean", (inner_own, inner_smooth, inner_arrived, rim_own),
         [(inner, share), (inner, share), (8, LANES)], cost=matmul // 4,
     )
-    rim_mean, rim_change, mass, later = call(
-        rim_mean_kernel, "rim_mean", (rim_own, rim_smooth, rim_arrived, inner_own, mass),
-        [(edge, share), (edge, share), (8, LANES), (height, share)], cost=matmul // 4,
+    turn = lax.ppermute(mass, "cols", [(i, i ^ 1) for i in range(lax.axis_size("cols") // 2 * 2)])
+    (later,) = call(later_kernel, "later", (rim_own, inner_own, turn), [(height, share)], cost=matmul // 4)
+    rim_mean, rim_change, mass = call(
+        rim_mean_kernel, "rim_mean", (rim_own, rim_smooth, rim_arrived, mass),
+        [(edge, share), (edge, share), (8, LANES)], cost=10 * matmul,
     )
     later_arrived = swap_hist(later)
     mass = total_over(mass, ("rows",))
-    mass = total_over(mass, ("hist", "cols"))
+    mass = total_aside(mass)
     later_mean, later_change = call(
         later_mean_kernel, "later_mean",
         (other_rim_own, other_rim_smooth, other_inner_own, other_inner_smooth, later_arrived),

time: 44.8 us -> 44.4 us (level)
  waiting for transfers between devices: 11.7 us -> 10.1 us
  starting transfers between devices: 24.5 us -> 25.5 us
    ppermute x6 -> x3, waiting for transfers between devices: 5.08 us -> 1.86 us  [total_over(): lax.ppermute(values, axes, [(i, i ^ mask) for i in range(count)])]
    ppermute x0 -> x4, waiting for transfers between devices: none -> 2.97 us  [the longest x3 1.82 us: total_aside(): lax.ppermute(values, ('hist', 'rows', 'cols'), [(i, apart(i, mask, rows *...]
    ppermute x0 -> x4, starting transfers between devices: none -> 2.83 us  [the longest x3 2.76 us: total_aside(): lax.ppermute(values, ('hist', 'rows', 'cols'), [(i, apart(i, mask, rows *...]
    ppermute x6 -> x3, starting transfers between devices: 6.25 us -> 4.45 us  [total_over(): lax.ppermute(values, axes, [(i, i ^ mask) for i in range(count)])]
    ppermute x3, waiting for transfers between devices: 4.73 us -> 3.39 us  [swap_hist(): return lax.ppermute(values, 'hist', [(0, 1), (1, 0)])]
    pallas_call x18 -> x19, Pallas kernels: 6.39 us -> 6.39 us  [call(): pl.pallas_call(kernel, name=name, input_output_aliases=aliases, out_shape...]
  transfers between devices with their start and end apart: 19 -> 20, of which waited for: 9 -> 10; matrix products, arithmetic and copies ran while one was open for 0% -> 0% of each run, Pallas kernels for 9% -> 10%
where the time goes in v6:
time: 44.4 us; the launch traced here: 44 us
  starting transfers between devices  25.5 us (57%)
  waiting for transfers between devices  10.1 us (23%)
  Pallas kernels  6.39 us (14%)
  local copies, waits for them, and re-layouts  1.23 us (3%)
  between operations  0.87 us (2%)
    ppermute x4, starting transfers between devices, swap_rows(): lax.ppermute(first, 'rows', pairs(flip))  11.1 us
    pallas_call x19, Pallas kernels, call(): pl.pallas_call(kernel, name=name, input_output_aliases=aliases, out_shape...  6.39 us
    ppermute x3, starting transfers between devices, total_over(): lax.ppermute(values, axes, [(i, i ^ mask) for i in range(count)])  4.45 us
    ppermute x4, starting transfers between devices, swap_rows(): lax.ppermute(second, 'rows', pairs(1 - flip))  3.79 us
    ppermute x3, waiting for transfers between devices, swap_hist(): return lax.ppermute(values, 'hist', [(0, 1), (1, 0)])  3.39 us
    ppermute x3, starting transfers between devices, total_aside(): lax.ppermute(values, ('hist', 'rows', 'cols'), [(i, apart(i, mask, rows *...  2.76 us
    ppermute x3, starting transfers between devices, swap_hist(): return lax.ppermute(values, 'hist', [(0, 1), (1, 0)])  2.76 us
    ppermute x3, waiting for transfers between devices, total_over(): lax.ppermute(values, axes, [(i, i ^ mask) for i in range(count)])  1.86 us
  transfers between devices with their start and end apart: 20, of which 10 were waited for; matrix products, arithmetic and copies ran while one was open for 0% of the time, Pallas kernels for 10%

profile of v6, /device:TPU:0, one launch (start us, length us, event | category | flops | bytes accessed | tf_op | source)
XLA Modules:
  0.0 44.0 jit_solution(14549435374929018286)
XLA Ops:
  0.6 0.1 bands.1
  0.7 0.0 copy-start
  0.7 1.2 %copy-done = f32[1,128,2048]{2,1,0:T(8,128)S(1)} copy-done((f32[1,128,2048]{2,1,0:T(8,128)S(1)}, f32[1,128,2048]{2,1,0:T(8,128)}, u32[]{:S(2)}) %copy-start) | copy-done | bytes 1048600
  2.0 0.1 log_edges.1
  2.0 0.5 %collective-permute-start = (f32[128,128]{1,0:T(8,128)S(1)}, f32[128,128]{1,0:T(8,128)S(1)}, u32[]{:S(2)}, u32[]{:S(2)}) collective-permute-start(f32[128,128]{1,0:T(8,128)S(1)} %get-tuple-element.40), channel_id=1, source_target_pairs={{0,1},{1,0},{2,3},{3,2},{4,5},{5,4},{6,7},{7,6},{8,9},{9,8},{10,11... | collective-permute-start | bytes 196616 | tf_op jit(solution)/shard_map/ppermute | solution.py:317
  2.5 0.8 %spread.1.partial = f32[128,2176]{1,0:T(8,128)S(1)} custom-call(f32[128,2048]{1,0:T(8,128)S(1)} %get-tuple-element.39.logs, bf16[192,256]{1,0:T(8,128)(2,1)S(1)} %get-tuple-element.38.taps), custom_call_target="tpu_custom_call" | custom-call | flops 2013265920 | bytes 1572864 | tf_op jit(solution)/shard_map/spread/pallas_call | solution.py:300
  3.3 0.0 copy-start.1
  3.3 0.1 collective-permute-done.from_left.from_right
  3.5 0.3 spread_edge.1
  3.8 0.7 %collective-permute-start.5 = (f32[32,1152]{1,0:T(8,128)S(1)}, f32[32,1152]{1,0:T(8,128)S(1)}, u32[]{:S(2)}, u32[]{:S(2)}) collective-permute-start(f32[32,1152]{1,0:T(8,128)S(1)} %get-tuple-element.50), channel_id=1, source_target_pairs={{2,4},{4,2},{3,5},{5,3},{10,12},{12,10},{11,13},{13,11},{18,20},{2... | collective-permute-start | bytes 442376 | tf_op jit(solution)/shard_map/ppermute | solution.py:332
  4.4 5.8 %collective-permute-start.4 = (f32[32,1152]{1,0:T(8,128)S(1)}, f32[32,1152]{1,0:T(8,128)S(1)}, u32[]{:S(2)}, u32[]{:S(2)}) collective-permute-start(f32[32,1152]{1,0:T(8,128)S(1)} %get-tuple-element.42.after), channel_id=1, source_target_pairs={{0,2},{2,0},{4,6},{6,4},{1,3},{3,1},{5,7},{7,5},{8,10},{10,8},{12,... | collective-permute-start | bytes 442376 | tf_op jit(solution)/shard_map/ppermute | solution.py:332
  10.3 0.1 collective-permute-start.1
  10.4 0.7 %collective-permute-start.2 = (f32[32,1152]{1,0:T(8,128)S(1)}, f32[32,1152]{1,0:T(8,128)S(1)}, u32[]{:S(2)}, u32[]{:S(2)}) collective-permute-start(f32[32,1152]{1,0:T(8,128)S(1)} %get-tuple-element.46), channel_id=1, source_target_pairs={{2,4},{4,2},{3,5},{5,3},{10,12},{12,10},{11,13},{13,11},{18,20},{2... | collective-permute-start | bytes 442376 | tf_op jit(solution)/shard_map/ppermute | solution.py:332
  11.0 1.8 %collective-permute-start.3 = (f32[32,1152]{1,0:T(8,128)S(1)}, f32[32,1152]{1,0:T(8,128)S(1)}, u32[]{:S(2)}, u32[]{:S(2)}) collective-permute-start(f32[32,1152]{1,0:T(8,128)S(1)} %get-tuple-element.47), channel_id=1, source_target_pairs={{0,2},{2,0},{4,6},{6,4},{1,3},{3,1},{5,7},{7,5},{8,10},{10,8},{12,... | collective-permute-start | bytes 442376 | tf_op jit(solution)/shard_map/ppermute | solution.py:332
  12.9 0.9 %inner_ratio.1 = (f32[64,2048]{1,0:T(8,128)S(1)}, f32[128,2176]{1,0:T(8,128)S(1)}, f32[8,128]{1,0:T(8,128)S(1)}) custom-call(f32[128,2176]{1,0:T(8,128)S(1)} %get-tuple-element.41.across, f32[128,2048]{1,0:T(8,128)S(1)} %bitcast.6, f32[128,128]{1,0:T(8,128)S(1)} %collective-permute-done.1.from_left.from_right, ...), custom_call_target="tpu_custom_call" | custom-call | tf_op jit(solution)/shard_map/inner_ratio/pallas_call | solution.py:300
  13.8 0.0 collective-permute-done.5.second
  13.8 0.3 collective-permute-done.4.first
  14.1 0.6 %other_rim_ratio.1.rims = f32[64,1024]{1,0:T(8,128)S(1)} custom-call(f32[128,2176]{1,0:T(8,128)S(1)} %get-tuple-element.41.across, f32[32,1152]{1,0:T(8,128)S(1)} %collective-permute-done.4.first, f32[32,1152]{1,0:T(8,128)S(1)} %collective-permute-done.5.second, f32[128,2176]{1,0:T(8,128)S(1)} %get-tuple-element.48.wide, ...), custom_call_target="tpu_custom_call" | custom-call | flops 2013265920 | bytes 1572864 | tf_op jit(solution)/shard_map/other_rim_ratio/pallas_call | solution.py:300
  14.8 0.3 other_inner_log.1
  15.1 1.6 %collective-permute-start.11 = (f32[64,1024]{1,0:T(8,128)S(1)}, f32[64,1024]{1,0:T(8,128)S(1)}, u32[]{:S(2)}, u32[]{:S(2)}) collective-permute-start(f32[64,1024]{1,0:T(8,128)S(1)} %get-tuple-element.52.after.inner_own), channel_id=1, source_target_pairs={{0,8},{8,0},{1,9},{9,1},{2,10},{10,2},{3,11},{11,3},{4,12},{12,4},... | collective-permute-start | bytes 786440 | tf_op jit(solution)/shard_map/ppermute | solution.py:336
  16.6 1.9 %collective-permute-start.8 = (f32[32,1024]{1,0:T(8,128)S(1)}, f32[32,1024]{1,0:T(8,128)S(1)}, u32[]{:S(2)}, u32[]{:S(2)}) collective-permute-start(f32[32,1024]{1,0:T(8,128)S(1)} %get-tuple-element.56), channel_id=1, source_target_pairs={{0,2},{2,0},{4,6},{6,4},{1,3},{3,1},{5,7},{7,5},{8,10},{10,8},{12,... | collective-permute-start | bytes 393224 | tf_op jit(solution)/shard_map/ppermute | solution.py:332
  18.5 0.7 %collective-permute-start.9 = (f32[32,1024]{1,0:T(8,128)S(1)}, f32[32,1024]{1,0:T(8,128)S(1)}, u32[]{:S(2)}, u32[]{:S(2)}) collective-permute-start(f32[32,1024]{1,0:T(8,128)S(1)} %get-tuple-element.57), channel_id=1, source_target_pairs={{2,4},{4,2},{3,5},{5,3},{10,12},{12,10},{11,13},{13,11},{18,20},{2... | collective-permute-start | bytes 393224 | tf_op jit(solution)/shard_map/ppermute | solution.py:332
  19.2 0.6 %own_rim_ratio.1.rims = f32[64,1024]{1,0:T(8,128)S(1)} custom-call(f32[128,2176]{1,0:T(8,128)S(1)} %get-tuple-element.41.across, f32[32,1152]{1,0:T(8,128)S(1)} %collective-permute-done.2.first, f32[32,1152]{1,0:T(8,128)S(1)} %collective-permute-done.3.second, f32[128,2176]{1,0:T(8,128)S(1)} %get-tuple-element.48.wide, ...), custom_call_target="tpu_custom_call" | custom-call | flops 2013265920 | bytes 1572864 | tf_op jit(solution)/shard_map/own_rim_ratio/pallas_call | solution.py:300
  19.8 0.3 own_inner_log.1
  20.2 2.7 %collective-permute-start.6 = (f32[32,1024]{1,0:T(8,128)S(1)}, f32[32,1024]{1,0:T(8,128)S(1)}, u32[]{:S(2)}, u32[]{:S(2)}) collective-permute-start(f32[32,1024]{1,0:T(8,128)S(1)} %get-tuple-element.54), channel_id=1, source_target_pairs={{0,2},{2,0},{4,6},{6,4},{1,3},{3,1},{5,7},{7,5},{8,10},{10,8},{12,... | collective-permute-start | bytes 393224 | tf_op jit(solution)/shard_map/ppermute | solution.py:332
  22.9 0.7 %collective-permute-start.7 = (f32[32,1024]{1,0:T(8,128)S(1)}, f32[32,1024]{1,0:T(8,128)S(1)}, u32[]{:S(2)}, u32[]{:S(2)}) collective-permute-start(f32[32,1024]{1,0:T(8,128)S(1)} %get-tuple-element.55), channel_id=1, source_target_pairs={{2,4},{4,2},{3,5},{5,3},{10,12},{12,10},{11,13},{13,11},{18,20},{2... | collective-permute-start | bytes 393224 | tf_op jit(solution)/shard_map/ppermute | solution.py:332
  23.5 0.3 other_rim_log.1
  23.8 0.6 %collective-permute-start.10 = (f32[64,1024]{1,0:T(8,128)S(1)}, f32[64,1024]{1,0:T(8,128)S(1)}, u32[]{:S(2)}, u32[]{:S(2)}) collective-permute-start(f32[64,1024]{1,0:T(8,128)S(1)} %get-tuple-element.58.after.rim_own), channel_id=1, source_target_pairs={{0,8},{8,0},{1,9},{9,1},{2,10},{10,2},{3,11},{11,3},{4,12},{12,4},... | collective-permute-start | bytes 786440 | tf_op jit(solution)/shard_map/ppermute | solution.py:336
  24.4 1.4 %collective-permute-done.6.from_first = f32[32,1024]{1,0:T(8,128)S(1)} collective-permute-done((f32[32,1024]{1,0:T(8,128)S(1)}, f32[32,1024]{1,0:T(8,128)S(1)}, u32[]{:S(2)}, u32[]{:S(2)}) %collective-permute-start.6) | collective-permute-done | bytes 131104 | tf_op jit(solution)/shard_map/ppermute | solution.py:332
  25.8 0.3 own_rim_log.1
  26.1 0.1 inner_mean.1
  26.2 0.1 collective-permute-start.18
  26.3 1.2 %collective-permute-done.18.after = f32[8,128]{1,0:T(8,128)S(1)} collective-permute-done((f32[8,128]{1,0:T(8,128)S(1)}, f32[8,128]{1,0:T(8,128)S(1)}, u32[]{:S(2)}, u32[]{:S(2)}) %collective-permute-start.18) | collective-permute-done | bytes 4128 | tf_op jit(solution)/shard_map/ppermute | solution.py:462
  27.5 0.6 %collective-permute-start.19 = (f32[128,1024]{1,0:T(8,128)S(1)}, f32[128,1024]{1,0:T(8,128)S(1)}, u32[]{:S(2)}, u32[]{:S(2)}) collective-permute-start(f32[128,1024]{1,0:T(8,128)S(1)} %later.1), channel_id=1, source_target_pairs={{0,8},{8,0},{1,9},{9,1},{2,10},{10,2},{3,11},{11,3},{4,12},{12,4},... | collective-permute-start | bytes 1572872 | tf_op jit(solution)/shard_map/ppermute | solution.py:336
  28.1 3.4 %collective-permute-done.10.arrived = f32[64,1024]{1,0:T(8,128)S(1)} collective-permute-done((f32[64,1024]{1,0:T(8,128)S(1)}, f32[64,1024]{1,0:T(8,128)S(1)}, u32[]{:S(2)}, u32[]{:S(2)}) %collective-permute-start.10) | collective-permute-done | bytes 262176 | tf_op jit(solution)/shard_map/ppermute | solution.py:336
  31.4 0.1 rim_mean.1
  31.5 1.1 %collective-permute-start.14 = (f32[8,128]{1,0:T(8,128)S(1)}, f32[8,128]{1,0:T(8,128)S(1)}, u32[]{:S(2)}, u32[]{:S(2)}) collective-permute-start(f32[8,128]{1,0:T(8,128)S(1)} %get-tuple-element.63), channel_id=1, source_target_pairs={{0,6},{2,4},{4,2},{6,0},{1,7},{3,5},{5,3},{7,1},{8,14},{10,12},{12... | collective-permute-start | bytes 12296 | tf_op jit(solution)/shard_map/ppermute | solution.py:343
  32.6 1.6 %collective-permute-start.13 = (f32[8,128]{1,0:T(8,128)S(1)}, f32[8,128]{1,0:T(8,128)S(1)}, u32[]{:S(2)}, u32[]{:S(2)}) collective-permute-start(f32[8,128]{1,0:T(8,128)S(1)} %get-tuple-element.63), channel_id=1, source_target_pairs={{0,4},{2,6},{4,0},{6,2},{1,5},{3,7},{5,1},{7,3},{8,12},{10,14},{12... | collective-permute-start | bytes 12296 | tf_op jit(solution)/shard_map/ppermute | solution.py:343
  34.2 1.7 %collective-permute-start.12 = (f32[8,128]{1,0:T(8,128)S(1)}, f32[8,128]{1,0:T(8,128)S(1)}, u32[]{:S(2)}, u32[]{:S(2)}) collective-permute-start(f32[8,128]{1,0:T(8,128)S(1)} %get-tuple-element.63), channel_id=1, source_target_pairs={{0,2},{2,0},{4,6},{6,4},{1,3},{3,1},{5,7},{7,5},{8,10},{10,8},{12,... | collective-permute-start | bytes 12296 | tf_op jit(solution)/shard_map/ppermute | solution.py:343
  36.0 1.0 %collective-permute-done.14 = f32[8,128]{1,0:T(8,128)S(1)} collective-permute-done((f32[8,128]{1,0:T(8,128)S(1)}, f32[8,128]{1,0:T(8,128)S(1)}, u32[]{:S(2)}, u32[]{:S(2)}) %collective-permute-start.14) | collective-permute-done | bytes 4128 | tf_op jit(solution)/shard_map/ppermute | solution.py:343
  37.0 0.2 collective-permute-done.13
  37.1 0.7 %collective-permute-done.12 = f32[8,128]{1,0:T(8,128)S(1)} collective-permute-done((f32[8,128]{1,0:T(8,128)S(1)}, f32[8,128]{1,0:T(8,128)S(1)}, u32[]{:S(2)}, u32[]{:S(2)}) %collective-permute-start.12) | collective-permute-done | bytes 4128 | tf_op jit(solution)/shard_map/ppermute | solution.py:343
  37.8 1.8 %collective-permute-start.16 = (f32[8,128]{1,0:T(8,128)S(1)}, f32[8,128]{1,0:T(8,128)S(1)}, u32[]{:S(2)}, u32[]{:S(2)}) collective-permute-start(f32[8,128]{1,0:T(8,128)S(1)} %add_add_fusion.1), channel_id=1, source_target_pairs={{0,10},{1,11},{2,8},{3,9},{4,14},{5,15},{6,12},{7,13},{8,2},{9,3},... | collective-permute-start | bytes 12296 | tf_op jit(solution)/shard_map/ppermute | solution.py:361
  39.6 1.0 %collective-permute-start.15 = (f32[8,128]{1,0:T(8,128)S(1)}, f32[8,128]{1,0:T(8,128)S(1)}, u32[]{:S(2)}, u32[]{:S(2)}) collective-permute-start(f32[8,128]{1,0:T(8,128)S(1)} %add_add_fusion.1), channel_id=1, source_target_pairs={{0,1},{1,0},{2,3},{3,2},{4,5},{5,4},{6,7},{7,6},{8,9},{9,8},{10,11... | collective-permute-start | bytes 12296 | tf_op jit(solution)/shard_map/ppermute | solution.py:361
  40.6 1.3 %collective-permute-done.17 = f32[8,128]{1,0:T(8,128)S(1)} collective-permute-done((f32[8,128]{1,0:T(8,128)S(1)}, f32[8,128]{1,0:T(8,128)S(1)}, u32[]{:S(2)}, u32[]{:S(2)}) %collective-permute-start.17) | collective-permute-done | bytes 4128 | tf_op jit(solution)/shard_map/ppermute | solution.py:361
  41.9 0.5 %collective-permute-done.16 = f32[8,128]{1,0:T(8,128)S(1)} collective-permute-done((f32[8,128]{1,0:T(8,128)S(1)}, f32[8,128]{1,0:T(8,128)S(1)}, u32[]{:S(2)}, u32[]{:S(2)}) %collective-permute-start.16) | collective-permute-done | bytes 4128 | tf_op jit(solution)/shard_map/ppermute | solution.py:361
  42.4 0.1 later_mean.1
  42.5 1.5 %final.1 = (f32[128,2048]{1,0:T(8,128)}, f32[128,2048]{1,0:T(8,128)}) custom-call(f32[8,128]{1,0:T(8,128)S(1)} %add_add_fusion.total, f32[64,1024]{1,0:T(8,128)S(1)} %get-tuple-element.64.rim_mean, f32[64,1024]{1,0:T(8,128)S(1)} %get-tuple-element.65.rim_change, f32[64,1024]{1,0:T(8,128)S(1)} %get-tuple-element.66.inner_mean, ...), custom_call_target="tpu_custom_call" | custom-call | flops 503316480 | bytes 393216 | tf_op jit(solution)/shard_map/final/pallas_call | solution.py:300
  (19 shorter events, 0.2 us)
Async XLA Ops:
  0.7 1.2 %copy-start = (f32[1,128,2048]{2,1,0:T(8,128)S(1)}, f32[1,128,2048]{2,1,0:T(8,128)}, u32[]{:S(2)}) copy-start(f32[1,128,2048]{2,1,0:T(8,128)} %param.4) | copy-start | bytes 3145732
  2.0 1.4 %collective-permute-start = (f32[128,128]{1,0:T(8,128)S(1)}, f32[128,128]{1,0:T(8,128)S(1)}, u32[]{:S(2)}, u32[]{:S(2)}) collective-permute-start(f32[128,128]{1,0:T(8,128)S(1)} %get-tuple-element.40), channel_id=1, source_target_pairs={{0,1},{1,0},{2,3},{3,2},{4,5},{5,4},{6,7},{7,6},{8,9},{9,8},{10,11... | collective-permute-start | bytes 196616 | tf_op jit(solution)/shard_map/ppermute | solution.py:317
  3.3 6.9 %copy-start.1 = (f32[1,128,2048]{2,1,0:T(8,128)S(1)}, f32[1,128,2048]{2,1,0:T(8,128)}, u32[]{:S(2)}) copy-start(f32[1,128,2048]{2,1,0:T(8,128)} %param.3) | copy-start | bytes 3145732
  3.8 10.0 %collective-permute-start.5 = (f32[32,1152]{1,0:T(8,128)S(1)}, f32[32,1152]{1,0:T(8,128)S(1)}, u32[]{:S(2)}, u32[]{:S(2)}) collective-permute-start(f32[32,1152]{1,0:T(8,128)S(1)} %get-tuple-element.50), channel_id=1, source_target_pairs={{2,4},{4,2},{3,5},{5,3},{10,12},{12,10},{11,13},{13,11},{18,20},{2... | collective-permute-start | bytes 442376 | tf_op jit(solution)/shard_map/ppermute | solution.py:332
  4.4 9.7 %collective-permute-start.4 = (f32[32,1152]{1,0:T(8,128)S(1)}, f32[32,1152]{1,0:T(8,128)S(1)}, u32[]{:S(2)}, u32[]{:S(2)}) collective-permute-start(f32[32,1152]{1,0:T(8,128)S(1)} %get-tuple-element.42.after), channel_id=1, source_target_pairs={{0,2},{2,0},{4,6},{6,4},{1,3},{3,1},{5,7},{7,5},{8,10},{10,8},{12,... | collective-permute-start | bytes 442376 | tf_op jit(solution)/shard_map/ppermute | solution.py:332
  10.3 2.6 %copy-start.2 = (f32[2]{0:T(128)S(1)}, f32[2]{0:T(128)}, u32[]{:S(2)}) copy-start(f32[2]{0:T(128)} %param.5) | copy-start | bytes 28
  10.3 2.6 %collective-permute-start.1 = (f32[128,128]{1,0:T(8,128)S(1)}, f32[128,128]{1,0:T(8,128)S(1)}, u32[]{:S(2)}, u32[]{:S(2)}) collective-permute-start(f32[128,128]{1,0:T(8,128)S(1)} %get-tuple-element.43), channel_id=1, source_target_pairs={{0,1},{1,0},{2,3},{3,2},{4,5},{5,4},{6,7},{7,6},{8,9},{9,8},{10,11... | collective-permute-start | bytes 196616 | tf_op jit(solution)/shard_map/ppermute | solution.py:317
  10.4 8.8 %collective-permute-start.2 = (f32[32,1152]{1,0:T(8,128)S(1)}, f32[32,1152]{1,0:T(8,128)S(1)}, u32[]{:S(2)}, u32[]{:S(2)}) collective-permute-start(f32[32,1152]{1,0:T(8,128)S(1)} %get-tuple-element.46), channel_id=1, source_target_pairs={{2,4},{4,2},{3,5},{5,3},{10,12},{12,10},{11,13},{13,11},{18,20},{2... | collective-permute-start | bytes 442376 | tf_op jit(solution)/shard_map/ppermute | solution.py:332
  11.0 8.2 %collective-permute-start.3 = (f32[32,1152]{1,0:T(8,128)S(1)}, f32[32,1152]{1,0:T(8,128)S(1)}, u32[]{:S(2)}, u32[]{:S(2)}) collective-permute-start(f32[32,1152]{1,0:T(8,128)S(1)} %get-tuple-element.47), channel_id=1, source_target_pairs={{0,2},{2,0},{4,6},{6,4},{1,3},{3,1},{5,7},{7,5},{8,10},{10,8},{12,... | collective-permute-start | bytes 442376 | tf_op jit(solution)/shard_map/ppermute | solution.py:332
  15.1 11.0 %collective-permute-start.11 = (f32[64,1024]{1,0:T(8,128)S(1)}, f32[64,1024]{1,0:T(8,128)S(1)}, u32[]{:S(2)}, u32[]{:S(2)}) collective-permute-start(f32[64,1024]{1,0:T(8,128)S(1)} %get-tuple-element.52.after.inner_own), channel_id=1, source_target_pairs={{0,8},{8,0},{1,9},{9,1},{2,10},{10,2},{3,11},{11,3},{4,12},{12,4},... | collective-permute-start | bytes 786440 | tf_op jit(solution)/shard_map/ppermute | solution.py:336
  16.6 6.9 %collective-permute-start.8 = (f32[32,1024]{1,0:T(8,128)S(1)}, f32[32,1024]{1,0:T(8,128)S(1)}, u32[]{:S(2)}, u32[]{:S(2)}) collective-permute-start(f32[32,1024]{1,0:T(8,128)S(1)} %get-tuple-element.56), channel_id=1, source_target_pairs={{0,2},{2,0},{4,6},{6,4},{1,3},{3,1},{5,7},{7,5},{8,10},{10,8},{12,... | collective-permute-start | bytes 393224 | tf_op jit(solution)/shard_map/ppermute | solution.py:332
  18.5 5.0 %collective-permute-start.9 = (f32[32,1024]{1,0:T(8,128)S(1)}, f32[32,1024]{1,0:T(8,128)S(1)}, u32[]{:S(2)}, u32[]{:S(2)}) collective-permute-start(f32[32,1024]{1,0:T(8,128)S(1)} %get-tuple-element.57), channel_id=1, source_target_pairs={{2,4},{4,2},{3,5},{5,3},{10,12},{12,10},{11,13},{13,11},{18,20},{2... | collective-permute-start | bytes 393224 | tf_op jit(solution)/shard_map/ppermute | solution.py:332
  20.2 5.6 %collective-permute-start.6 = (f32[32,1024]{1,0:T(8,128)S(1)}, f32[32,1024]{1,0:T(8,128)S(1)}, u32[]{:S(2)}, u32[]{:S(2)}) collective-permute-start(f32[32,1024]{1,0:T(8,128)S(1)} %get-tuple-element.54), channel_id=1, source_target_pairs={{0,2},{2,0},{4,6},{6,4},{1,3},{3,1},{5,7},{7,5},{8,10},{10,8},{12,... | collective-permute-start | bytes 393224 | tf_op jit(solution)/shard_map/ppermute | solution.py:332
  22.9 3.0 %collective-permute-start.7 = (f32[32,1024]{1,0:T(8,128)S(1)}, f32[32,1024]{1,0:T(8,128)S(1)}, u32[]{:S(2)}, u32[]{:S(2)}) collective-permute-start(f32[32,1024]{1,0:T(8,128)S(1)} %get-tuple-element.55), channel_id=1, source_target_pairs={{2,4},{4,2},{3,5},{5,3},{10,12},{12,10},{11,13},{13,11},{18,20},{2... | collective-permute-start | bytes 393224 | tf_op jit(solution)/shard_map/ppermute | solution.py:332
  23.8 7.6 %collective-permute-start.10 = (f32[64,1024]{1,0:T(8,128)S(1)}, f32[64,1024]{1,0:T(8,128)S(1)}, u32[]{:S(2)}, u32[]{:S(2)}) collective-permute-start(f32[64,1024]{1,0:T(8,128)S(1)} %get-tuple-element.58.after.rim_own), channel_id=1, source_target_pairs={{0,8},{8,0},{1,9},{9,1},{2,10},{10,2},{3,11},{11,3},{4,12},{12,4},... | collective-permute-start | bytes 786440 | tf_op jit(solution)/shard_map/ppermute | solution.py:336
  26.2 1.2 %collective-permute-start.18 = (f32[8,128]{1,0:T(8,128)S(1)}, f32[8,128]{1,0:T(8,128)S(1)}, u32[]{:S(2)}, u32[]{:S(2)}) collective-permute-start(f32[8,128]{1,0:T(8,128)S(1)} %get-tuple-element.62.before), channel_id=1, source_target_pairs={{0,1},{1,0},{2,3},{3,2},{4,5},{5,4},{6,7},{7,6},{8,9},{9,8},{10,11... | collective-permute-start | bytes 12296 | tf_op jit(solution)/shard_map/ppermute | solution.py:462
  27.5 15.0 %collective-permute-start.19 = (f32[128,1024]{1,0:T(8,128)S(1)}, f32[128,1024]{1,0:T(8,128)S(1)}, u32[]{:S(2)}, u32[]{:S(2)}) collective-permute-start(f32[128,1024]{1,0:T(8,128)S(1)} %later.1), channel_id=1, source_target_pairs={{0,8},{8,0},{1,9},{9,1},{2,10},{10,2},{3,11},{11,3},{4,12},{12,4},... | collective-permute-start | bytes 1572872 | tf_op jit(solution)/shard_map/ppermute | solution.py:336
  31.5 5.5 %collective-permute-start.14 = (f32[8,128]{1,0:T(8,128)S(1)}, f32[8,128]{1,0:T(8,128)S(1)}, u32[]{:S(2)}, u32[]{:S(2)}) collective-permute-start(f32[8,128]{1,0:T(8,128)S(1)} %get-tuple-element.63), channel_id=1, source_target_pairs={{0,6},{2,4},{4,2},{6,0},{1,7},{3,5},{5,3},{7,1},{8,14},{10,12},{12... | collective-permute-start | bytes 12296 | tf_op jit(solution)/shard_map/ppermute | solution.py:343
  32.6 4.5 %collective-permute-start.13 = (f32[8,128]{1,0:T(8,128)S(1)}, f32[8,128]{1,0:T(8,128)S(1)}, u32[]{:S(2)}, u32[]{:S(2)}) collective-permute-start(f32[8,128]{1,0:T(8,128)S(1)} %get-tuple-element.63), channel_id=1, source_target_pairs={{0,4},{2,6},{4,0},{6,2},{1,5},{3,7},{5,1},{7,3},{8,12},{10,14},{12... | collective-permute-start | bytes 12296 | tf_op jit(solution)/shard_map/ppermute | solution.py:343
  34.2 3.6 %collective-permute-start.12 = (f32[8,128]{1,0:T(8,128)S(1)}, f32[8,128]{1,0:T(8,128)S(1)}, u32[]{:S(2)}, u32[]{:S(2)}) collective-permute-start(f32[8,128]{1,0:T(8,128)S(1)} %get-tuple-element.63), channel_id=1, source_target_pairs={{0,2},{2,0},{4,6},{6,4},{1,3},{3,1},{5,7},{7,5},{8,10},{10,8},{12,... | collective-permute-start | bytes 12296 | tf_op jit(solution)/shard_map/ppermute | solution.py:343
  37.8 4.0 %collective-permute-start.17 = (f32[8,128]{1,0:T(8,128)S(1)}, f32[8,128]{1,0:T(8,128)S(1)}, u32[]{:S(2)}, u32[]{:S(2)}) collective-permute-start(f32[8,128]{1,0:T(8,128)S(1)} %add_add_fusion.1), channel_id=1, source_target_pairs={{0,11},{1,10},{2,9},{3,8},{4,15},{5,14},{6,13},{7,12},{8,3},{9,2},... | collective-permute-start | bytes 12296 | tf_op jit(solution)/shard_map/ppermute | solution.py:361
  37.8 4.6 %collective-permute-start.16 = (f32[8,128]{1,0:T(8,128)S(1)}, f32[8,128]{1,0:T(8,128)S(1)}, u32[]{:S(2)}, u32[]{:S(2)}) collective-permute-start(f32[8,128]{1,0:T(8,128)S(1)} %add_add_fusion.1), channel_id=1, source_target_pairs={{0,10},{1,11},{2,8},{3,9},{4,14},{5,15},{6,12},{7,13},{8,2},{9,3},... | collective-permute-start | bytes 12296 | tf_op jit(solution)/shard_map/ppermute | solution.py:361
  39.6 2.8 %collective-permute-start.15 = (f32[8,128]{1,0:T(8,128)S(1)}, f32[8,128]{1,0:T(8,128)S(1)}, u32[]{:S(2)}, u32[]{:S(2)}) collective-permute-start(f32[8,128]{1,0:T(8,128)S(1)} %add_add_fusion.1), channel_id=1, source_target_pairs={{0,1},{1,0},{2,3},{3,2},{4,5},{5,4},{6,7},{7,6},{8,9},{9,8},{10,11... | collective-permute-start | bytes 12296 | tf_op jit(solution)/shard_map/ppermute | solution.py:361

commit v7 on v6

--- a/solution.py
+++ b/solution.py
@@ -250,45 +250,36 @@
     partial[...] = before[...] + mean_part(own, smooth, arrived, mean, change)
 
 
-def later_mean_kernel(rim_own, rim_smooth, inner_own, inner_smooth, later, mean, change):
-    rest = mean.shape[0] - HALF
-    for rows, own, smooth in (
-        (slice(0, HALF), rim_own[:HALF, :], rim_smooth[:HALF, :]),
-        (slice(HALF, rest), inner_own[...], inner_smooth[...]),
-        (slice(rest, rest + HALF), rim_own[HALF:, :], rim_smooth[HALF:, :]),
-    ):
-        log_mean = own + later[rows, :]
-        mean[rows, :] = jnp.exp(log_mean)
-        change[rows, :] = log_mean - smooth
-
-
 def final_kernel(
-    cells, total, rim_mean, rim_change, inner_mean, inner_change, later_mean, later_change, barycenter, new_logs,
-    stage, sems,
+    cells, total, rim_mean, rim_change, inner_mean, inner_change, rim_own, rim_smooth, inner_own, inner_smooth, later,
+    barycenter, new_logs, stage, sems,
 ):
     height, width = barycenter.shape
     share = width // 2
+    rest = height - HALF
     scale = cells / jnp.sum(total[...], axis=(0, 1), keepdims=True)
     log_scale = jnp.log(scale)
+    rows = ((slice(0, HALF), slice(0, HALF)), (slice(HALF, rest), slice(None)), (slice(rest, height), slice(HALF, 2 * HALF)))
     copies = []
-    for k, (out, rim, inner, later, apply) in enumerate(
-        (
-            (barycenter, rim_mean, inner_mean, later_mean, lambda x: x * scale),
-            (new_logs, rim_change, inner_change, later_change, lambda x: x + log_scale),
-        )
-    ):
-        for step, which in enumerate(("own", "other")):
-            slot = slice(step * share, (step + 1) * share)
-            if which == "own":
-                stage[k, :HALF, slot] = apply(rim[:HALF, :])
-                stage[k, HALF : height - HALF, slot] = apply(inner[...])
-                stage[k, height - HALF :, slot] = apply(rim[HALF:, :])
-            else:
-                stage[k, :, slot] = apply(later[...])
-            lanes = pl.ds(pl.multiple_of(half_place(which) * share, LANES), share)
-            copy = pltpu.make_async_copy(stage.at[k, :, slot], out.at[:, lanes], sems.at[k, step])
-            copy.start()
-            copies.append(copy)
+
+    def send(k, step, which):
+        lanes = pl.ds(pl.multiple_of(half_place(which) * share, LANES), share)
+        source = stage.at[k, :, slice(step * share, (step + 1) * share)]
+        copy = pltpu.make_async_copy(source, (barycenter, new_logs)[k].at[:, lanes], sems.at[k, step])
+        copy.start()
+        copies.append(copy)
+
+    for (to, part), mean, change in zip(rows, (rim_mean, inner_mean, rim_mean), (rim_change, inner_change, rim_change)):
+        stage[0, to, :share] = mean[part, :] * scale
+        stage[1, to, :share] = change[part, :] + log_scale
+    send(0, 0, "own")
+    send(1, 0, "own")
+    for (to, part), own, smooth in zip(rows, (rim_own, inner_own, rim_own), (rim_smooth, inner_smooth, rim_smooth)):
+        log_mean = own[part, :] + later[to, :]
+        stage[0, to, share:] = jnp.exp(log_mean) * scale
+        stage[1, to, share:] = log_mean - smooth[part, :] + log_scale
+    send(0, 1, "other")
+    send(1, 1, "other")
     for copy in copies:
         copy.wait()
 
@@ -468,14 +459,10 @@
     later_arrived = swap_hist(later)
     mass = total_over(mass, ("rows",))
     mass = total_aside(mass)
-    later_mean, later_change = call(
-        later_mean_kernel, "later_mean",
-        (other_rim_own, other_rim_smooth, other_inner_own, other_inner_smooth, later_arrived),
-        [(height, share)] * 2, cost=matmul // 4,
-    )
     barycenter, new_logs = call(
         functools.partial(final_kernel, float(cells)), "final",
-        (mass, rim_mean, rim_change, inner_mean, inner_change, later_mean, later_change),
+        (mass, rim_mean, rim_change, inner_mean, inner_change, other_rim_own, other_rim_smooth, other_inner_own,
+         other_inner_smooth, later_arrived),
         [(height, width)] * 2, [(2, height, width)], far_out=True, sems=(2, 2), cost=matmul // 4,
     )
     return (barycenter, new_logs[None])

time: 44.4 us -> 44.4 us (level)
    pallas_call x19 -> x18, Pallas kernels: 6.39 us -> 6.32 us  [call(): pl.pallas_call(kernel, name=name, input_output_aliases=aliases, out_shape...]
where the time goes in v7:
time: 44.4 us; the launch traced here: 44 us
  starting transfers between devices  25.5 us (57%)
  waiting for transfers between devices  10.1 us (23%)
  Pallas kernels  6.32 us (14%)
  local copies, waits for them, and re-layouts  1.23 us (3%)
  between operations  0.86 us (2%)
    ppermute x4, starting transfers between devices, swap_rows(): lax.ppermute(first, 'rows', pairs(flip))  11.1 us
    pallas_call x18, Pallas kernels, call(): pl.pallas_call(kernel, name=name, input_output_aliases=aliases, out_shape...  6.32 us
    ppermute x3, starting transfers between devices, total_over(): lax.ppermute(values, axes, [(i, i ^ mask) for i in range(count)])  4.45 us
    ppermute x4, starting transfers between devices, swap_rows(): lax.ppermute(second, 'rows', pairs(1 - flip))  3.79 us
    ppermute x3, waiting for transfers between devices, swap_hist(): return lax.ppermute(values, 'hist', [(0, 1), (1, 0)])  3.41 us
    ppermute x3, starting transfers between devices, swap_hist(): return lax.ppermute(values, 'hist', [(0, 1), (1, 0)])  2.76 us
    ppermute x3, starting transfers between devices, total_aside(): lax.ppermute(values, ('hist', 'rows', 'cols'), [(i, apart(i, mask, rows *...  2.76 us
    ppermute x3, waiting for transfers between devices, total_over(): lax.ppermute(values, axes, [(i, i ^ mask) for i in range(count)])  1.84 us
  transfers between devices with their start and end apart: 20, of which 10 were waited for; matrix products, arithmetic and copies ran while one was open for 0% of the time, Pallas kernels for 10%

profile of v7, /device:TPU:0, one launch (start us, length us, event | category | flops | bytes accessed | tf_op | source)
XLA Modules:
  0.0 44.0 jit_solution(15346146731912432877)
XLA Ops:
  0.6 0.1 bands.1
  0.7 0.0 copy-start
  0.7 1.2 %copy-done = f32[1,128,2048]{2,1,0:T(8,128)S(1)} copy-done((f32[1,128,2048]{2,1,0:T(8,128)S(1)}, f32[1,128,2048]{2,1,0:T(8,128)}, u32[]{:S(2)}) %copy-start) | copy-done | bytes 1048600
  2.0 0.1 log_edges.1
  2.0 0.5 %collective-permute-start = (f32[128,128]{1,0:T(8,128)S(1)}, f32[128,128]{1,0:T(8,128)S(1)}, u32[]{:S(2)}, u32[]{:S(2)}) collective-permute-start(f32[128,128]{1,0:T(8,128)S(1)} %get-tuple-element.38), channel_id=1, source_target_pairs={{0,1},{1,0},{2,3},{3,2},{4,5},{5,4},{6,7},{7,6},{8,9},{9,8},{10,11... | collective-permute-start | bytes 196616 | tf_op jit(solution)/shard_map/ppermute | solution.py:308
  2.5 0.8 %spread.1.partial = f32[128,2176]{1,0:T(8,128)S(1)} custom-call(f32[128,2048]{1,0:T(8,128)S(1)} %get-tuple-element.37.logs, bf16[192,256]{1,0:T(8,128)(2,1)S(1)} %get-tuple-element.36.taps), custom_call_target="tpu_custom_call" | custom-call | flops 2013265920 | bytes 1572864 | tf_op jit(solution)/shard_map/spread/pallas_call | solution.py:291
  3.3 0.0 copy-start.1
  3.3 0.1 collective-permute-done.from_left.from_right
  3.5 0.3 spread_edge.1
  3.8 0.7 %collective-permute-start.5 = (f32[32,1152]{1,0:T(8,128)S(1)}, f32[32,1152]{1,0:T(8,128)S(1)}, u32[]{:S(2)}, u32[]{:S(2)}) collective-permute-start(f32[32,1152]{1,0:T(8,128)S(1)} %get-tuple-element.48), channel_id=1, source_target_pairs={{2,4},{4,2},{3,5},{5,3},{10,12},{12,10},{11,13},{13,11},{18,20},{2... | collective-permute-start | bytes 442376 | tf_op jit(solution)/shard_map/ppermute | solution.py:323
  4.4 5.8 %collective-permute-start.4 = (f32[32,1152]{1,0:T(8,128)S(1)}, f32[32,1152]{1,0:T(8,128)S(1)}, u32[]{:S(2)}, u32[]{:S(2)}) collective-permute-start(f32[32,1152]{1,0:T(8,128)S(1)} %get-tuple-element.40.after), channel_id=1, source_target_pairs={{0,2},{2,0},{4,6},{6,4},{1,3},{3,1},{5,7},{7,5},{8,10},{10,8},{12,... | collective-permute-start | bytes 442376 | tf_op jit(solution)/shard_map/ppermute | solution.py:323
  10.3 0.1 collective-permute-start.1
  10.4 0.7 %collective-permute-start.2 = (f32[32,1152]{1,0:T(8,128)S(1)}, f32[32,1152]{1,0:T(8,128)S(1)}, u32[]{:S(2)}, u32[]{:S(2)}) collective-permute-start(f32[32,1152]{1,0:T(8,128)S(1)} %get-tuple-element.44), channel_id=1, source_target_pairs={{2,4},{4,2},{3,5},{5,3},{10,12},{12,10},{11,13},{13,11},{18,20},{2... | collective-permute-start | bytes 442376 | tf_op jit(solution)/shard_map/ppermute | solution.py:323
  11.0 1.8 %collective-permute-start.3 = (f32[32,1152]{1,0:T(8,128)S(1)}, f32[32,1152]{1,0:T(8,128)S(1)}, u32[]{:S(2)}, u32[]{:S(2)}) collective-permute-start(f32[32,1152]{1,0:T(8,128)S(1)} %get-tuple-element.45), channel_id=1, source_target_pairs={{0,2},{2,0},{4,6},{6,4},{1,3},{3,1},{5,7},{7,5},{8,10},{10,8},{12,... | collective-permute-start | bytes 442376 | tf_op jit(solution)/shard_map/ppermute | solution.py:323
  12.9 0.9 %inner_ratio.1 = (f32[64,2048]{1,0:T(8,128)S(1)}, f32[128,2176]{1,0:T(8,128)S(1)}, f32[8,128]{1,0:T(8,128)S(1)}) custom-call(f32[128,2176]{1,0:T(8,128)S(1)} %get-tuple-element.39.across, f32[128,2048]{1,0:T(8,128)S(1)} %bitcast.6, f32[128,128]{1,0:T(8,128)S(1)} %collective-permute-done.1.from_left.from_right, ...), custom_call_target="tpu_custom_call" | custom-call | tf_op jit(solution)/shard_map/inner_ratio/pallas_call | solution.py:291
  13.8 0.0 collective-permute-done.5.second
  13.8 0.3 collective-permute-done.4.first
  14.1 0.6 %other_rim_ratio.1.rims = f32[64,1024]{1,0:T(8,128)S(1)} custom-call(f32[128,2176]{1,0:T(8,128)S(1)} %get-tuple-element.39.across, f32[32,1152]{1,0:T(8,128)S(1)} %collective-permute-done.4.first, f32[32,1152]{1,0:T(8,128)S(1)} %collective-permute-done.5.second, f32[128,2176]{1,0:T(8,128)S(1)} %get-tuple-element.46.wide, ...), custom_call_target="tpu_custom_call" | custom-call | flops 2013265920 | bytes 1572864 | tf_op jit(solution)/shard_map/other_rim_ratio/pallas_call | solution.py:291
  14.8 0.3 other_inner_log.1
  15.1 1.6 %collective-permute-start.11 = (f32[64,1024]{1,0:T(8,128)S(1)}, f32[64,1024]{1,0:T(8,128)S(1)}, u32[]{:S(2)}, u32[]{:S(2)}) collective-permute-start(f32[64,1024]{1,0:T(8,128)S(1)} %get-tuple-element.50.after.inner_own), channel_id=1, source_target_pairs={{0,8},{8,0},{1,9},{9,1},{2,10},{10,2},{3,11},{11,3},{4,12},{12,4},... | collective-permute-start | bytes 786440 | tf_op jit(solution)/shard_map/ppermute | solution.py:327
  16.6 1.9 %collective-permute-start.8 = (f32[32,1024]{1,0:T(8,128)S(1)}, f32[32,1024]{1,0:T(8,128)S(1)}, u32[]{:S(2)}, u32[]{:S(2)}) collective-permute-start(f32[32,1024]{1,0:T(8,128)S(1)} %get-tuple-element.54), channel_id=1, source_target_pairs={{0,2},{2,0},{4,6},{6,4},{1,3},{3,1},{5,7},{7,5},{8,10},{10,8},{12,... | collective-permute-start | bytes 393224 | tf_op jit(solution)/shard_map/ppermute | solution.py:323
  18.5 0.7 %collective-permute-start.9 = (f32[32,1024]{1,0:T(8,128)S(1)}, f32[32,1024]{1,0:T(8,128)S(1)}, u32[]{:S(2)}, u32[]{:S(2)}) collective-permute-start(f32[32,1024]{1,0:T(8,128)S(1)} %get-tuple-element.55), channel_id=1, source_target_pairs={{2,4},{4,2},{3,5},{5,3},{10,12},{12,10},{11,13},{13,11},{18,20},{2... | collective-permute-start | bytes 393224 | tf_op jit(solution)/shard_map/ppermute | solution.py:323
  19.2 0.0 collective-permute-done.3.second
  19.2 0.6 %own_rim_ratio.1.rims = f32[64,1024]{1,0:T(8,128)S(1)} custom-call(f32[128,2176]{1,0:T(8,128)S(1)} %get-tuple-element.39.across, f32[32,1152]{1,0:T(8,128)S(1)} %collective-permute-done.2.first, f32[32,1152]{1,0:T(8,128)S(1)} %collective-permute-done.3.second, f32[128,2176]{1,0:T(8,128)S(1)} %get-tuple-element.46.wide, ...), custom_call_target="tpu_custom_call" | custom-call | flops 2013265920 | bytes 1572864 | tf_op jit(solution)/shard_map/own_rim_ratio/pallas_call | solution.py:291
  19.8 0.3 own_inner_log.1
  20.2 2.7 %collective-permute-start.6 = (f32[32,1024]{1,0:T(8,128)S(1)}, f32[32,1024]{1,0:T(8,128)S(1)}, u32[]{:S(2)}, u32[]{:S(2)}) collective-permute-start(f32[32,1024]{1,0:T(8,128)S(1)} %get-tuple-element.52), channel_id=1, source_target_pairs={{0,2},{2,0},{4,6},{6,4},{1,3},{3,1},{5,7},{7,5},{8,10},{10,8},{12,... | collective-permute-start | bytes 393224 | tf_op jit(solution)/shard_map/ppermute | solution.py:323
  22.8 0.7 %collective-permute-start.7 = (f32[32,1024]{1,0:T(8,128)S(1)}, f32[32,1024]{1,0:T(8,128)S(1)}, u32[]{:S(2)}, u32[]{:S(2)}) collective-permute-start(f32[32,1024]{1,0:T(8,128)S(1)} %get-tuple-element.53), channel_id=1, source_target_pairs={{2,4},{4,2},{3,5},{5,3},{10,12},{12,10},{11,13},{13,11},{18,20},{2... | collective-permute-start | bytes 393224 | tf_op jit(solution)/shard_map/ppermute | solution.py:323
  23.5 0.3 other_rim_log.1
  23.8 0.6 %collective-permute-start.10 = (f32[64,1024]{1,0:T(8,128)S(1)}, f32[64,1024]{1,0:T(8,128)S(1)}, u32[]{:S(2)}, u32[]{:S(2)}) collective-permute-start(f32[64,1024]{1,0:T(8,128)S(1)} %get-tuple-element.56.after.rim_own), channel_id=1, source_target_pairs={{0,8},{8,0},{1,9},{9,1},{2,10},{10,2},{3,11},{11,3},{4,12},{12,4},... | collective-permute-start | bytes 786440 | tf_op jit(solution)/shard_map/ppermute | solution.py:327
  24.4 1.4 %collective-permute-done.6.from_first = f32[32,1024]{1,0:T(8,128)S(1)} collective-permute-done((f32[32,1024]{1,0:T(8,128)S(1)}, f32[32,1024]{1,0:T(8,128)S(1)}, u32[]{:S(2)}, u32[]{:S(2)}) %collective-permute-start.6) | collective-permute-done | bytes 131104 | tf_op jit(solution)/shard_map/ppermute | solution.py:323
  25.8 0.3 own_rim_log.1
  26.1 0.1 inner_mean.1
  26.2 0.1 collective-permute-start.18
  26.3 1.2 %collective-permute-done.18.after = f32[8,128]{1,0:T(8,128)S(1)} collective-permute-done((f32[8,128]{1,0:T(8,128)S(1)}, f32[8,128]{1,0:T(8,128)S(1)}, u32[]{:S(2)}, u32[]{:S(2)}) %collective-permute-start.18) | collective-permute-done | bytes 4128 | tf_op jit(solution)/shard_map/ppermute | solution.py:453
  27.4 0.6 %collective-permute-start.19 = (f32[128,1024]{1,0:T(8,128)S(1)}, f32[128,1024]{1,0:T(8,128)S(1)}, u32[]{:S(2)}, u32[]{:S(2)}) collective-permute-start(f32[128,1024]{1,0:T(8,128)S(1)} %later.1), channel_id=1, source_target_pairs={{0,8},{8,0},{1,9},{9,1},{2,10},{10,2},{3,11},{11,3},{4,12},{12,4},... | collective-permute-start | bytes 1572872 | tf_op jit(solution)/shard_map/ppermute | solution.py:327
  28.1 3.4 %collective-permute-done.10.arrived = f32[64,1024]{1,0:T(8,128)S(1)} collective-permute-done((f32[64,1024]{1,0:T(8,128)S(1)}, f32[64,1024]{1,0:T(8,128)S(1)}, u32[]{:S(2)}, u32[]{:S(2)}) %collective-permute-start.10) | collective-permute-done | bytes 262176 | tf_op jit(solution)/shard_map/ppermute | solution.py:327
  31.5 0.1 rim_mean.1
  31.5 1.1 %collective-permute-start.14 = (f32[8,128]{1,0:T(8,128)S(1)}, f32[8,128]{1,0:T(8,128)S(1)}, u32[]{:S(2)}, u32[]{:S(2)}) collective-permute-start(f32[8,128]{1,0:T(8,128)S(1)} %get-tuple-element.61), channel_id=1, source_target_pairs={{0,6},{2,4},{4,2},{6,0},{1,7},{3,5},{5,3},{7,1},{8,14},{10,12},{12... | collective-permute-start | bytes 12296 | tf_op jit(solution)/shard_map/ppermute | solution.py:334
  32.6 1.6 %collective-permute-start.13 = (f32[8,128]{1,0:T(8,128)S(1)}, f32[8,128]{1,0:T(8,128)S(1)}, u32[]{:S(2)}, u32[]{:S(2)}) collective-permute-start(f32[8,128]{1,0:T(8,128)S(1)} %get-tuple-element.61), channel_id=1, source_target_pairs={{0,4},{2,6},{4,0},{6,2},{1,5},{3,7},{5,1},{7,3},{8,12},{10,14},{12... | collective-permute-start | bytes 12296 | tf_op jit(solution)/shard_map/ppermute | solution.py:334
  34.2 1.8 %collective-permute-start.12 = (f32[8,128]{1,0:T(8,128)S(1)}, f32[8,128]{1,0:T(8,128)S(1)}, u32[]{:S(2)}, u32[]{:S(2)}) collective-permute-start(f32[8,128]{1,0:T(8,128)S(1)} %get-tuple-element.61), channel_id=1, source_target_pairs={{0,2},{2,0},{4,6},{6,4},{1,3},{3,1},{5,7},{7,5},{8,10},{10,8},{12,... | collective-permute-start | bytes 12296 | tf_op jit(solution)/shard_map/ppermute | solution.py:334
  36.0 1.0 %collective-permute-done.14 = f32[8,128]{1,0:T(8,128)S(1)} collective-permute-done((f32[8,128]{1,0:T(8,128)S(1)}, f32[8,128]{1,0:T(8,128)S(1)}, u32[]{:S(2)}, u32[]{:S(2)}) %collective-permute-start.14) | collective-permute-done | bytes 4128 | tf_op jit(solution)/shard_map/ppermute | solution.py:334
  37.0 0.1 collective-permute-done.13
  37.1 0.7 %collective-permute-done.12 = f32[8,128]{1,0:T(8,128)S(1)} collective-permute-done((f32[8,128]{1,0:T(8,128)S(1)}, f32[8,128]{1,0:T(8,128)S(1)}, u32[]{:S(2)}, u32[]{:S(2)}) %collective-permute-start.12) | collective-permute-done | bytes 4128 | tf_op jit(solution)/shard_map/ppermute | solution.py:334
  37.8 1.8 %collective-permute-start.16 = (f32[8,128]{1,0:T(8,128)S(1)}, f32[8,128]{1,0:T(8,128)S(1)}, u32[]{:S(2)}, u32[]{:S(2)}) collective-permute-start(f32[8,128]{1,0:T(8,128)S(1)} %add_add_fusion.1), channel_id=1, source_target_pairs={{0,10},{1,11},{2,8},{3,9},{4,14},{5,15},{6,12},{7,13},{8,2},{9,3},... | collective-permute-start | bytes 12296 | tf_op jit(solution)/shard_map/ppermute | solution.py:352
  39.6 1.0 %collective-permute-start.15 = (f32[8,128]{1,0:T(8,128)S(1)}, f32[8,128]{1,0:T(8,128)S(1)}, u32[]{:S(2)}, u32[]{:S(2)}) collective-permute-start(f32[8,128]{1,0:T(8,128)S(1)} %add_add_fusion.1), channel_id=1, source_target_pairs={{0,1},{1,0},{2,3},{3,2},{4,5},{5,4},{6,7},{7,6},{8,9},{9,8},{10,11... | collective-permute-start | bytes 12296 | tf_op jit(solution)/shard_map/ppermute | solution.py:352
  40.6 1.3 %collective-permute-done.17 = f32[8,128]{1,0:T(8,128)S(1)} collective-permute-done((f32[8,128]{1,0:T(8,128)S(1)}, f32[8,128]{1,0:T(8,128)S(1)}, u32[]{:S(2)}, u32[]{:S(2)}) %collective-permute-start.17) | collective-permute-done | bytes 4128 | tf_op jit(solution)/shard_map/ppermute | solution.py:352
  41.9 0.5 %collective-permute-done.16 = f32[8,128]{1,0:T(8,128)S(1)} collective-permute-done((f32[8,128]{1,0:T(8,128)S(1)}, f32[8,128]{1,0:T(8,128)S(1)}, u32[]{:S(2)}, u32[]{:S(2)}) %collective-permute-start.16) | collective-permute-done | bytes 4128 | tf_op jit(solution)/shard_map/ppermute | solution.py:352
  42.4 1.5 %final.1 = (f32[128,2048]{1,0:T(8,128)}, f32[128,2048]{1,0:T(8,128)}) custom-call(f32[8,128]{1,0:T(8,128)S(1)} %add_add_fusion.total, f32[64,1024]{1,0:T(8,128)S(1)} %get-tuple-element.62.rim_mean, f32[64,1024]{1,0:T(8,128)S(1)} %get-tuple-element.63.rim_change, f32[64,1024]{1,0:T(8,128)S(1)} %get-tuple-element.64.inner_mean, ...), custom_call_target="tpu_custom_call" | custom-call | flops 503316480 | bytes 393216 | tf_op jit(solution)/shard_map/final/pallas_call | solution.py:291
  (18 shorter events, 0.2 us)
Async XLA Ops:
  0.7 1.2 %copy-start = (f32[1,128,2048]{2,1,0:T(8,128)S(1)}, f32[1,128,2048]{2,1,0:T(8,128)}, u32[]{:S(2)}) copy-start(f32[1,128,2048]{2,1,0:T(8,128)} %param.4) | copy-start | bytes 3145732
  2.0 1.4 %collective-permute-start = (f32[128,128]{1,0:T(8,128)S(1)}, f32[128,128]{1,0:T(8,128)S(1)}, u32[]{:S(2)}, u32[]{:S(2)}) collective-permute-start(f32[128,128]{1,0:T(8,128)S(1)} %get-tuple-element.38), channel_id=1, source_target_pairs={{0,1},{1,0},{2,3},{3,2},{4,5},{5,4},{6,7},{7,6},{8,9},{9,8},{10,11... | collective-permute-start | bytes 196616 | tf_op jit(solution)/shard_map/ppermute | solution.py:308
  3.3 6.9 %copy-start.1 = (f32[1,128,2048]{2,1,0:T(8,128)S(1)}, f32[1,128,2048]{2,1,0:T(8,128)}, u32[]{:S(2)}) copy-start(f32[1,128,2048]{2,1,0:T(8,128)} %param.3) | copy-start | bytes 3145732
  3.8 10.0 %collective-permute-start.5 = (f32[32,1152]{1,0:T(8,128)S(1)}, f32[32,1152]{1,0:T(8,128)S(1)}, u32[]{:S(2)}, u32[]{:S(2)}) collective-permute-start(f32[32,1152]{1,0:T(8,128)S(1)} %get-tuple-element.48), channel_id=1, source_target_pairs={{2,4},{4,2},{3,5},{5,3},{10,12},{12,10},{11,13},{13,11},{18,20},{2... | collective-permute-start | bytes 442376 | tf_op jit(solution)/shard_map/ppermute | solution.py:323
  4.4 9.7 %collective-permute-start.4 = (f32[32,1152]{1,0:T(8,128)S(1)}, f32[32,1152]{1,0:T(8,128)S(1)}, u32[]{:S(2)}, u32[]{:S(2)}) collective-permute-start(f32[32,1152]{1,0:T(8,128)S(1)} %get-tuple-element.40.after), channel_id=1, source_target_pairs={{0,2},{2,0},{4,6},{6,4},{1,3},{3,1},{5,7},{7,5},{8,10},{10,8},{12,... | collective-permute-start | bytes 442376 | tf_op jit(solution)/shard_map/ppermute | solution.py:323
  10.3 2.6 %copy-start.2 = (f32[2]{0:T(128)S(1)}, f32[2]{0:T(128)}, u32[]{:S(2)}) copy-start(f32[2]{0:T(128)} %param.5) | copy-start | bytes 28
  10.3 2.6 %collective-permute-start.1 = (f32[128,128]{1,0:T(8,128)S(1)}, f32[128,128]{1,0:T(8,128)S(1)}, u32[]{:S(2)}, u32[]{:S(2)}) collective-permute-start(f32[128,128]{1,0:T(8,128)S(1)} %get-tuple-element.41), channel_id=1, source_target_pairs={{0,1},{1,0},{2,3},{3,2},{4,5},{5,4},{6,7},{7,6},{8,9},{9,8},{10,11... | collective-permute-start | bytes 196616 | tf_op jit(solution)/shard_map/ppermute | solution.py:308
  10.4 8.8 %collective-permute-start.2 = (f32[32,1152]{1,0:T(8,128)S(1)}, f32[32,1152]{1,0:T(8,128)S(1)}, u32[]{:S(2)}, u32[]{:S(2)}) collective-permute-start(f32[32,1152]{1,0:T(8,128)S(1)} %get-tuple-element.44), channel_id=1, source_target_pairs={{2,4},{4,2},{3,5},{5,3},{10,12},{12,10},{11,13},{13,11},{18,20},{2... | collective-permute-start | bytes 442376 | tf_op jit(solution)/shard_map/ppermute | solution.py:323
  11.0 8.2 %collective-permute-start.3 = (f32[32,1152]{1,0:T(8,128)S(1)}, f32[32,1152]{1,0:T(8,128)S(1)}, u32[]{:S(2)}, u32[]{:S(2)}) collective-permute-start(f32[32,1152]{1,0:T(8,128)S(1)} %get-tuple-element.45), channel_id=1, source_target_pairs={{0,2},{2,0},{4,6},{6,4},{1,3},{3,1},{5,7},{7,5},{8,10},{10,8},{12,... | collective-permute-start | bytes 442376 | tf_op jit(solution)/shard_map/ppermute | solution.py:323
  15.1 11.0 %collective-permute-start.11 = (f32[64,1024]{1,0:T(8,128)S(1)}, f32[64,1024]{1,0:T(8,128)S(1)}, u32[]{:S(2)}, u32[]{:S(2)}) collective-permute-start(f32[64,1024]{1,0:T(8,128)S(1)} %get-tuple-element.50.after.inner_own), channel_id=1, source_target_pairs={{0,8},{8,0},{1,9},{9,1},{2,10},{10,2},{3,11},{11,3},{4,12},{12,4},... | collective-permute-start | bytes 786440 | tf_op jit(solution)/shard_map/ppermute | solution.py:327
  16.6 6.9 %collective-permute-start.8 = (f32[32,1024]{1,0:T(8,128)S(1)}, f32[32,1024]{1,0:T(8,128)S(1)}, u32[]{:S(2)}, u32[]{:S(2)}) collective-permute-start(f32[32,1024]{1,0:T(8,128)S(1)} %get-tuple-element.54), channel_id=1, source_target_pairs={{0,2},{2,0},{4,6},{6,4},{1,3},{3,1},{5,7},{7,5},{8,10},{10,8},{12,... | collective-permute-start | bytes 393224 | tf_op jit(solution)/shard_map/ppermute | solution.py:323
  18.5 5.0 %collective-permute-start.9 = (f32[32,1024]{1,0:T(8,128)S(1)}, f32[32,1024]{1,0:T(8,128)S(1)}, u32[]{:S(2)}, u32[]{:S(2)}) collective-permute-start(f32[32,1024]{1,0:T(8,128)S(1)} %get-tuple-element.55), channel_id=1, source_target_pairs={{2,4},{4,2},{3,5},{5,3},{10,12},{12,10},{11,13},{13,11},{18,20},{2... | collective-permute-start | bytes 393224 | tf_op jit(solution)/shard_map/ppermute | solution.py:323
  20.2 5.6 %collective-permute-start.6 = (f32[32,1024]{1,0:T(8,128)S(1)}, f32[32,1024]{1,0:T(8,128)S(1)}, u32[]{:S(2)}, u32[]{:S(2)}) collective-permute-start(f32[32,1024]{1,0:T(8,128)S(1)} %get-tuple-element.52), channel_id=1, source_target_pairs={{0,2},{2,0},{4,6},{6,4},{1,3},{3,1},{5,7},{7,5},{8,10},{10,8},{12,... | collective-permute-start | bytes 393224 | tf_op jit(solution)/shard_map/ppermute | solution.py:323
  22.8 3.0 %collective-permute-start.7 = (f32[32,1024]{1,0:T(8,128)S(1)}, f32[32,1024]{1,0:T(8,128)S(1)}, u32[]{:S(2)}, u32[]{:S(2)}) collective-permute-start(f32[32,1024]{1,0:T(8,128)S(1)} %get-tuple-element.53), channel_id=1, source_target_pairs={{2,4},{4,2},{3,5},{5,3},{10,12},{12,10},{11,13},{13,11},{18,20},{2... | collective-permute-start | bytes 393224 | tf_op jit(solution)/shard_map/ppermute | solution.py:323
  23.8 7.6 %collective-permute-start.10 = (f32[64,1024]{1,0:T(8,128)S(1)}, f32[64,1024]{1,0:T(8,128)S(1)}, u32[]{:S(2)}, u32[]{:S(2)}) collective-permute-start(f32[64,1024]{1,0:T(8,128)S(1)} %get-tuple-element.56.after.rim_own), channel_id=1, source_target_pairs={{0,8},{8,0},{1,9},{9,1},{2,10},{10,2},{3,11},{11,3},{4,12},{12,4},... | collective-permute-start | bytes 786440 | tf_op jit(solution)/shard_map/ppermute | solution.py:327
  26.2 1.2 %collective-permute-start.18 = (f32[8,128]{1,0:T(8,128)S(1)}, f32[8,128]{1,0:T(8,128)S(1)}, u32[]{:S(2)}, u32[]{:S(2)}) collective-permute-start(f32[8,128]{1,0:T(8,128)S(1)} %get-tuple-element.60.before), channel_id=1, source_target_pairs={{0,1},{1,0},{2,3},{3,2},{4,5},{5,4},{6,7},{7,6},{8,9},{9,8},{10,11... | collective-permute-start | bytes 12296 | tf_op jit(solution)/shard_map/ppermute | solution.py:453
  27.4 15.0 %collective-permute-start.19 = (f32[128,1024]{1,0:T(8,128)S(1)}, f32[128,1024]{1,0:T(8,128)S(1)}, u32[]{:S(2)}, u32[]{:S(2)}) collective-permute-start(f32[128,1024]{1,0:T(8,128)S(1)} %later.1), channel_id=1, source_target_pairs={{0,8},{8,0},{1,9},{9,1},{2,10},{10,2},{3,11},{11,3},{4,12},{12,4},... | collective-permute-start | bytes 1572872 | tf_op jit(solution)/shard_map/ppermute | solution.py:327
  31.5 5.5 %collective-permute-start.14 = (f32[8,128]{1,0:T(8,128)S(1)}, f32[8,128]{1,0:T(8,128)S(1)}, u32[]{:S(2)}, u32[]{:S(2)}) collective-permute-start(f32[8,128]{1,0:T(8,128)S(1)} %get-tuple-element.61), channel_id=1, source_target_pairs={{0,6},{2,4},{4,2},{6,0},{1,7},{3,5},{5,3},{7,1},{8,14},{10,12},{12... | collective-permute-start | bytes 12296 | tf_op jit(solution)/shard_map/ppermute | solution.py:334
  32.6 4.5 %collective-permute-start.13 = (f32[8,128]{1,0:T(8,128)S(1)}, f32[8,128]{1,0:T(8,128)S(1)}, u32[]{:S(2)}, u32[]{:S(2)}) collective-permute-start(f32[8,128]{1,0:T(8,128)S(1)} %get-tuple-element.61), channel_id=1, source_target_pairs={{0,4},{2,6},{4,0},{6,2},{1,5},{3,7},{5,1},{7,3},{8,12},{10,14},{12... | collective-permute-start | bytes 12296 | tf_op jit(solution)/shard_map/ppermute | solution.py:334
  34.2 3.6 %collective-permute-start.12 = (f32[8,128]{1,0:T(8,128)S(1)}, f32[8,128]{1,0:T(8,128)S(1)}, u32[]{:S(2)}, u32[]{:S(2)}) collective-permute-start(f32[8,128]{1,0:T(8,128)S(1)} %get-tuple-element.61), channel_id=1, source_target_pairs={{0,2},{2,0},{4,6},{6,4},{1,3},{3,1},{5,7},{7,5},{8,10},{10,8},{12,... | collective-permute-start | bytes 12296 | tf_op jit(solution)/shard_map/ppermute | solution.py:334
  37.8 4.0 %collective-permute-start.17 = (f32[8,128]{1,0:T(8,128)S(1)}, f32[8,128]{1,0:T(8,128)S(1)}, u32[]{:S(2)}, u32[]{:S(2)}) collective-permute-start(f32[8,128]{1,0:T(8,128)S(1)} %add_add_fusion.1), channel_id=1, source_target_pairs={{0,11},{1,10},{2,9},{3,8},{4,15},{5,14},{6,13},{7,12},{8,3},{9,2},... | collective-permute-start | bytes 12296 | tf_op jit(solution)/shard_map/ppermute | solution.py:352
  37.8 4.6 %collective-permute-start.16 = (f32[8,128]{1,0:T(8,128)S(1)}, f32[8,128]{1,0:T(8,128)S(1)}, u32[]{:S(2)}, u32[]{:S(2)}) collective-permute-start(f32[8,128]{1,0:T(8,128)S(1)} %add_add_fusion.1), channel_id=1, source_target_pairs={{0,10},{1,11},{2,8},{3,9},{4,14},{5,15},{6,12},{7,13},{8,2},{9,3},... | collective-permute-start | bytes 12296 | tf_op jit(solution)/shard_map/ppermute | solution.py:352
  39.6 2.8 %collective-permute-start.15 = (f32[8,128]{1,0:T(8,128)S(1)}, f32[8,128]{1,0:T(8,128)S(1)}, u32[]{:S(2)}, u32[]{:S(2)}) collective-permute-start(f32[8,128]{1,0:T(8,128)S(1)} %add_add_fusion.1), channel_id=1, source_target_pairs={{0,1},{1,0},{2,3},{3,2},{4,5},{5,4},{6,7},{7,6},{8,9},{9,8},{10,11... | collective-permute-start | bytes 12296 | tf_op jit(solution)/shard_map/ppermute | solution.py:352

commit v8 on v7

--- a/solution.py
+++ b/solution.py
@@ -269,10 +269,11 @@
         copy.start()
         copies.append(copy)
 
-    for (to, part), mean, change in zip(rows, (rim_mean, inner_mean, rim_mean), (rim_change, inner_change, rim_change)):
+    for (to, part), mean in zip(rows, (rim_mean, inner_mean, rim_mean)):
         stage[0, to, :share] = mean[part, :] * scale
+    send(0, 0, "own")
+    for (to, part), change in zip(rows, (rim_change, inner_change, rim_change)):
         stage[1, to, :share] = change[part, :] + log_scale
-    send(0, 0, "own")
     send(1, 0, "own")
     for (to, part), own, smooth in zip(rows, (rim_own, inner_own, rim_own), (rim_smooth, inner_smooth, rim_smooth)):
         log_mean = own[part, :] + later[to, :]

time: 44.4 us -> 44.3 us (level)
  no operation moved by 1% of the time
where the time goes in v8:
time: 44.3 us; the launch traced here: 43.9 us
  starting transfers between devices  25.5 us (58%)
  waiting for transfers between devices  10.1 us (23%)
  Pallas kernels  6.28 us (14%)
  local copies, waits for them, and re-layouts  1.23 us (3%)
  between operations  0.86 us (2%)
    ppermute x4, starting transfers between devices, swap_rows(): lax.ppermute(first, 'rows', pairs(flip))  11.1 us
    pallas_call x18, Pallas kernels, call(): pl.pallas_call(kernel, name=name, input_output_aliases=aliases, out_shape...  6.28 us
    ppermute x3, starting transfers between devices, total_over(): lax.ppermute(values, axes, [(i, i ^ mask) for i in range(count)])  4.45 us
    ppermute x4, starting transfers between devices, swap_rows(): lax.ppermute(second, 'rows', pairs(1 - flip))  3.79 us
    ppermute x3, waiting for transfers between devices, swap_hist(): return lax.ppermute(values, 'hist', [(0, 1), (1, 0)])  3.41 us
    ppermute x3, starting transfers between devices, swap_hist(): return lax.ppermute(values, 'hist', [(0, 1), (1, 0)])  2.76 us
    ppermute x3, starting transfers between devices, total_aside(): lax.ppermute(values, ('hist', 'rows', 'cols'), [(i, apart(i, mask, rows *...  2.76 us
    ppermute x3, waiting for transfers between devices, total_over(): lax.ppermute(values, axes, [(i, i ^ mask) for i in range(count)])  1.84 us
  transfers between devices with their start and end apart: 20, of which 10 were waited for; matrix products, arithmetic and copies ran while one was open for 0% of the time, Pallas kernels for 10%

profile of v8, /device:TPU:0, one launch (start us, length us, event | category | flops | bytes accessed | tf_op | source)
XLA Modules:
  0.0 43.9 jit_solution(14354474539212815031)
XLA Ops:
  0.6 0.1 bands.1
  0.7 0.0 copy-start
  0.7 1.2 %copy-done = f32[1,128,2048]{2,1,0:T(8,128)S(1)} copy-done((f32[1,128,2048]{2,1,0:T(8,128)S(1)}, f32[1,128,2048]{2,1,0:T(8,128)}, u32[]{:S(2)}) %copy-start) | copy-done | bytes 1048600
  2.0 0.1 log_edges.1
  2.0 0.5 %collective-permute-start = (f32[128,128]{1,0:T(8,128)S(1)}, f32[128,128]{1,0:T(8,128)S(1)}, u32[]{:S(2)}, u32[]{:S(2)}) collective-permute-start(f32[128,128]{1,0:T(8,128)S(1)} %get-tuple-element.38), channel_id=1, source_target_pairs={{0,1},{1,0},{2,3},{3,2},{4,5},{5,4},{6,7},{7,6},{8,9},{9,8},{10,11... | collective-permute-start | bytes 196616 | tf_op jit(solution)/shard_map/ppermute | solution.py:309
  2.5 0.8 %spread.1.partial = f32[128,2176]{1,0:T(8,128)S(1)} custom-call(f32[128,2048]{1,0:T(8,128)S(1)} %get-tuple-element.37.logs, bf16[192,256]{1,0:T(8,128)(2,1)S(1)} %get-tuple-element.36.taps), custom_call_target="tpu_custom_call" | custom-call | flops 2013265920 | bytes 1572864 | tf_op jit(solution)/shard_map/spread/pallas_call | solution.py:292
  3.3 0.0 copy-start.1
  3.3 0.1 collective-permute-done.from_left.from_right
  3.5 0.3 spread_edge.1
  3.8 0.7 %collective-permute-start.5 = (f32[32,1152]{1,0:T(8,128)S(1)}, f32[32,1152]{1,0:T(8,128)S(1)}, u32[]{:S(2)}, u32[]{:S(2)}) collective-permute-start(f32[32,1152]{1,0:T(8,128)S(1)} %get-tuple-element.48), channel_id=1, source_target_pairs={{2,4},{4,2},{3,5},{5,3},{10,12},{12,10},{11,13},{13,11},{18,20},{2... | collective-permute-start | bytes 442376 | tf_op jit(solution)/shard_map/ppermute | solution.py:324
  4.4 5.8 %collective-permute-start.4 = (f32[32,1152]{1,0:T(8,128)S(1)}, f32[32,1152]{1,0:T(8,128)S(1)}, u32[]{:S(2)}, u32[]{:S(2)}) collective-permute-start(f32[32,1152]{1,0:T(8,128)S(1)} %get-tuple-element.40.after), channel_id=1, source_target_pairs={{0,2},{2,0},{4,6},{6,4},{1,3},{3,1},{5,7},{7,5},{8,10},{10,8},{12,... | collective-permute-start | bytes 442376 | tf_op jit(solution)/shard_map/ppermute | solution.py:324
  10.3 0.1 collective-permute-start.1
  10.4 0.7 %collective-permute-start.2 = (f32[32,1152]{1,0:T(8,128)S(1)}, f32[32,1152]{1,0:T(8,128)S(1)}, u32[]{:S(2)}, u32[]{:S(2)}) collective-permute-start(f32[32,1152]{1,0:T(8,128)S(1)} %get-tuple-element.44), channel_id=1, source_target_pairs={{2,4},{4,2},{3,5},{5,3},{10,12},{12,10},{11,13},{13,11},{18,20},{2... | collective-permute-start | bytes 442376 | tf_op jit(solution)/shard_map/ppermute | solution.py:324
  11.0 1.8 %collective-permute-start.3 = (f32[32,1152]{1,0:T(8,128)S(1)}, f32[32,1152]{1,0:T(8,128)S(1)}, u32[]{:S(2)}, u32[]{:S(2)}) collective-permute-start(f32[32,1152]{1,0:T(8,128)S(1)} %get-tuple-element.45), channel_id=1, source_target_pairs={{0,2},{2,0},{4,6},{6,4},{1,3},{3,1},{5,7},{7,5},{8,10},{10,8},{12,... | collective-permute-start | bytes 442376 | tf_op jit(solution)/shard_map/ppermute | solution.py:324
  12.9 0.9 %inner_ratio.1 = (f32[64,2048]{1,0:T(8,128)S(1)}, f32[128,2176]{1,0:T(8,128)S(1)}, f32[8,128]{1,0:T(8,128)S(1)}) custom-call(f32[128,2176]{1,0:T(8,128)S(1)} %get-tuple-element.39.across, f32[128,2048]{1,0:T(8,128)S(1)} %bitcast.6, f32[128,128]{1,0:T(8,128)S(1)} %collective-permute-done.1.from_left.from_right, ...), custom_call_target="tpu_custom_call" | custom-call | tf_op jit(solution)/shard_map/inner_ratio/pallas_call | solution.py:292
  13.8 0.0 collective-permute-done.5.second
  13.8 0.3 collective-permute-done.4.first
  14.1 0.6 %other_rim_ratio.1.rims = f32[64,1024]{1,0:T(8,128)S(1)} custom-call(f32[128,2176]{1,0:T(8,128)S(1)} %get-tuple-element.39.across, f32[32,1152]{1,0:T(8,128)S(1)} %collective-permute-done.4.first, f32[32,1152]{1,0:T(8,128)S(1)} %collective-permute-done.5.second, f32[128,2176]{1,0:T(8,128)S(1)} %get-tuple-element.46.wide, ...), custom_call_target="tpu_custom_call" | custom-call | flops 2013265920 | bytes 1572864 | tf_op jit(solution)/shard_map/other_rim_ratio/pallas_call | solution.py:292
  14.8 0.3 other_inner_log.1
  15.1 1.6 %collective-permute-start.11 = (f32[64,1024]{1,0:T(8,128)S(1)}, f32[64,1024]{1,0:T(8,128)S(1)}, u32[]{:S(2)}, u32[]{:S(2)}) collective-permute-start(f32[64,1024]{1,0:T(8,128)S(1)} %get-tuple-element.50.after.inner_own), channel_id=1, source_target_pairs={{0,8},{8,0},{1,9},{9,1},{2,10},{10,2},{3,11},{11,3},{4,12},{12,4},... | collective-permute-start | bytes 786440 | tf_op jit(solution)/shard_map/ppermute | solution.py:328
  16.6 1.9 %collective-permute-start.8 = (f32[32,1024]{1,0:T(8,128)S(1)}, f32[32,1024]{1,0:T(8,128)S(1)}, u32[]{:S(2)}, u32[]{:S(2)}) collective-permute-start(f32[32,1024]{1,0:T(8,128)S(1)} %get-tuple-element.54), channel_id=1, source_target_pairs={{0,2},{2,0},{4,6},{6,4},{1,3},{3,1},{5,7},{7,5},{8,10},{10,8},{12,... | collective-permute-start | bytes 393224 | tf_op jit(solution)/shard_map/ppermute | solution.py:324
  18.5 0.7 %collective-permute-start.9 = (f32[32,1024]{1,0:T(8,128)S(1)}, f32[32,1024]{1,0:T(8,128)S(1)}, u32[]{:S(2)}, u32[]{:S(2)}) collective-permute-start(f32[32,1024]{1,0:T(8,128)S(1)} %get-tuple-element.55), channel_id=1, source_target_pairs={{2,4},{4,2},{3,5},{5,3},{10,12},{12,10},{11,13},{13,11},{18,20},{2... | collective-permute-start | bytes 393224 | tf_op jit(solution)/shard_map/ppermute | solution.py:324
  19.2 0.0 collective-permute-done.3.second
  19.2 0.6 %own_rim_ratio.1.rims = f32[64,1024]{1,0:T(8,128)S(1)} custom-call(f32[128,2176]{1,0:T(8,128)S(1)} %get-tuple-element.39.across, f32[32,1152]{1,0:T(8,128)S(1)} %collective-permute-done.2.first, f32[32,1152]{1,0:T(8,128)S(1)} %collective-permute-done.3.second, f32[128,2176]{1,0:T(8,128)S(1)} %get-tuple-element.46.wide, ...), custom_call_target="tpu_custom_call" | custom-call | flops 2013265920 | bytes 1572864 | tf_op jit(solution)/shard_map/own_rim_ratio/pallas_call | solution.py:292
  19.8 0.3 own_inner_log.1
  20.2 2.7 %collective-permute-start.6 = (f32[32,1024]{1,0:T(8,128)S(1)}, f32[32,1024]{1,0:T(8,128)S(1)}, u32[]{:S(2)}, u32[]{:S(2)}) collective-permute-start(f32[32,1024]{1,0:T(8,128)S(1)} %get-tuple-element.52), channel_id=1, source_target_pairs={{0,2},{2,0},{4,6},{6,4},{1,3},{3,1},{5,7},{7,5},{8,10},{10,8},{12,... | collective-permute-start | bytes 393224 | tf_op jit(solution)/shard_map/ppermute | solution.py:324
  22.8 0.7 %collective-permute-start.7 = (f32[32,1024]{1,0:T(8,128)S(1)}, f32[32,1024]{1,0:T(8,128)S(1)}, u32[]{:S(2)}, u32[]{:S(2)}) collective-permute-start(f32[32,1024]{1,0:T(8,128)S(1)} %get-tuple-element.53), channel_id=1, source_target_pairs={{2,4},{4,2},{3,5},{5,3},{10,12},{12,10},{11,13},{13,11},{18,20},{2... | collective-permute-start | bytes 393224 | tf_op jit(solution)/shard_map/ppermute | solution.py:324
  23.5 0.3 other_rim_log.1
  23.8 0.6 %collective-permute-start.10 = (f32[64,1024]{1,0:T(8,128)S(1)}, f32[64,1024]{1,0:T(8,128)S(1)}, u32[]{:S(2)}, u32[]{:S(2)}) collective-permute-start(f32[64,1024]{1,0:T(8,128)S(1)} %get-tuple-element.56.after.rim_own), channel_id=1, source_target_pairs={{0,8},{8,0},{1,9},{9,1},{2,10},{10,2},{3,11},{11,3},{4,12},{12,4},... | collective-permute-start | bytes 786440 | tf_op jit(solution)/shard_map/ppermute | solution.py:328
  24.4 1.4 %collective-permute-done.6.from_first = f32[32,1024]{1,0:T(8,128)S(1)} collective-permute-done((f32[32,1024]{1,0:T(8,128)S(1)}, f32[32,1024]{1,0:T(8,128)S(1)}, u32[]{:S(2)}, u32[]{:S(2)}) %collective-permute-start.6) | collective-permute-done | bytes 131104 | tf_op jit(solution)/shard_map/ppermute | solution.py:324
  25.8 0.3 own_rim_log.1
  26.1 0.1 inner_mean.1
  26.2 0.1 collective-permute-start.18
  26.3 1.2 %collective-permute-done.18.after = f32[8,128]{1,0:T(8,128)S(1)} collective-permute-done((f32[8,128]{1,0:T(8,128)S(1)}, f32[8,128]{1,0:T(8,128)S(1)}, u32[]{:S(2)}, u32[]{:S(2)}) %collective-permute-start.18) | collective-permute-done | bytes 4128 | tf_op jit(solution)/shard_map/ppermute | solution.py:454
  27.4 0.6 %collective-permute-start.19 = (f32[128,1024]{1,0:T(8,128)S(1)}, f32[128,1024]{1,0:T(8,128)S(1)}, u32[]{:S(2)}, u32[]{:S(2)}) collective-permute-start(f32[128,1024]{1,0:T(8,128)S(1)} %later.1), channel_id=1, source_target_pairs={{0,8},{8,0},{1,9},{9,1},{2,10},{10,2},{3,11},{11,3},{4,12},{12,4},... | collective-permute-start | bytes 1572872 | tf_op jit(solution)/shard_map/ppermute | solution.py:328
  28.1 3.4 %collective-permute-done.10.arrived = f32[64,1024]{1,0:T(8,128)S(1)} collective-permute-done((f32[64,1024]{1,0:T(8,128)S(1)}, f32[64,1024]{1,0:T(8,128)S(1)}, u32[]{:S(2)}, u32[]{:S(2)}) %collective-permute-start.10) | collective-permute-done | bytes 262176 | tf_op jit(solution)/shard_map/ppermute | solution.py:328
  31.5 0.1 rim_mean.1
  31.5 1.1 %collective-permute-start.14 = (f32[8,128]{1,0:T(8,128)S(1)}, f32[8,128]{1,0:T(8,128)S(1)}, u32[]{:S(2)}, u32[]{:S(2)}) collective-permute-start(f32[8,128]{1,0:T(8,128)S(1)} %get-tuple-element.61), channel_id=1, source_target_pairs={{0,6},{2,4},{4,2},{6,0},{1,7},{3,5},{5,3},{7,1},{8,14},{10,12},{12... | collective-permute-start | bytes 12296 | tf_op jit(solution)/shard_map/ppermute | solution.py:335
  32.6 1.6 %collective-permute-start.13 = (f32[8,128]{1,0:T(8,128)S(1)}, f32[8,128]{1,0:T(8,128)S(1)}, u32[]{:S(2)}, u32[]{:S(2)}) collective-permute-start(f32[8,128]{1,0:T(8,128)S(1)} %get-tuple-element.61), channel_id=1, source_target_pairs={{0,4},{2,6},{4,0},{6,2},{1,5},{3,7},{5,1},{7,3},{8,12},{10,14},{12... | collective-permute-start | bytes 12296 | tf_op jit(solution)/shard_map/ppermute | solution.py:335
  34.2 1.8 %collective-permute-start.12 = (f32[8,128]{1,0:T(8,128)S(1)}, f32[8,128]{1,0:T(8,128)S(1)}, u32[]{:S(2)}, u32[]{:S(2)}) collective-permute-start(f32[8,128]{1,0:T(8,128)S(1)} %get-tuple-element.61), channel_id=1, source_target_pairs={{0,2},{2,0},{4,6},{6,4},{1,3},{3,1},{5,7},{7,5},{8,10},{10,8},{12,... | collective-permute-start | bytes 12296 | tf_op jit(solution)/shard_map/ppermute | solution.py:335
  36.0 1.0 %collective-permute-done.14 = f32[8,128]{1,0:T(8,128)S(1)} collective-permute-done((f32[8,128]{1,0:T(8,128)S(1)}, f32[8,128]{1,0:T(8,128)S(1)}, u32[]{:S(2)}, u32[]{:S(2)}) %collective-permute-start.14) | collective-permute-done | bytes 4128 | tf_op jit(solution)/shard_map/ppermute | solution.py:335
  37.0 0.1 collective-permute-done.13
  37.1 0.7 %collective-permute-done.12 = f32[8,128]{1,0:T(8,128)S(1)} collective-permute-done((f32[8,128]{1,0:T(8,128)S(1)}, f32[8,128]{1,0:T(8,128)S(1)}, u32[]{:S(2)}, u32[]{:S(2)}) %collective-permute-start.12) | collective-permute-done | bytes 4128 | tf_op jit(solution)/shard_map/ppermute | solution.py:335
  37.8 1.8 %collective-permute-start.16 = (f32[8,128]{1,0:T(8,128)S(1)}, f32[8,128]{1,0:T(8,128)S(1)}, u32[]{:S(2)}, u32[]{:S(2)}) collective-permute-start(f32[8,128]{1,0:T(8,128)S(1)} %add_add_fusion.1), channel_id=1, source_target_pairs={{0,10},{1,11},{2,8},{3,9},{4,14},{5,15},{6,12},{7,13},{8,2},{9,3},... | collective-permute-start | bytes 12296 | tf_op jit(solution)/shard_map/ppermute | solution.py:353
  39.6 1.0 %collective-permute-start.15 = (f32[8,128]{1,0:T(8,128)S(1)}, f32[8,128]{1,0:T(8,128)S(1)}, u32[]{:S(2)}, u32[]{:S(2)}) collective-permute-start(f32[8,128]{1,0:T(8,128)S(1)} %add_add_fusion.1), channel_id=1, source_target_pairs={{0,1},{1,0},{2,3},{3,2},{4,5},{5,4},{6,7},{7,6},{8,9},{9,8},{10,11... | collective-permute-start | bytes 12296 | tf_op jit(solution)/shard_map/ppermute | solution.py:353
  40.6 1.3 %collective-permute-done.17 = f32[8,128]{1,0:T(8,128)S(1)} collective-permute-done((f32[8,128]{1,0:T(8,128)S(1)}, f32[8,128]{1,0:T(8,128)S(1)}, u32[]{:S(2)}, u32[]{:S(2)}) %collective-permute-start.17) | collective-permute-done | bytes 4128 | tf_op jit(solution)/shard_map/ppermute | solution.py:353
  41.9 0.5 %collective-permute-done.16 = f32[8,128]{1,0:T(8,128)S(1)} collective-permute-done((f32[8,128]{1,0:T(8,128)S(1)}, f32[8,128]{1,0:T(8,128)S(1)}, u32[]{:S(2)}, u32[]{:S(2)}) %collective-permute-start.16) | collective-permute-done | bytes 4128 | tf_op jit(solution)/shard_map/ppermute | solution.py:353
  42.4 1.5 %final.1 = (f32[128,2048]{1,0:T(8,128)}, f32[128,2048]{1,0:T(8,128)}) custom-call(f32[8,128]{1,0:T(8,128)S(1)} %add_add_fusion.total, f32[64,1024]{1,0:T(8,128)S(1)} %get-tuple-element.62.rim_mean, f32[64,1024]{1,0:T(8,128)S(1)} %get-tuple-element.63.rim_change, f32[64,1024]{1,0:T(8,128)S(1)} %get-tuple-element.64.inner_mean, ...), custom_call_target="tpu_custom_call" | custom-call | flops 503316480 | bytes 393216 | tf_op jit(solution)/shard_map/final/pallas_call | solution.py:292
  (18 shorter events, 0.2 us)
Async XLA Ops:
  0.7 1.2 %copy-start = (f32[1,128,2048]{2,1,0:T(8,128)S(1)}, f32[1,128,2048]{2,1,0:T(8,128)}, u32[]{:S(2)}) copy-start(f32[1,128,2048]{2,1,0:T(8,128)} %param.4) | copy-start | bytes 3145732
  2.0 1.4 %collective-permute-start = (f32[128,128]{1,0:T(8,128)S(1)}, f32[128,128]{1,0:T(8,128)S(1)}, u32[]{:S(2)}, u32[]{:S(2)}) collective-permute-start(f32[128,128]{1,0:T(8,128)S(1)} %get-tuple-element.38), channel_id=1, source_target_pairs={{0,1},{1,0},{2,3},{3,2},{4,5},{5,4},{6,7},{7,6},{8,9},{9,8},{10,11... | collective-permute-start | bytes 196616 | tf_op jit(solution)/shard_map/ppermute | solution.py:309
  3.3 6.9 %copy-start.1 = (f32[1,128,2048]{2,1,0:T(8,128)S(1)}, f32[1,128,2048]{2,1,0:T(8,128)}, u32[]{:S(2)}) copy-start(f32[1,128,2048]{2,1,0:T(8,128)} %param.3) | copy-start | bytes 3145732
  3.8 10.0 %collective-permute-start.5 = (f32[32,1152]{1,0:T(8,128)S(1)}, f32[32,1152]{1,0:T(8,128)S(1)}, u32[]{:S(2)}, u32[]{:S(2)}) collective-permute-start(f32[32,1152]{1,0:T(8,128)S(1)} %get-tuple-element.48), channel_id=1, source_target_pairs={{2,4},{4,2},{3,5},{5,3},{10,12},{12,10},{11,13},{13,11},{18,20},{2... | collective-permute-start | bytes 442376 | tf_op jit(solution)/shard_map/ppermute | solution.py:324
  4.4 9.7 %collective-permute-start.4 = (f32[32,1152]{1,0:T(8,128)S(1)}, f32[32,1152]{1,0:T(8,128)S(1)}, u32[]{:S(2)}, u32[]{:S(2)}) collective-permute-start(f32[32,1152]{1,0:T(8,128)S(1)} %get-tuple-element.40.after), channel_id=1, source_target_pairs={{0,2},{2,0},{4,6},{6,4},{1,3},{3,1},{5,7},{7,5},{8,10},{10,8},{12,... | collective-permute-start | bytes 442376 | tf_op jit(solution)/shard_map/ppermute | solution.py:324
  10.3 2.6 %copy-start.2 = (f32[2]{0:T(128)S(1)}, f32[2]{0:T(128)}, u32[]{:S(2)}) copy-start(f32[2]{0:T(128)} %param.5) | copy-start | bytes 28
  10.3 2.6 %collective-permute-start.1 = (f32[128,128]{1,0:T(8,128)S(1)}, f32[128,128]{1,0:T(8,128)S(1)}, u32[]{:S(2)}, u32[]{:S(2)}) collective-permute-start(f32[128,128]{1,0:T(8,128)S(1)} %get-tuple-element.41), channel_id=1, source_target_pairs={{0,1},{1,0},{2,3},{3,2},{4,5},{5,4},{6,7},{7,6},{8,9},{9,8},{10,11... | collective-permute-start | bytes 196616 | tf_op jit(solution)/shard_map/ppermute | solution.py:309
  10.4 8.8 %collective-permute-start.2 = (f32[32,1152]{1,0:T(8,128)S(1)}, f32[32,1152]{1,0:T(8,128)S(1)}, u32[]{:S(2)}, u32[]{:S(2)}) collective-permute-start(f32[32,1152]{1,0:T(8,128)S(1)} %get-tuple-element.44), channel_id=1, source_target_pairs={{2,4},{4,2},{3,5},{5,3},{10,12},{12,10},{11,13},{13,11},{18,20},{2... | collective-permute-start | bytes 442376 | tf_op jit(solution)/shard_map/ppermute | solution.py:324
  11.0 8.2 %collective-permute-start.3 = (f32[32,1152]{1,0:T(8,128)S(1)}, f32[32,1152]{1,0:T(8,128)S(1)}, u32[]{:S(2)}, u32[]{:S(2)}) collective-permute-start(f32[32,1152]{1,0:T(8,128)S(1)} %get-tuple-element.45), channel_id=1, source_target_pairs={{0,2},{2,0},{4,6},{6,4},{1,3},{3,1},{5,7},{7,5},{8,10},{10,8},{12,... | collective-permute-start | bytes 442376 | tf_op jit(solution)/shard_map/ppermute | solution.py:324
  15.1 11.0 %collective-permute-start.11 = (f32[64,1024]{1,0:T(8,128)S(1)}, f32[64,1024]{1,0:T(8,128)S(1)}, u32[]{:S(2)}, u32[]{:S(2)}) collective-permute-start(f32[64,1024]{1,0:T(8,128)S(1)} %get-tuple-element.50.after.inner_own), channel_id=1, source_target_pairs={{0,8},{8,0},{1,9},{9,1},{2,10},{10,2},{3,11},{11,3},{4,12},{12,4},... | collective-permute-start | bytes 786440 | tf_op jit(solution)/shard_map/ppermute | solution.py:328
  16.6 6.9 %collective-permute-start.8 = (f32[32,1024]{1,0:T(8,128)S(1)}, f32[32,1024]{1,0:T(8,128)S(1)}, u32[]{:S(2)}, u32[]{:S(2)}) collective-permute-start(f32[32,1024]{1,0:T(8,128)S(1)} %get-tuple-element.54), channel_id=1, source_target_pairs={{0,2},{2,0},{4,6},{6,4},{1,3},{3,1},{5,7},{7,5},{8,10},{10,8},{12,... | collective-permute-start | bytes 393224 | tf_op jit(solution)/shard_map/ppermute | solution.py:324
  18.5 5.0 %collective-permute-start.9 = (f32[32,1024]{1,0:T(8,128)S(1)}, f32[32,1024]{1,0:T(8,128)S(1)}, u32[]{:S(2)}, u32[]{:S(2)}) collective-permute-start(f32[32,1024]{1,0:T(8,128)S(1)} %get-tuple-element.55), channel_id=1, source_target_pairs={{2,4},{4,2},{3,5},{5,3},{10,12},{12,10},{11,13},{13,11},{18,20},{2... | collective-permute-start | bytes 393224 | tf_op jit(solution)/shard_map/ppermute | solution.py:324
  20.2 5.6 %collective-permute-start.6 = (f32[32,1024]{1,0:T(8,128)S(1)}, f32[32,1024]{1,0:T(8,128)S(1)}, u32[]{:S(2)}, u32[]{:S(2)}) collective-permute-start(f32[32,1024]{1,0:T(8,128)S(1)} %get-tuple-element.52), channel_id=1, source_target_pairs={{0,2},{2,0},{4,6},{6,4},{1,3},{3,1},{5,7},{7,5},{8,10},{10,8},{12,... | collective-permute-start | bytes 393224 | tf_op jit(solution)/shard_map/ppermute | solution.py:324
  22.8 3.0 %collective-permute-start.7 = (f32[32,1024]{1,0:T(8,128)S(1)}, f32[32,1024]{1,0:T(8,128)S(1)}, u32[]{:S(2)}, u32[]{:S(2)}) collective-permute-start(f32[32,1024]{1,0:T(8,128)S(1)} %get-tuple-element.53), channel_id=1, source_target_pairs={{2,4},{4,2},{3,5},{5,3},{10,12},{12,10},{11,13},{13,11},{18,20},{2... | collective-permute-start | bytes 393224 | tf_op jit(solution)/shard_map/ppermute | solution.py:324
  23.8 7.6 %collective-permute-start.10 = (f32[64,1024]{1,0:T(8,128)S(1)}, f32[64,1024]{1,0:T(8,128)S(1)}, u32[]{:S(2)}, u32[]{:S(2)}) collective-permute-start(f32[64,1024]{1,0:T(8,128)S(1)} %get-tuple-element.56.after.rim_own), channel_id=1, source_target_pairs={{0,8},{8,0},{1,9},{9,1},{2,10},{10,2},{3,11},{11,3},{4,12},{12,4},... | collective-permute-start | bytes 786440 | tf_op jit(solution)/shard_map/ppermute | solution.py:328
  26.2 1.2 %collective-permute-start.18 = (f32[8,128]{1,0:T(8,128)S(1)}, f32[8,128]{1,0:T(8,128)S(1)}, u32[]{:S(2)}, u32[]{:S(2)}) collective-permute-start(f32[8,128]{1,0:T(8,128)S(1)} %get-tuple-element.60.before), channel_id=1, source_target_pairs={{0,1},{1,0},{2,3},{3,2},{4,5},{5,4},{6,7},{7,6},{8,9},{9,8},{10,11... | collective-permute-start | bytes 12296 | tf_op jit(solution)/shard_map/ppermute | solution.py:454
  27.4 15.0 %collective-permute-start.19 = (f32[128,1024]{1,0:T(8,128)S(1)}, f32[128,1024]{1,0:T(8,128)S(1)}, u32[]{:S(2)}, u32[]{:S(2)}) collective-permute-start(f32[128,1024]{1,0:T(8,128)S(1)} %later.1), channel_id=1, source_target_pairs={{0,8},{8,0},{1,9},{9,1},{2,10},{10,2},{3,11},{11,3},{4,12},{12,4},... | collective-permute-start | bytes 1572872 | tf_op jit(solution)/shard_map/ppermute | solution.py:328
  31.5 5.5 %collective-permute-start.14 = (f32[8,128]{1,0:T(8,128)S(1)}, f32[8,128]{1,0:T(8,128)S(1)}, u32[]{:S(2)}, u32[]{:S(2)}) collective-permute-start(f32[8,128]{1,0:T(8,128)S(1)} %get-tuple-element.61), channel_id=1, source_target_pairs={{0,6},{2,4},{4,2},{6,0},{1,7},{3,5},{5,3},{7,1},{8,14},{10,12},{12... | collective-permute-start | bytes 12296 | tf_op jit(solution)/shard_map/ppermute | solution.py:335
  32.6 4.5 %collective-permute-start.13 = (f32[8,128]{1,0:T(8,128)S(1)}, f32[8,128]{1,0:T(8,128)S(1)}, u32[]{:S(2)}, u32[]{:S(2)}) collective-permute-start(f32[8,128]{1,0:T(8,128)S(1)} %get-tuple-element.61), channel_id=1, source_target_pairs={{0,4},{2,6},{4,0},{6,2},{1,5},{3,7},{5,1},{7,3},{8,12},{10,14},{12... | collective-permute-start | bytes 12296 | tf_op jit(solution)/shard_map/ppermute | solution.py:335
  34.2 3.6 %collective-permute-start.12 = (f32[8,128]{1,0:T(8,128)S(1)}, f32[8,128]{1,0:T(8,128)S(1)}, u32[]{:S(2)}, u32[]{:S(2)}) collective-permute-start(f32[8,128]{1,0:T(8,128)S(1)} %get-tuple-element.61), channel_id=1, source_target_pairs={{0,2},{2,0},{4,6},{6,4},{1,3},{3,1},{5,7},{7,5},{8,10},{10,8},{12,... | collective-permute-start | bytes 12296 | tf_op jit(solution)/shard_map/ppermute | solution.py:335
  37.8 4.0 %collective-permute-start.17 = (f32[8,128]{1,0:T(8,128)S(1)}, f32[8,128]{1,0:T(8,128)S(1)}, u32[]{:S(2)}, u32[]{:S(2)}) collective-permute-start(f32[8,128]{1,0:T(8,128)S(1)} %add_add_fusion.1), channel_id=1, source_target_pairs={{0,11},{1,10},{2,9},{3,8},{4,15},{5,14},{6,13},{7,12},{8,3},{9,2},... | collective-permute-start | bytes 12296 | tf_op jit(solution)/shard_map/ppermute | solution.py:353
  37.8 4.6 %collective-permute-start.16 = (f32[8,128]{1,0:T(8,128)S(1)}, f32[8,128]{1,0:T(8,128)S(1)}, u32[]{:S(2)}, u32[]{:S(2)}) collective-permute-start(f32[8,128]{1,0:T(8,128)S(1)} %add_add_fusion.1), channel_id=1, source_target_pairs={{0,10},{1,11},{2,8},{3,9},{4,14},{5,15},{6,12},{7,13},{8,2},{9,3},... | collective-permute-start | bytes 12296 | tf_op jit(solution)/shard_map/ppermute | solution.py:353
  39.6 2.8 %collective-permute-start.15 = (f32[8,128]{1,0:T(8,128)S(1)}, f32[8,128]{1,0:T(8,128)S(1)}, u32[]{:S(2)}, u32[]{:S(2)}) collective-permute-start(f32[8,128]{1,0:T(8,128)S(1)} %add_add_fusion.1), channel_id=1, source_target_pairs={{0,1},{1,0},{2,3},{3,2},{4,5},{5,4},{6,7},{7,6},{8,9},{9,8},{10,11... | collective-permute-start | bytes 12296 | tf_op jit(solution)/shard_map/ppermute | solution.py:353
